TPU v7x, 512 devices: a whole 4x8x8 slice. The times are simulated.
512 devices in a mesh: sx: 4 (over x), sy: 2 (over core), dict: 64 (over z, y).
Axes of the slice: x: 4, y: 8, z: 8, core: 2. Of those that a mesh axis runs over, the one named last changes fastest.
Arguments:
- patterns: bfloat16 [8, 512, 1600], P('sx', ('sy', 'dict')), may hold values from -12 to 12
- nlpar_weights: float32 [9, 8, 512], P(None, 'sx', ('sy', 'dict')), may hold values from 0.2 to 2
- dictionary: bfloat16 [1600, 180224], P(None, ('sy', 'dict')), as said below
Outputs:
- best_score: float32 [8, 512], P('sx', ('sy', 'dict'))
Inputs may be any that keep to these rules, and one draw needn't show every extreme that they name: Each dictionary column has mean zero and unit Euclidean norm over its 1600 pixels, up to rounding to bfloat16.
All inputs are finite; a program needn't handle non-finite values.
Results may differ from a plain program's by a relative error of at most 0.0003.
Values may be sent and summed in bfloat16 or wider, within the bound.
No kernel may reach another device: no remote copies, remote signals or barrier semaphores. Data moves between devices by JAX's collectives and lax.ppermute only.
A program may use at most 64 MiB of HBM per device.

v0:
```python
import jax
import jax.numpy as jnp
from jax import lax
from jax.sharding import PartitionSpec as P

PH = 40
PW = 40


def padded_2(block, sides, width):
    for axis, dim in sides:
        count = lax.axis_size(axis)
        forward = [(i, i + 1) for i in range(count - 1)]
        backward = [(target, source) for source, target in forward]
        low = lax.ppermute(
            lax.slice_in_dim(block, block.shape[dim] - width, None, axis=dim), axis, forward
        )
        high = lax.ppermute(lax.slice_in_dim(block, 0, width, axis=dim), axis, backward)
        block = jnp.concatenate([low, block, high], axis=dim)
    return block


def box_filter(image):
    extra = [(0, 0)] * (image.ndim - 2) + [(2, 2), (2, 2)]
    padded = jnp.pad(image, extra)
    vertical = padded[..., 0:PH, :]
    for offset in range(1, 5):
        vertical = vertical + padded[..., offset : offset + PH, :]
    total = vertical[..., :, 0:PW]
    for offset in range(1, 5):
        total = total + vertical[..., :, offset : offset + PW]
    return total


def normalize(averaged):
    shaped = averaged.reshape(averaged.shape[:-1] + (PH, PW))
    high = shaped - box_filter(shaped) / 25.0
    high = high.reshape(averaged.shape)
    centered = high - jnp.mean(high, axis=-1, keepdims=True)
    scale = jnp.sqrt(jnp.mean(centered * centered, axis=-1, keepdims=True) + 1e-06)
    return (centered / scale).astype(jnp.bfloat16)


def on_device(patterns, nlpar_weights, dictionary):
    rows = patterns.shape[0]
    cols = patterns.shape[1]
    points = rows * cols
    padded = padded_2(patterns, (("sx", 0), (("sy", "dict"), 1)), 1)
    row_first = lax.axis_index("sx") * rows
    col_first = lax.axis_index(("sy", "dict")) * cols
    row_total = rows * lax.axis_size("sx")
    col_total = cols * lax.axis_size(("sy", "dict"))
    row_place = row_first + jnp.arange(rows, dtype=jnp.int32)
    col_place = col_first + jnp.arange(cols, dtype=jnp.int32)
    total = jnp.zeros((rows, cols, patterns.shape[2]), jnp.float32)
    weight_sum = jnp.zeros((rows, cols), jnp.float32)
    for row_step in range(3):
        row_near = row_place + (row_step - 1)
        row_valid = ((row_near >= 0) & (row_near < row_total)).astype(jnp.float32)
        for col_step in range(3):
            col_near = col_place + (col_step - 1)
            col_valid = ((col_near >= 0) & (col_near < col_total)).astype(jnp.float32)
            index = 3 * row_step + col_step
            weight = nlpar_weights[index] * row_valid[:, None] * col_valid[None, :]
            neighbour = padded[row_step : row_step + rows, col_step : col_step + cols, :].astype(
                jnp.float32
            )
            total = total + weight[:, :, None] * neighbour
            weight_sum = weight_sum + weight
    averaged = total / weight_sum[:, :, None]
    normalized = normalize(averaged).reshape(points, patterns.shape[2])
    scores = jnp.dot(
        lax.all_gather(normalized, ("sy", "dict"), axis=0, tiled=True),
        dictionary,
        preferred_element_type=jnp.float32,
    )
    table = jnp.max(scores, axis=1)
    merged = lax.pmax(table, ("sy", "dict"))
    best = lax.dynamic_slice_in_dim(merged, lax.axis_index(("sy", "dict")) * points, points, 0)
    return best.reshape(rows, cols)


def solution(mesh):
    return jax.shard_map(
        on_device,
        mesh=mesh,
        in_specs=(
            P("sx", ("sy", "dict"), None),
            P(None, "sx", ("sy", "dict")),
            P(None, ("sy", "dict")),
        ),
        out_specs=P("sx", ("sy", "dict")),
        check_vma=False,
    )
```

profile of v0, /device:TPU:258, one launch (start us, length us, event | category | flops | bytes accessed | tf_op | source)
XLA Modules:
  0.0 406.1 jit_solution(10687890163070477907)
XLA Ops:
  6.5 0.0 all-gather.2.cloned.1.call-start
  6.5 0.7 fusion.9
  7.3 2.4 collective-permute-start.1
  9.7 3.4 collective-permute-start
  13.2 1.2 slice_reduce_fusion.7
  14.4 0.9 collective-permute-done
  15.3 0.8 constant_dynamic-update-slice_fusion.1
  16.1 0.0 collective-permute-done.1
  16.2 3.5 collective-permute-start.2
  19.7 5.7 %collective-permute-start.3 = (bf16[4,1,1600]{2,1,0:T(2,128)(2,1)S(1)}, bf16[4,1,1600]{2,1,0:T(2,128)(2,1)S(1)}, u32[]{:S(2)}, u32[]{:S(2)}) collective-permute-start(bf16[4,1,1600]{2,1,0:T(2,128)(2,1)S(1)} %get-tuple-element.27), channel_id=1, source_target_pairs={{1,0},{2,1},{3,2},{4,3},{5,4},{6,5},{7,6},{8,7},{9,8},{10,9},{11,1... | collective-permute-start | bytes 38408 | tf_op jit(solution)/shard_map/ppermute | solution.py:18
  25.4 0.1 add_add_fusion
  25.4 0.0 collective-permute-done.2
  25.5 1.4 collective-permute-done.3
  26.9 1.0 add_divide_fusion
  27.9 0.1 reshape.637
  28.1 0.3 fusion.3
  28.3 0.3 fusion.6
  28.7 0.1 div.36
  28.8 0.2 multiply_reduce_fusion
  29.0 0.1 reshape.638
  29.1 0.1 sqrt.12
  29.2 0.7 divide_convert_fusion
  29.9 0.0 all-gather.2.cloned.1.call-update
  29.9 82.3 %all-gather.2.cloned.1.call-done = bf16[1024,1600]{1,0:T(8,128)(2,1)} async-done(((bf16[8,1600]{1,0:T(8,128)(2,1)}), bf16[1024,1600]{1,0:T(8,128)(2,1)}) %all-gather.2.cloned.1.call-update) | async-done | bytes 3276816 | tf_op jit(solution)/shard_map/all_gather | solution.py:73
  112.2 8.9 %convolution_reduce_fusion = f32[1024]{0:T(1024)S(1)} fusion(bf16[1024,1600]{1,0:T(8,128)(2,1)} %all-gather.2.cloned.1.call-done, bf16[1600,1408]{1,0:T(8,128)(2,1)} %param.5), kind=kOutput, calls=%fused_computation | convolution fusion | flops 4615175168 | bytes 7786496 | tf_op jit(solution)/shard_map/dot_general | solution.py:72
  121.1 277.4 %pmax.7 = f32[1024]{0:T(1024)S(1)} all-reduce(f32[1024]{0:T(1024)S(1)} %convolution_reduce_fusion), channel_id=1, replica_groups=mesh['sx'=4,'sy'=2,'dict'=64] {'sy','dict'}, use_global_device_ids=true, to_apply=%region_3.4 | all-reduce | flops 1024 | bytes 8192 | tf_op jit(solution)/shard_map/pmax | solution.py:78
  398.5 0.1 dynamic_slice.3
  398.6 0.6 reshape.639
  (9 shorter events, 0.1 us)
Async XLA Ops:
  6.5 105.7 %all-gather.2.cloned.1.call-start = ((), (), s32[]{:S(2)}) async-start(), calls=%async_computation | async-start | bytes 3434496 | tf_op jit(solution)/shard_map/all_gather | solution.py:73
  7.3 8.8 %collective-permute-start.1 = (bf16[1,4,1600]{2,1,0:T(4,128)(2,1)S(1)}, bf16[1,4,1600]{2,1,0:T(4,128)(2,1)S(1)}, u32[]{:S(2)}, u32[]{:S(2)}) collective-permute-start(bf16[1,4,1600]{2,1,0:T(4,128)(2,1)S(1)} %get-tuple-element.28), channel_id=1, source_target_pairs={{128,0},{256,128},{384,256},{129,1},{257,129},{385,257},{130,2},{2... | collective-permute-start | bytes 38408 | tf_op jit(solution)/shard_map/ppermute | solution.py:18
  9.7 5.6 %collective-permute-start = (bf16[1,4,1600]{2,1,0:T(4,128)(2,1)S(1)}, bf16[1,4,1600]{2,1,0:T(4,128)(2,1)S(1)}, u32[]{:S(2)}, u32[]{:S(2)}) collective-permute-start(bf16[1,4,1600]{2,1,0:T(4,128)(2,1)S(1)} %get-tuple-element.29), channel_id=1, source_target_pairs={{0,128},{128,256},{256,384},{1,129},{129,257},{257,385},{2,130},{1... | collective-permute-start | bytes 38408 | tf_op jit(solution)/shard_map/ppermute | solution.py:15
  16.2 9.3 %collective-permute-start.2 = (bf16[4,1,1600]{2,1,0:T(2,128)(2,1)S(1)}, bf16[4,1,1600]{2,1,0:T(2,128)(2,1)S(1)}, u32[]{:S(2)}, u32[]{:S(2)}) collective-permute-start(bf16[4,1,1600]{2,1,0:T(2,128)(2,1)S(1)} %get-tuple-element.26), channel_id=1, source_target_pairs={{0,1},{1,2},{2,3},{3,4},{4,5},{5,6},{6,7},{7,8},{8,9},{9,10},{10,1... | collective-permute-start | bytes 38408 | tf_op jit(solution)/shard_map/ppermute | solution.py:15
  19.7 7.2 %collective-permute-start.3 = (bf16[4,1,1600]{2,1,0:T(2,128)(2,1)S(1)}, bf16[4,1,1600]{2,1,0:T(2,128)(2,1)S(1)}, u32[]{:S(2)}, u32[]{:S(2)}) collective-permute-start(bf16[4,1,1600]{2,1,0:T(2,128)(2,1)S(1)} %get-tuple-element.27), channel_id=1, source_target_pairs={{1,0},{2,1},{3,2},{4,3},{5,4},{6,5},{7,6},{8,7},{9,8},{10,9},{11,1... | collective-permute-start | bytes 38408 | tf_op jit(solution)/shard_map/ppermute | solution.py:18
Sparse Core Ops, SparseCore 0:
  30.0 82.1 all-gather.1
where the time goes:
time: 407 us; the launch traced here: 406 us
  blocking collectives  277 us (68%)
  waiting for transfers between devices  84.7 us (21%)
  starting transfers between devices  15 us (4%)
  between operations  13.5 us (3%)
  matrix products  8.89 us (2%)
    pmax x1, blocking collectives, on_device(): merged = lax.pmax(table, ('sy', 'dict'))  277 us
    all_gather x1, waiting for transfers between devices, on_device(): lax.all_gather(normalized, ('sy', 'dict'), axis=0, tiled=True)  82.3 us
    dot_general x1, matrix products, on_device(): jnp.dot(lax.all_gather(normalized, ('sy', 'dict'), axis=0, tiled=True), d...  8.89 us
  transfers between devices with their start and end apart: 5, of which 3 were waited for; matrix products, arithmetic and copies ran while one was open for 1% of the time, Pallas kernels for 0%

commit v1 on v0

v1 whole, which is shorter than its diff:
```python
import jax
import jax.numpy as jnp
from jax import lax
from jax.experimental import pallas as pl
from jax.experimental.pallas import tpu as pltpu
from jax.sharding import Mesh
from jax.sharding import PartitionSpec as P

PH = 40
PW = 40
PIX = PH * PW
WIDE = 1792
COLS = ("sy", "z", "y")


def average_kernel(own_ref, low_ref, high_ref, above_ref, below_ref, weight_ref, out_ref):
    f32 = jnp.float32
    lines = [above_ref[0].astype(f32)]
    for row in range(2):
        lines.append(
            jnp.concatenate(
                [
                    low_ref[row].astype(f32)[3:4],
                    own_ref[row].astype(f32),
                    high_ref[row].astype(f32)[0:1],
                ],
                axis=0,
            )
        )
    lines.append(below_ref[0].astype(f32))
    averaged = []
    for row in range(2):
        weight = weight_ref[row]
        total = jnp.zeros((4, PIX), f32)
        for row_step in range(3):
            for col_step in range(3):
                index = 3 * row_step + col_step
                near = lines[row + row_step][col_step : col_step + 4]
                total = total + weight[:, index : index + 1] * near
        averaged.append(total / weight[:, 9:10])
    image = jnp.concatenate(averaged, axis=0)
    image = jnp.concatenate([image, jnp.zeros((8, WIDE - PIX), f32)], axis=1)
    pixel = lax.broadcasted_iota(jnp.int32, (8, WIDE), 1)
    column = pixel % PW
    vertical = image
    for offset in (-2, -1, 1, 2):
        vertical = vertical + pltpu.roll(image, (-offset * PW) % WIDE, 1)
    box = vertical
    for offset in (-2, -1, 1, 2):
        inside = (column + offset >= 0) & (column + offset < PW)
        box = box + jnp.where(inside, pltpu.roll(vertical, (-offset) % WIDE, 1), 0.0)
    high = jnp.where(pixel < PIX, image - box / 25.0, 0.0)
    mean = jnp.sum(high, axis=1, keepdims=True) / PIX
    centered = jnp.where(pixel < PIX, high - mean, 0.0)
    scale = jnp.sqrt(jnp.sum(centered * centered, axis=1, keepdims=True) / PIX + 1e-06)
    out_ref[...] = (centered / scale)[:, :PIX].astype(jnp.bfloat16)


def average(own, low, high, above, below, weights):
    return pl.pallas_call(
        average_kernel,
        out_shape=jax.ShapeDtypeStruct((8, PIX), jnp.bfloat16),
        in_specs=[pl.BlockSpec(memory_space=pltpu.VMEM)] * 6,
        out_specs=pl.BlockSpec(memory_space=pltpu.VMEM),
        compiler_params=pltpu.CompilerParams(vmem_limit_bytes=16 * 1024 * 1024),
        cost_estimate=pl.CostEstimate(flops=1000000, bytes_accessed=200000, transcendentals=0),
    )(own, low, high, above, below, weights)


CHUNKS = [(0, 384), (384, 384), (768, 384), (1152, 256)]


def best_kernel(first_ref, second_ref, own_ref, partner_ref, out_ref, held, sems):
    copies = []
    for side, source in enumerate((own_ref, partner_ref)):
        for part, (start, size) in enumerate(CHUNKS):
            columns = pl.ds(start, size)
            copy = pltpu.make_async_copy(
                source.at[:, columns], held.at[side, :, columns], sems.at[side, part]
            )
            copy.start()
            copies.append((copy, side, start, size))
    points = jnp.concatenate([first_ref[...], second_ref[...]], axis=0)
    best = jnp.full((256, 128), -jnp.inf, jnp.float32)
    for copy, side, start, size in copies:
        copy.wait()
        scores = jnp.dot(
            points, held[side, :, start : start + size], preferred_element_type=jnp.float32
        )
        for piece in range(0, size, 128):
            best = jnp.maximum(best, scores[:, piece : piece + 128])
    out_ref[...] = jnp.max(best.T, axis=0, keepdims=True)


def best_of(first, second, own, partner):
    vmem = pl.BlockSpec(memory_space=pltpu.VMEM)
    whole = pl.BlockSpec(memory_space=pl.ANY)
    return pl.pallas_call(
        best_kernel,
        out_shape=jax.ShapeDtypeStruct((1, 256), jnp.float32),
        in_specs=[vmem, vmem, whole, whole],
        out_specs=vmem,
        scratch_shapes=[
            pltpu.VMEM((2,) + own.shape, own.dtype),
            pltpu.SemaphoreType.DMA((2, len(CHUNKS))),
        ],
        compiler_params=pltpu.CompilerParams(vmem_limit_bytes=24 * 1024 * 1024),
        cost_estimate=pl.CostEstimate(
            flops=2 * 256 * 2 * own.size, bytes_accessed=4 * own.size, transcendentals=0
        ),
    )(first, second, own, partner)


def place(core, z, y):
    return 64 * core + 8 * (z % 8) + y % 8


def parity_class(core, z_odd, y_odd):
    return [place(core, z, y) for z in range(z_odd, 8, 2) for y in range(y_odd, 8, 2)]


PARITIES = [(0, 0), (0, 1), (1, 0), (1, 1)]


def gather_class(block):
    groups = [parity_class(core, z, y) for core in range(2) for z, y in PARITIES]
    copies = jnp.broadcast_to(block[None], (16,) + block.shape)
    got = lax.all_to_all(copies, COLS, 0, 0, axis_index_groups=groups)
    return got.reshape(-1, block.shape[1])


def from_neighbour(block, z_step, y_step):
    pairs = []
    for core, sign in ((0, 1), (1, -1)):
        for z in range(8):
            for y in range(8):
                source = place(core, z + sign * z_step, y + sign * y_step)
                pairs.append((source, place(core, z, y)))
    return lax.ppermute(block, COLS, pairs)


def merge(tables):
    table = jnp.stack([pair.reshape(2, 128) for pair in tables])
    table = jnp.where(lax.axis_index("z") % 2 == 1, table[::-1], table)
    table = jnp.where(lax.axis_index("y") % 2 == 1, table[:, ::-1], table)
    groups = [sum([parity_class(core, z, y) for z, y in PARITIES], []) for core in range(2)]
    shares = lax.all_to_all(table.reshape(64, -1), COLS, 0, 0, axis_index_groups=groups)
    return jnp.max(shares, axis=0)


def rim(patterns):
    last = 63
    at = lax.axis_index(("z", "y"))
    swap = [pair for k in (0, last) for pair in ((k, 64 + k), (64 + k, k))]
    partner = lax.ppermute(patterns, COLS, swap)
    ahead = [(64 * core + k, 64 * core + (k + 1) % 64) for core in range(2) for k in range(64)]
    behind = [(target, source) for source, target in ahead]
    low = lax.ppermute(jnp.where(at == last, partner, patterns), COLS, ahead)
    high = lax.ppermute(jnp.where(at == 0, partner, patterns), COLS, behind)
    lines = [
        jnp.concatenate([low[r : r + 1, 3:], patterns[r : r + 1], high[r : r + 1, :1]], axis=1)
        for r in range(2)
    ]
    down = [(i, i + 1) for i in range(3)]
    above = lax.ppermute(lines[1], "sx", down)
    below = lax.ppermute(lines[0], "sx", [(target, source) for source, target in down])
    return low, high, above, below


def valid_weights(weights, rows, cols):
    row = lax.axis_index("sx") * rows + jnp.arange(rows)
    col = lax.axis_index(COLS) * cols + jnp.arange(cols)
    steps = jnp.arange(-1, 2)
    row_near = row[:, None] + steps
    col_near = col[:, None] + steps
    row_valid = (row_near >= 0) & (row_near < rows * lax.axis_size("sx"))
    col_valid = (col_near >= 0) & (col_near < cols * lax.axis_size(COLS))
    valid = row_valid[:, None, :, None] & col_valid[None, :, None, :]
    kept = jnp.where(valid.reshape(rows, cols, 9), jnp.transpose(weights, (1, 2, 0)), 0.0)
    return jnp.concatenate([kept, jnp.sum(kept, axis=2, keepdims=True)], axis=2)


def on_device(patterns, nlpar_weights, dictionary):
    rows, cols = patterns.shape[:2]
    partner = lax.ppermute(dictionary, "sy", [(0, 1), (1, 0)])
    weights = valid_weights(nlpar_weights, rows, cols)
    normalized = average(patterns, *rim(patterns), weights)
    own = gather_class(normalized)
    ahead = from_neighbour(own, 0, 1)
    across = from_neighbour(own, 1, 0)
    diagonal = from_neighbour(own, 1, 1)
    tables = [
        best_of(own, ahead, dictionary, partner),
        best_of(across, diagonal, dictionary, partner),
    ]
    return merge(tables).reshape(rows, cols)


def solution(mesh):
    split = Mesh(mesh.devices.reshape(4, 2, 8, 8), ("sx",) + COLS)
    return jax.shard_map(
        on_device,
        mesh=split,
        in_specs=(
            P("sx", COLS, None),
            P(None, "sx", COLS),
            P(None, COLS),
        ),
        out_specs=P("sx", COLS),
        check_vma=False,
    )
```

time: 407 us -> 102 us (0.25)
  the two profiles are of different devices: /device:TPU:258 before, /device:TPU:2 now
where the time goes in v1:
time: 102 us
  blocking collectives  35.7 us (35%)
  starting transfers between devices  34.4 us (34%)
  Pallas kernels  12.9 us (13%)
  waiting for transfers between devices  11.8 us (12%)
  local copies, waits for them, and re-layouts  4.94 us (5%)
  other arithmetic  1.94 us (2%)
    all_to_all x1, blocking collectives, merge(): lax.all_to_all(table.reshape(64, -1), COLS, 0, 0, axis_index_groups=groups)  18.2 us
    all_to_all x1, blocking collectives, gather_class(): got = lax.all_to_all(copies, COLS, 0, 0, axis_index_groups=groups)  17.5 us
    ppermute x1, starting transfers between devices, rim(): high = lax.ppermute(jnp.where(at == 0, partner, patterns), COLS, behind)  13.8 us
    pallas_call x2, Pallas kernels, best_of(): pl.pallas_call(best_kernel, out_shape=jax.ShapeDtypeStruct((1, 256), jnp....  12.3 us
    ppermute x3, starting transfers between devices, from_neighbour(): return lax.ppermute(block, COLS, pairs)  8.48 us
    ppermute x1, waiting for transfers between devices, rim(): low = lax.ppermute(jnp.where(at == last, partner, patterns), COLS, ahead)  7.1 us
    ppermute x1, starting transfers between devices, rim(): above = lax.ppermute(lines[1], 'sx', down)  3.4 us
    ppermute x1, waiting for transfers between devices, rim(): lax.ppermute(lines[0], 'sx', [(target, source) for source, target in down])  3.21 us
  transfers between devices with their start and end apart: 9, of which 3 were waited for; matrix products, arithmetic and copies ran while one was open for 3% of the time, Pallas kernels for 7%

profile of v1, /device:TPU:2, one launch (start us, length us, event | category | flops | bytes accessed | tf_op | source)
XLA Modules:
  0.0 101.9 jit_solution(13653344722544484683)
XLA Ops:
  0.0 1.9 %collective-permute-start = (bf16[2,4,1600]{2,1,0:T(4,128)(2,1)}, bf16[2,4,1600]{2,1,0:T(4,128)(2,1)S(1)}, u32[]{:S(2)}, u32[]{:S(2)}) collective-permute-start(bf16[2,4,1600]{2,1,0:T(4,128)(2,1)} %own_ref.3), channel_id=1, source_target_pairs={{0,64},{64,0},{63,127},{127,63},{128,192},{192,128},{191,255},{255... | collective-permute-start | bytes 76808 | tf_op jit(solution)/shard_map/ppermute | solution.py:155
  1.9 2.4 %collective-permute-start.6 = (bf16[1600,1408]{1,0:T(8,128)(2,1)}, bf16[1600,1408]{1,0:T(8,128)(2,1)}, u32[]{:S(2)}, u32[]{:S(2)}) collective-permute-start(bf16[1600,1408]{1,0:T(8,128)(2,1)} %own_ref.5), channel_id=1, source_target_pairs={{0,64},{64,0},{1,65},{65,1},{2,66},{66,2},{3,67},{67,3},{4,68},{68... | collective-permute-start | bytes 13516808 | tf_op jit(solution)/shard_map/ppermute | solution.py:185
  4.4 0.1 fusion
  4.5 0.7 fusion.3
  5.2 0.1 compare_and_fusion
  5.3 0.1 and.57
  5.4 0.1 and.52
  5.4 0.1 and.53
  5.5 0.8 broadcast_select_fusion
  6.3 13.8 %collective-permute-start.2 = (bf16[2,4,1600]{2,1,0:T(4,128)(2,1)S(1)}, bf16[2,4,1600]{2,1,0:T(4,128)(2,1)S(1)}, u32[]{:S(2)}, u32[]{:S(2)}) collective-permute-start(bf16[2,4,1600]{2,1,0:T(4,128)(2,1)S(1)} %bitcast.22), channel_id=1, source_target_pairs={{1,0},{2,1},{3,2},{4,3},{5,4},{6,5},{7,6},{8,7},{9,8},{10,9},{11,1... | collective-permute-start | bytes 76808 | tf_op jit(solution)/shard_map/ppermute | solution.py:159
  20.1 0.8 fusion.1
  20.9 0.1 copy.6
  21.0 1.9 %collective-permute-start.1 = (bf16[2,4,1600]{2,1,0:T(4,128)(2,1)S(1)}, bf16[2,4,1600]{2,1,0:T(4,128)(2,1)S(1)}, u32[]{:S(2)}, u32[]{:S(2)}) collective-permute-start(bf16[2,4,1600]{2,1,0:T(4,128)(2,1)S(1)} %bitcast.21), channel_id=1, source_target_pairs={{0,1},{1,2},{2,3},{3,4},{4,5},{5,6},{6,7},{7,8},{8,9},{9,10},{10,1... | collective-permute-start | bytes 76808 | tf_op jit(solution)/shard_map/ppermute | solution.py:158
  23.0 7.1 %collective-permute-done.1.low_ref = bf16[2,4,1600]{2,1,0:T(4,128)(2,1)S(1)} collective-permute-done((bf16[2,4,1600]{2,1,0:T(4,128)(2,1)S(1)}, bf16[2,4,1600]{2,1,0:T(4,128)(2,1)S(1)}, u32[]{:S(2)}, u32[]{:S(2)}) %collective-permute-start.1) | collective-permute-done | bytes 25632 | tf_op jit(solution)/shard_map/ppermute | solution.py:158
  30.1 3.4 %collective-permute-start.3 = (bf16[1,6,1600]{2,1,0:T(8,128)(2,1)S(1)}, bf16[1,6,1600]{2,1,0:T(8,128)(2,1)S(1)}, u32[]{:S(2)}, u32[]{:S(2)}) collective-permute-start(bf16[1,6,1600]{2,1,0:T(8,128)(2,1)S(1)} %pad_maximum_fusion), channel_id=1, source_target_pairs={{0,128},{128,256},{256,384},{1,129},{129,257},{257,385},{2,130},{1... | collective-permute-start | bytes 57608 | tf_op jit(solution)/shard_map/ppermute | solution.py:165
  33.6 2.4 %collective-permute-start.4 = (bf16[1,6,1600]{2,1,0:T(8,128)(2,1)S(1)}, bf16[1,6,1600]{2,1,0:T(8,128)(2,1)S(1)}, u32[]{:S(2)}, u32[]{:S(2)}) collective-permute-start(bf16[1,6,1600]{2,1,0:T(8,128)(2,1)S(1)} %pad_maximum_fusion.1), channel_id=1, source_target_pairs={{128,0},{256,128},{384,256},{129,1},{257,129},{385,257},{130,2},{2... | collective-permute-start | bytes 57608 | tf_op jit(solution)/shard_map/ppermute | solution.py:166
  36.0 0.1 pad_maximum_fusion.2.weight_ref
  36.1 3.2 %collective-permute-done.4.below_ref = bf16[1,6,1600]{2,1,0:T(8,128)(2,1)S(1)} collective-permute-done((bf16[1,6,1600]{2,1,0:T(8,128)(2,1)S(1)}, bf16[1,6,1600]{2,1,0:T(8,128)(2,1)S(1)}, u32[]{:S(2)}, u32[]{:S(2)}) %collective-permute-start.4) | collective-permute-done | bytes 19232 | tf_op jit(solution)/shard_map/ppermute | solution.py:166
  39.3 0.7 copy-done.2
  40.1 0.6 shard_map.37
  40.7 17.5 %all_to_all.14 = bf16[16,8,1600]{2,1,0:T(8,128)(2,1)S(1)} all-to-all(bf16[16,8,1600]{2,1,0:T(8,128)(2,1)S(1)} %broadcast_in_dim.10), channel_id=1, replica_groups={{0,2,4,6,16,18,20,22,32,34,36,38,48,50,52,54},{1,3,5,7,17,19,21,23,33,3..., dimensions={0} | all-to-all | bytes 819200 | tf_op jit(solution)/shard_map/all_to_all | solution.py:128
  58.2 2.0 %collective-permute-start.5 = (bf16[128,1600]{1,0:T(8,128)(2,1)S(1)}, bf16[128,1600]{1,0:T(8,128)(2,1)S(1)}, u32[]{:S(2)}, u32[]{:S(2)}) collective-permute-start(bf16[128,1600]{1,0:T(8,128)(2,1)S(1)} %bitcast.12), channel_id=1, source_target_pairs={{1,0},{2,1},{3,2},{4,3},{5,4},{6,5},{7,6},{0,7},{9,8},{10,9},{11,1... | collective-permute-start | bytes 1228808 | tf_op jit(solution)/shard_map/ppermute | solution.py:139
  60.2 3.0 %collective-permute-start.7 = (bf16[128,1600]{1,0:T(8,128)(2,1)S(1)}, bf16[128,1600]{1,0:T(8,128)(2,1)S(1)}, u32[]{:S(2)}, u32[]{:S(2)}) collective-permute-start(bf16[128,1600]{1,0:T(8,128)(2,1)S(1)} %bitcast.13), channel_id=1, source_target_pairs={{8,0},{9,1},{10,2},{11,3},{12,4},{13,5},{14,6},{15,7},{16,8},{17,9... | collective-permute-start | bytes 1228808 | tf_op jit(solution)/shard_map/ppermute | solution.py:139
  63.2 3.4 %collective-permute-start.8 = (bf16[128,1600]{1,0:T(8,128)(2,1)S(1)}, bf16[128,1600]{1,0:T(8,128)(2,1)S(1)}, u32[]{:S(2)}, u32[]{:S(2)}) collective-permute-start(bf16[128,1600]{1,0:T(8,128)(2,1)S(1)} %bitcast.14), channel_id=1, source_target_pairs={{9,0},{10,1},{11,2},{12,3},{13,4},{14,5},{15,6},{8,7},{17,8},{18,9... | collective-permute-start | bytes 1228808 | tf_op jit(solution)/shard_map/ppermute | solution.py:139
  66.7 1.5 %collective-permute-done.5.second_ref = bf16[128,1600]{1,0:T(8,128)(2,1)S(1)} collective-permute-done((bf16[128,1600]{1,0:T(8,128)(2,1)S(1)}, bf16[128,1600]{1,0:T(8,128)(2,1)S(1)}, u32[]{:S(2)}, u32[]{:S(2)}) %collective-permute-start.5) | collective-permute-done | bytes 409632 | tf_op jit(solution)/shard_map/ppermute | solution.py:139
  68.2 2.3 %copy-done = bf16[1600,1408]{1,0:T(8,128)(2,1)S(1)} copy-done((bf16[1600,1408]{1,0:T(8,128)(2,1)S(1)}, bf16[1600,1408]{1,0:T(8,128)(2,1)}, u32[]{:S(2)}) %copy-start) | copy-done | bytes 4505624
  70.5 6.1 %shard_map.38 = f32[1,256]{1,0:T(1,128)S(1)} custom-call(bf16[128,1600]{1,0:T(8,128)(2,1)S(1)} %bitcast.15, bf16[128,1600]{1,0:T(8,128)(2,1)S(1)} %collective-permute-done.5.second_ref, bf16[1600,1408]{1,0:T(8,128)(2,1)S(1)} %copy-done, bf16[1600,1408]{1,0:T(8,128)(2,1)} %collective-permute-done.6.partner_ref), custom_call_target="tpu_custom_call" | custom-call | flops 2306867200 | bytes 9011200 | tf_op jit(solution)/shard_map/pallas_call | solution.py:98
  76.6 6.2 %shard_map.39 = f32[1,256]{1,0:T(1,128)S(1)} custom-call(bf16[128,1600]{1,0:T(8,128)(2,1)S(1)} %collective-permute-done.7.first_ref, bf16[128,1600]{1,0:T(8,128)(2,1)S(1)} %collective-permute-done.8.second_ref, bf16[1600,1408]{1,0:T(8,128)(2,1)S(1)} %copy-done.1, bf16[1600,1408]{1,0:T(8,128)(2,1)} %collective-permute-done.6.partner_ref), custom_call_target="tpu_custom_call" | custom-call | flops 2306867200 | bytes 9011200 | tf_op jit(solution)/shard_map/pallas_call | solution.py:98
  82.9 0.1 all_to_all.10
  83.0 18.2 %all_to_all.15 = f32[64,1,8]{2,1,0:T(1,128)S(1)} all-to-all(f32[64,1,8]{2,1,0:T(1,128)S(1)} %bitcast.19), channel_id=1, replica_groups={{0,2,4,6,16,18,20,22,32,34,36,38,48,50,52,54,1,3,5,7,17,19,21,23,33,35,..., dimensions={0} | all-to-all | bytes 4096 | tf_op jit(solution)/shard_map/all_to_all | solution.py:147
  101.1 0.1 reduce_max.9
  101.2 0.6 reshape.85
  (23 shorter events, 0.2 us)
Async XLA Ops:
  0.0 5.5 %collective-permute-start = (bf16[2,4,1600]{2,1,0:T(4,128)(2,1)}, bf16[2,4,1600]{2,1,0:T(4,128)(2,1)S(1)}, u32[]{:S(2)}, u32[]{:S(2)}) collective-permute-start(bf16[2,4,1600]{2,1,0:T(4,128)(2,1)} %own_ref.3), channel_id=1, source_target_pairs={{0,64},{64,0},{63,127},{127,63},{128,192},{192,128},{191,255},{255... | collective-permute-start | bytes 76808 | tf_op jit(solution)/shard_map/ppermute | solution.py:155
  1.9 66.3 %collective-permute-start.6 = (bf16[1600,1408]{1,0:T(8,128)(2,1)}, bf16[1600,1408]{1,0:T(8,128)(2,1)}, u32[]{:S(2)}, u32[]{:S(2)}) collective-permute-start(bf16[1600,1408]{1,0:T(8,128)(2,1)} %own_ref.5), channel_id=1, source_target_pairs={{0,64},{64,0},{1,65},{65,1},{2,66},{66,2},{3,67},{67,3},{4,68},{68... | collective-permute-start | bytes 13516808 | tf_op jit(solution)/shard_map/ppermute | solution.py:185
  6.3 16.7 %collective-permute-start.2 = (bf16[2,4,1600]{2,1,0:T(4,128)(2,1)S(1)}, bf16[2,4,1600]{2,1,0:T(4,128)(2,1)S(1)}, u32[]{:S(2)}, u32[]{:S(2)}) collective-permute-start(bf16[2,4,1600]{2,1,0:T(4,128)(2,1)S(1)} %bitcast.22), channel_id=1, source_target_pairs={{1,0},{2,1},{3,2},{4,3},{5,4},{6,5},{7,6},{8,7},{9,8},{10,9},{11,1... | collective-permute-start | bytes 76808 | tf_op jit(solution)/shard_map/ppermute | solution.py:159
  21.0 9.1 %collective-permute-start.1 = (bf16[2,4,1600]{2,1,0:T(4,128)(2,1)S(1)}, bf16[2,4,1600]{2,1,0:T(4,128)(2,1)S(1)}, u32[]{:S(2)}, u32[]{:S(2)}) collective-permute-start(bf16[2,4,1600]{2,1,0:T(4,128)(2,1)S(1)} %bitcast.21), channel_id=1, source_target_pairs={{0,1},{1,2},{2,3},{3,4},{4,5},{5,6},{6,7},{7,8},{8,9},{9,10},{10,1... | collective-permute-start | bytes 76808 | tf_op jit(solution)/shard_map/ppermute | solution.py:158
  30.1 6.0 %collective-permute-start.3 = (bf16[1,6,1600]{2,1,0:T(8,128)(2,1)S(1)}, bf16[1,6,1600]{2,1,0:T(8,128)(2,1)S(1)}, u32[]{:S(2)}, u32[]{:S(2)}) collective-permute-start(bf16[1,6,1600]{2,1,0:T(8,128)(2,1)S(1)} %pad_maximum_fusion), channel_id=1, source_target_pairs={{0,128},{128,256},{256,384},{1,129},{129,257},{257,385},{2,130},{1... | collective-permute-start | bytes 57608 | tf_op jit(solution)/shard_map/ppermute | solution.py:165
  33.6 5.7 %collective-permute-start.4 = (bf16[1,6,1600]{2,1,0:T(8,128)(2,1)S(1)}, bf16[1,6,1600]{2,1,0:T(8,128)(2,1)S(1)}, u32[]{:S(2)}, u32[]{:S(2)}) collective-permute-start(bf16[1,6,1600]{2,1,0:T(8,128)(2,1)S(1)} %pad_maximum_fusion.1), channel_id=1, source_target_pairs={{128,0},{256,128},{384,256},{129,1},{257,129},{385,257},{130,2},{2... | collective-permute-start | bytes 57608 | tf_op jit(solution)/shard_map/ppermute | solution.py:166
  39.3 0.7 copy-start.2
  58.2 10.0 %collective-permute-start.5 = (bf16[128,1600]{1,0:T(8,128)(2,1)S(1)}, bf16[128,1600]{1,0:T(8,128)(2,1)S(1)}, u32[]{:S(2)}, u32[]{:S(2)}) collective-permute-start(bf16[128,1600]{1,0:T(8,128)(2,1)S(1)} %bitcast.12), channel_id=1, source_target_pairs={{1,0},{2,1},{3,2},{4,3},{5,4},{6,5},{7,6},{0,7},{9,8},{10,9},{11,1... | collective-permute-start | bytes 1228808 | tf_op jit(solution)/shard_map/ppermute | solution.py:139
  60.2 16.4 %collective-permute-start.7 = (bf16[128,1600]{1,0:T(8,128)(2,1)S(1)}, bf16[128,1600]{1,0:T(8,128)(2,1)S(1)}, u32[]{:S(2)}, u32[]{:S(2)}) collective-permute-start(bf16[128,1600]{1,0:T(8,128)(2,1)S(1)} %bitcast.13), channel_id=1, source_target_pairs={{8,0},{9,1},{10,2},{11,3},{12,4},{13,5},{14,6},{15,7},{16,8},{17,9... | collective-permute-start | bytes 1228808 | tf_op jit(solution)/shard_map/ppermute | solution.py:139
  63.2 13.4 %collective-permute-start.8 = (bf16[128,1600]{1,0:T(8,128)(2,1)S(1)}, bf16[128,1600]{1,0:T(8,128)(2,1)S(1)}, u32[]{:S(2)}, u32[]{:S(2)}) collective-permute-start(bf16[128,1600]{1,0:T(8,128)(2,1)S(1)} %bitcast.14), channel_id=1, source_target_pairs={{9,0},{10,1},{11,2},{12,3},{13,4},{14,5},{15,6},{8,7},{17,8},{18,9... | collective-permute-start | bytes 1228808 | tf_op jit(solution)/shard_map/ppermute | solution.py:139
  68.2 2.3 %copy-start = (bf16[1600,1408]{1,0:T(8,128)(2,1)S(1)}, bf16[1600,1408]{1,0:T(8,128)(2,1)}, u32[]{:S(2)}) copy-start(bf16[1600,1408]{1,0:T(8,128)(2,1)} %own_ref.5) | copy-start | bytes 13516804
  70.5 6.2 %copy-start.1 = (bf16[1600,1408]{1,0:T(8,128)(2,1)S(1)}, bf16[1600,1408]{1,0:T(8,128)(2,1)}, u32[]{:S(2)}) copy-start(bf16[1600,1408]{1,0:T(8,128)(2,1)} %own_ref.5) | copy-start | bytes 13516804

commit v2 on v1

v2 whole, which is shorter than its diff:
```python
import jax
import jax.numpy as jnp
from jax import lax
from jax.experimental import pallas as pl
from jax.experimental.pallas import tpu as pltpu
from jax.sharding import Mesh
from jax.sharding import PartitionSpec as P

PH = 40
PW = 40
PIX = PH * PW
WIDE = 1792
COLS = ("sy", "z", "y")


def average_kernel(block_ref, low_ref, high_ref, weight_ref, out_ref):
    f32 = jnp.float32
    lines = [
        jnp.concatenate([low_ref[row], block_ref[row], high_ref[row]], axis=0).astype(f32)
        for row in range(4)
    ]
    averaged = []
    for row in range(2):
        weight = weight_ref[row]
        total = jnp.zeros((4, PIX), f32)
        for row_step in range(3):
            for col_step in range(3):
                index = 3 * row_step + col_step
                near = lines[row + row_step][col_step : col_step + 4]
                total = total + weight[:, index : index + 1] * near
        averaged.append(total / weight[:, 9:10])
    image = jnp.concatenate(averaged, axis=0)
    image = jnp.concatenate([image, jnp.zeros((8, WIDE - PIX), f32)], axis=1)
    pixel = lax.broadcasted_iota(jnp.int32, (8, WIDE), 1)
    column = pixel % PW
    vertical = image
    for offset in (-2, -1, 1, 2):
        vertical = vertical + pltpu.roll(image, (-offset * PW) % WIDE, 1)
    box = vertical
    for offset in (-2, -1, 1, 2):
        inside = (column + offset >= 0) & (column + offset < PW)
        box = box + jnp.where(inside, pltpu.roll(vertical, (-offset) % WIDE, 1), 0.0)
    high = jnp.where(pixel < PIX, image - box / 25.0, 0.0)
    mean = jnp.sum(high, axis=1, keepdims=True) / PIX
    centered = jnp.where(pixel < PIX, high - mean, 0.0)
    scale = jnp.sqrt(jnp.sum(centered * centered, axis=1, keepdims=True) / PIX + 1e-06)
    out_ref[...] = (centered / scale)[:, :PIX].astype(jnp.bfloat16)


def average(block, low, high, weights):
    return pl.pallas_call(
        average_kernel,
        out_shape=jax.ShapeDtypeStruct((8, PIX), jnp.bfloat16),
        in_specs=[pl.BlockSpec(memory_space=pltpu.VMEM)] * 4,
        out_specs=pl.BlockSpec(memory_space=pltpu.VMEM),
        compiler_params=pltpu.CompilerParams(vmem_limit_bytes=16 * 1024 * 1024),
        cost_estimate=pl.CostEstimate(flops=1000000, bytes_accessed=200000, transcendentals=0),
    )(block, low, high, weights)


def hold_kernel(own_ref, partner_ref, own_held, partner_held, sems):
    copies = [
        pltpu.make_async_copy(own_ref, own_held, sems.at[0]),
        pltpu.make_async_copy(partner_ref, partner_held, sems.at[1]),
    ]
    for copy in copies:
        copy.start()
    for copy in copies:
        copy.wait()


def hold(own, partner):
    return pl.pallas_call(
        hold_kernel,
        out_shape=[pltpu.VMEM(half.shape, half.dtype) for half in (own, partner)],
        in_specs=[pl.BlockSpec(memory_space=space) for space in (pltpu.HBM, pl.ANY)],
        out_specs=[pl.BlockSpec(memory_space=pltpu.VMEM)] * 2,
        scratch_shapes=[pltpu.SemaphoreType.DMA((2,))],
        compiler_params=pltpu.CompilerParams(vmem_limit_bytes=16 * 1024 * 1024),
        cost_estimate=pl.CostEstimate(
            flops=0, bytes_accessed=2 * 4 * own.size, transcendentals=0
        ),
    )(pltpu.with_memory_space_constraint(own, pltpu.HBM), partner)


def row_best(points, half):
    scores = jnp.dot(points, half, preferred_element_type=jnp.float32)
    return jnp.max(scores, axis=1)


def best_of(first, second, halves):
    points = jnp.concatenate([first, second], axis=0)
    return jnp.maximum(*[row_best(points, half) for half in halves])


def place(core, z, y):
    return 64 * core + 8 * (z % 8) + y % 8


def parity_class(core, z_odd, y_odd):
    return [place(core, z, y) for z in range(z_odd, 8, 2) for y in range(y_odd, 8, 2)]


PARITIES = [(0, 0), (0, 1), (1, 0), (1, 1)]


def gather_class(block):
    groups = [parity_class(core, z, y) for core in range(2) for z, y in PARITIES]
    copies = jnp.broadcast_to(block[None], (16,) + block.shape)
    got = lax.all_to_all(copies, COLS, 0, 0, axis_index_groups=groups)
    return got.reshape(-1, block.shape[1])


def from_neighbour(block, z_step, y_step):
    pairs = []
    for core, sign in ((0, 1), (1, -1)):
        for z in range(8):
            for y in range(8):
                source = place(core, z + sign * z_step, y + sign * y_step)
                pairs.append((source, place(core, z, y)))
    return lax.ppermute(block, COLS, pairs)


def merge(tables):
    table = jnp.stack([pair.reshape(2, 128) for pair in tables])
    table = jnp.where(lax.axis_index("z") % 2 == 1, table[::-1], table)
    table = jnp.where(lax.axis_index("y") % 2 == 1, table[:, ::-1], table)
    groups = [sum([parity_class(core, z, y) for z, y in PARITIES], []) for core in range(2)]
    shares = lax.all_to_all(table.reshape(64, -1), COLS, 0, 0, axis_index_groups=groups)
    return jnp.max(shares, axis=0)


def rim(patterns):
    count = lax.axis_size(COLS)
    down = [(i, i + 1) for i in range(3)]
    up = [(target, source) for source, target in down]
    below = lax.ppermute(patterns, "sx", up)[:1]
    above = lax.ppermute(patterns, "sx", down)[1:]
    block = jnp.concatenate([above, patterns, below], axis=0)
    ahead = [(i, i + 1) for i in range(count - 1)]
    behind = [(target, source) for source, target in ahead]
    low = lax.ppermute(block[:, 3:4], COLS, ahead)
    high = lax.ppermute(block[:, 0:1], COLS, behind)
    return block, low, high


def valid_weights(weights, rows, cols):
    row = lax.axis_index("sx") * rows + jnp.arange(rows)
    col = lax.axis_index(COLS) * cols + jnp.arange(cols)
    steps = jnp.arange(-1, 2)
    row_near = row[:, None] + steps
    col_near = col[:, None] + steps
    row_valid = (row_near >= 0) & (row_near < rows * lax.axis_size("sx"))
    col_valid = (col_near >= 0) & (col_near < cols * lax.axis_size(COLS))
    valid = row_valid[:, None, :, None] & col_valid[None, :, None, :]
    kept = jnp.where(valid.reshape(rows, cols, 9), jnp.transpose(weights, (1, 2, 0)), 0.0)
    return jnp.concatenate([kept, jnp.sum(kept, axis=2, keepdims=True)], axis=2)


def on_device(patterns, nlpar_weights, dictionary):
    rows, cols = patterns.shape[:2]
    shared, patterns = lax.optimization_barrier((dictionary, patterns))
    partner = lax.ppermute(shared, "sy", [(0, 1), (1, 0)])
    weights = valid_weights(nlpar_weights, rows, cols)
    normalized = average(*rim(patterns), weights)
    own = gather_class(normalized)
    ahead = from_neighbour(own, 0, 1)
    across = from_neighbour(own, 1, 0)
    diagonal = from_neighbour(own, 1, 1)
    ahead, *halves = lax.optimization_barrier((ahead, dictionary, partner))
    halves = hold(*halves)
    early = best_of(own, ahead, halves)
    early, across, diagonal = lax.optimization_barrier((early, across, diagonal))
    tables = [early, best_of(across, diagonal, halves)]
    return merge(tables).reshape(rows, cols)


def solution(mesh):
    split = Mesh(mesh.devices.reshape(4, 2, 8, 8), ("sx",) + COLS)
    return jax.shard_map(
        on_device,
        mesh=split,
        in_specs=(
            P("sx", COLS, None),
            P(None, "sx", COLS),
            P(None, COLS),
        ),
        out_specs=P("sx", COLS),
        check_vma=False,
    )
```

time: 102 us -> 95.1 us (0.932)
  blocking collectives: 35.7 us -> 49.9 us
  starting transfers between devices: 34.4 us -> 22.6 us
  Pallas kernels: 12.9 us -> 4.26 us
  matrix products: 0 us -> 6.7 us
  waiting for transfers between devices: 11.8 us -> 7.76 us
  local copies, waits for them, and re-layouts: 4.94 us -> 1.29 us
    all_to_all x1, blocking collectives: 17.5 us -> 30.8 us  [gather_class(): got = lax.all_to_all(copies, COLS, 0, 0, axis_index_groups=groups)]
    ppermute x6 -> x5, starting transfers between devices: 25.9 us -> 14.3 us  [the longest x1 5.71 us: rim(): below = lax.ppermute(patterns, 'sx', up)[:1]]
    pallas_call x2 -> x1, Pallas kernels: 12.3 us -> 3.67 us  [hold(): pl.pallas_call(hold_kernel, out_shape=[pltpu.VMEM(half.shape, half.dtype)...]
    dot_general x0 -> x4, matrix products: none -> 6.7 us  [row_best(): scores = jnp.dot(points, half, preferred_element_type=jnp.float32)]
    ppermute x6 -> x5, waiting for transfers between devices: 10.3 us -> 4.74 us  [the longest x1 4.22 us: rim(): high = lax.ppermute(block[:, 0:1], COLS, behind)]
    unnamed x6 -> x1, local copies, waits for them, and re-layouts: 3.02 us -> 0.03 us
    ppermute x3, waiting for transfers between devices: 1.49 us -> 3.02 us  [from_neighbour(): return lax.ppermute(block, COLS, pairs)]
  transfers between devices with their start and end apart: 9 -> 8, of which waited for: 3 -> 5; matrix products, arithmetic and copies ran while one was open for 3% -> 6% of each run, Pallas kernels for 7% -> 5%
where the time goes in v2:
time: 95.1 us; the launch traced here: 94.7 us
  blocking collectives  49.9 us (52%)
  starting transfers between devices  22.6 us (24%)
  waiting for transfers between devices  7.76 us (8%)
  matrix products  6.7 us (7%)
  Pallas kernels  4.26 us (4%)
  other arithmetic  1.92 us (2%)
  local copies, waits for them, and re-layouts  1.29 us (1%)
    all_to_all x1, blocking collectives, gather_class(): got = lax.all_to_all(copies, COLS, 0, 0, axis_index_groups=groups)  30.8 us
    all_to_all x1, blocking collectives, merge(): lax.all_to_all(table.reshape(64, -1), COLS, 0, 0, axis_index_groups=groups)  19.1 us
    ppermute x3, starting transfers between devices, from_neighbour(): return lax.ppermute(block, COLS, pairs)  8.32 us
    dot_general x4, matrix products, row_best(): scores = jnp.dot(points, half, preferred_element_type=jnp.float32)  6.7 us
    ppermute x1, starting transfers between devices, rim(): below = lax.ppermute(patterns, 'sx', up)[:1]  5.71 us
    ppermute x1, waiting for transfers between devices, rim(): high = lax.ppermute(block[:, 0:1], COLS, behind)  4.22 us
    pallas_call x1, Pallas kernels, hold(): pl.pallas_call(hold_kernel, out_shape=[pltpu.VMEM(half.shape, half.dtype)...  3.67 us
    ppermute x1, starting transfers between devices, rim(): above = lax.ppermute(patterns, 'sx', down)[1:]  3.4 us
  transfers between devices with their start and end apart: 8, of which 5 were waited for; matrix products, arithmetic and copies ran while one was open for 6% of the time, Pallas kernels for 5%

profile of v2, /device:TPU:2, one launch (start us, length us, event | category | flops | bytes accessed | tf_op | source)
XLA Modules:
  0.0 94.7 jit_solution(18107425821795572716)
XLA Ops:
  0.0 1.9 %collective-permute-start.5 = (bf16[1600,1408]{1,0:T(8,128)(2,1)}, bf16[1600,1408]{1,0:T(8,128)(2,1)}, u32[]{:S(2)}, u32[]{:S(2)}) collective-permute-start(bf16[1600,1408]{1,0:T(8,128)(2,1)} %own_ref), channel_id=1, source_target_pairs={{0,64},{64,0},{1,65},{65,1},{2,66},{66,2},{3,67},{67,3},{4,68},{68... | collective-permute-start | bytes 13516808 | tf_op jit(solution)/shard_map/ppermute | solution.py:163
  1.9 3.4 %collective-permute-start = (bf16[2,4,1600]{2,1,0:T(4,128)(2,1)}, bf16[2,4,1600]{2,1,0:T(4,128)(2,1)S(1)}, u32[]{:S(2)}, u32[]{:S(2)}) collective-permute-start(bf16[2,4,1600]{2,1,0:T(4,128)(2,1)} %param.3), channel_id=1, source_target_pairs={{0,128},{128,256},{256,384},{1,129},{129,257},{257,385},{2,130},{1... | collective-permute-start | bytes 76808 | tf_op jit(solution)/shard_map/ppermute | solution.py:138
  5.3 5.7 %collective-permute-start.1 = (bf16[2,4,1600]{2,1,0:T(4,128)(2,1)}, bf16[2,4,1600]{2,1,0:T(4,128)(2,1)S(1)}, u32[]{:S(2)}, u32[]{:S(2)}) collective-permute-start(bf16[2,4,1600]{2,1,0:T(4,128)(2,1)} %param.3), channel_id=1, source_target_pairs={{128,0},{256,128},{384,256},{129,1},{257,129},{385,257},{130,2},{2... | collective-permute-start | bytes 76808 | tf_op jit(solution)/shard_map/ppermute | solution.py:137
  11.2 0.1 and.57
  11.3 0.1 compare_and_fusion
  11.3 0.1 and.52
  11.4 0.1 and.53
  11.5 0.8 fusion.3
  12.3 0.1 copy.6
  12.4 0.4 collective-permute-done.1
  12.8 0.8 pad_maximum_fusion.3.block_ref
  13.6 2.0 %collective-permute-start.2 = (bf16[4,1,1600]{2,1,0:T(2,128)(2,1)S(1)}, bf16[4,1,1600]{2,1,0:T(2,128)(2,1)S(1)}, u32[]{:S(2)}, u32[]{:S(2)}) collective-permute-start(bf16[4,1,1600]{2,1,0:T(2,128)(2,1)S(1)} %get-tuple-element.28), channel_id=1, source_target_pairs={{0,1},{1,2},{2,3},{3,4},{4,5},{5,6},{6,7},{7,8},{8,9},{9,10},{10,1... | collective-permute-start | bytes 38408 | tf_op jit(solution)/shard_map/ppermute | solution.py:142
  15.6 1.3 %collective-permute-start.3 = (bf16[4,1,1600]{2,1,0:T(2,128)(2,1)S(1)}, bf16[4,1,1600]{2,1,0:T(2,128)(2,1)S(1)}, u32[]{:S(2)}, u32[]{:S(2)}) collective-permute-start(bf16[4,1,1600]{2,1,0:T(2,128)(2,1)S(1)} %get-tuple-element.27), channel_id=1, source_target_pairs={{1,0},{2,1},{3,2},{4,3},{5,4},{6,5},{7,6},{8,7},{9,8},{10,9},{11,1... | collective-permute-start | bytes 38408 | tf_op jit(solution)/shard_map/ppermute | solution.py:143
  16.9 0.1 pad_maximum_fusion.4.weight_ref
  17.0 0.1 collective-permute-done.2.low_ref
  17.1 4.2 %collective-permute-done.3.high_ref = bf16[4,1,1600]{2,1,0:T(2,128)(2,1)S(1)} collective-permute-done((bf16[4,1,1600]{2,1,0:T(2,128)(2,1)S(1)}, bf16[4,1,1600]{2,1,0:T(2,128)(2,1)S(1)}, u32[]{:S(2)}, u32[]{:S(2)}) %collective-permute-start.3) | collective-permute-done | bytes 12832 | tf_op jit(solution)/shard_map/ppermute | solution.py:143
  21.4 0.6 shard_map.37
  22.0 30.8 %all_to_all.14 = bf16[16,8,1600]{2,1,0:T(8,128)(2,1)S(1)} all-to-all(bf16[16,8,1600]{2,1,0:T(8,128)(2,1)S(1)} %broadcast_in_dim.10), channel_id=1, replica_groups={{0,2,4,6,16,18,20,22,32,34,36,38,48,50,52,54},{1,3,5,7,17,19,21,23,33,3..., dimensions={0} | all-to-all | bytes 819200 | tf_op jit(solution)/shard_map/all_to_all | solution.py:110
  52.9 3.8 %collective-permute-start.4 = (bf16[128,1600]{1,0:T(8,128)(2,1)S(1)}, bf16[128,1600]{1,0:T(8,128)(2,1)S(1)}, u32[]{:S(2)}, u32[]{:S(2)}) collective-permute-start(bf16[128,1600]{1,0:T(8,128)(2,1)S(1)} %bitcast.15), channel_id=1, source_target_pairs={{1,0},{2,1},{3,2},{4,3},{5,4},{6,5},{7,6},{0,7},{9,8},{10,9},{11,1... | collective-permute-start | bytes 1228808 | tf_op jit(solution)/shard_map/ppermute | solution.py:121
  56.7 2.4 %collective-permute-start.6 = (bf16[128,1600]{1,0:T(8,128)(2,1)S(1)}, bf16[128,1600]{1,0:T(8,128)(2,1)S(1)}, u32[]{:S(2)}, u32[]{:S(2)}) collective-permute-start(bf16[128,1600]{1,0:T(8,128)(2,1)S(1)} %bitcast.16), channel_id=1, source_target_pairs={{8,0},{9,1},{10,2},{11,3},{12,4},{13,5},{14,6},{15,7},{16,8},{17,9... | collective-permute-start | bytes 1228808 | tf_op jit(solution)/shard_map/ppermute | solution.py:121
  59.0 2.2 %collective-permute-start.7 = (bf16[128,1600]{1,0:T(8,128)(2,1)S(1)}, bf16[128,1600]{1,0:T(8,128)(2,1)S(1)}, u32[]{:S(2)}, u32[]{:S(2)}) collective-permute-start(bf16[128,1600]{1,0:T(8,128)(2,1)S(1)} %bitcast.17), channel_id=1, source_target_pairs={{9,0},{10,1},{11,2},{12,3},{13,4},{14,5},{15,6},{8,7},{17,8},{18,9... | collective-permute-start | bytes 1228808 | tf_op jit(solution)/shard_map/ppermute | solution.py:121
  61.2 1.6 %collective-permute-done.4 = bf16[128,1600]{1,0:T(8,128)(2,1)S(1)} collective-permute-done((bf16[128,1600]{1,0:T(8,128)(2,1)S(1)}, bf16[128,1600]{1,0:T(8,128)(2,1)S(1)}, u32[]{:S(2)}, u32[]{:S(2)}) %collective-permute-start.4) | collective-permute-done | bytes 409632 | tf_op jit(solution)/shard_map/ppermute | solution.py:121
  62.9 3.7 %shard_map.38 = (bf16[1600,1408]{1,0:T(8,128)(2,1)S(1)}, bf16[1600,1408]{1,0:T(8,128)(2,1)S(1)}) custom-call(bf16[1600,1408]{1,0:T(8,128)(2,1)} %own_ref, bf16[1600,1408]{1,0:T(8,128)(2,1)} %collective-permute-done.5.partner_ref), custom_call_target="tpu_custom_call" | custom-call | bytes 18022400 | tf_op jit(solution)/shard_map/pallas_call | solution.py:73
  66.5 1.7 %convolution_reduce_fusion.2 = f32[256]{0:T(256)S(1)} fusion(bf16[1600,1408]{1,0:T(8,128)(2,1)S(1)} %get-tuple-element.21, bf16[128,1600]{1,0:T(8,128)(2,1)S(1)} %collective-permute-done.4, bf16[128,1600]{1,0:T(8,128)(2,1)S(1)} %bitcast.18), kind=kOutput, calls=%fused_computation.2 | convolution fusion | flops 1155432192 | bytes 5325824 | tf_op jit(solution)/shard_map/dot_general | solution.py:87
  68.2 1.7 %convolution_reduce_fusion.3 = f32[256]{0:T(256)S(1)} fusion(bf16[1600,1408]{1,0:T(8,128)(2,1)S(1)} %get-tuple-element.20, bf16[128,1600]{1,0:T(8,128)(2,1)S(1)} %collective-permute-done.4, bf16[128,1600]{1,0:T(8,128)(2,1)S(1)} %bitcast.19), kind=kOutput, calls=%fused_computation.3 | convolution fusion | flops 1155432192 | bytes 5325824 | tf_op jit(solution)/shard_map/dot_general | solution.py:87
  69.9 1.4 %collective-permute-done.6 = bf16[128,1600]{1,0:T(8,128)(2,1)S(1)} collective-permute-done((bf16[128,1600]{1,0:T(8,128)(2,1)S(1)}, bf16[128,1600]{1,0:T(8,128)(2,1)S(1)}, u32[]{:S(2)}, u32[]{:S(2)}) %collective-permute-start.6) | collective-permute-done | bytes 409632 | tf_op jit(solution)/shard_map/ppermute | solution.py:121
  71.3 1.7 %convolution_reduce_fusion = f32[256]{0:T(256)S(1)} fusion(bf16[256,1600]{1,0:T(8,128)(2,1)S(1)} %constant_dynamic-update-slice_fusion, bf16[1600,1408]{1,0:T(8,128)(2,1)S(1)} %get-tuple-element.21), kind=kOutput, calls=%fused_computation | convolution fusion | flops 1153793792 | bytes 5325824 | tf_op jit(solution)/shard_map/dot_general | solution.py:87
  73.0 1.7 %convolution_reduce_fusion.1 = f32[256]{0:T(256)S(1)} fusion(bf16[256,1600]{1,0:T(8,128)(2,1)S(1)} %constant_dynamic-update-slice_fusion, bf16[1600,1408]{1,0:T(8,128)(2,1)S(1)} %get-tuple-element.20), kind=kOutput, calls=%fused_computation.1 | convolution fusion | flops 1153793792 | bytes 5325824 | tf_op jit(solution)/shard_map/dot_general | solution.py:87
  74.8 0.1 all_to_all.10
  74.9 19.1 %all_to_all.15 = f32[64,1,8]{2,1,0:T(1,128)S(1)} all-to-all(f32[64,1,8]{2,1,0:T(1,128)S(1)} %bitcast.20), channel_id=1, replica_groups={{0,2,4,6,16,18,20,22,32,34,36,38,48,50,52,54,1,3,5,7,17,19,21,23,33,35,..., dimensions={0} | all-to-all | bytes 4096 | tf_op jit(solution)/shard_map/all_to_all | solution.py:129
  94.0 0.1 reduce_max.49
  94.0 0.6 reshape.103
  (20 shorter events, 0.3 us)
Async XLA Ops:
  0.0 62.9 %collective-permute-start.5 = (bf16[1600,1408]{1,0:T(8,128)(2,1)}, bf16[1600,1408]{1,0:T(8,128)(2,1)}, u32[]{:S(2)}, u32[]{:S(2)}) collective-permute-start(bf16[1600,1408]{1,0:T(8,128)(2,1)} %own_ref), channel_id=1, source_target_pairs={{0,64},{64,0},{1,65},{65,1},{2,66},{66,2},{3,67},{67,3},{4,68},{68... | collective-permute-start | bytes 13516808 | tf_op jit(solution)/shard_map/ppermute | solution.py:163
  1.9 10.5 %collective-permute-start = (bf16[2,4,1600]{2,1,0:T(4,128)(2,1)}, bf16[2,4,1600]{2,1,0:T(4,128)(2,1)S(1)}, u32[]{:S(2)}, u32[]{:S(2)}) collective-permute-start(bf16[2,4,1600]{2,1,0:T(4,128)(2,1)} %param.3), channel_id=1, source_target_pairs={{0,128},{128,256},{256,384},{1,129},{129,257},{257,385},{2,130},{1... | collective-permute-start | bytes 76808 | tf_op jit(solution)/shard_map/ppermute | solution.py:138
  5.3 7.4 %collective-permute-start.1 = (bf16[2,4,1600]{2,1,0:T(4,128)(2,1)}, bf16[2,4,1600]{2,1,0:T(4,128)(2,1)S(1)}, u32[]{:S(2)}, u32[]{:S(2)}) collective-permute-start(bf16[2,4,1600]{2,1,0:T(4,128)(2,1)} %param.3), channel_id=1, source_target_pairs={{128,0},{256,128},{384,256},{129,1},{257,129},{385,257},{130,2},{2... | collective-permute-start | bytes 76808 | tf_op jit(solution)/shard_map/ppermute | solution.py:137
  13.6 3.5 %collective-permute-start.2 = (bf16[4,1,1600]{2,1,0:T(2,128)(2,1)S(1)}, bf16[4,1,1600]{2,1,0:T(2,128)(2,1)S(1)}, u32[]{:S(2)}, u32[]{:S(2)}) collective-permute-start(bf16[4,1,1600]{2,1,0:T(2,128)(2,1)S(1)} %get-tuple-element.28), channel_id=1, source_target_pairs={{0,1},{1,2},{2,3},{3,4},{4,5},{5,6},{6,7},{7,8},{8,9},{9,10},{10,1... | collective-permute-start | bytes 38408 | tf_op jit(solution)/shard_map/ppermute | solution.py:142
  15.6 5.7 %collective-permute-start.3 = (bf16[4,1,1600]{2,1,0:T(2,128)(2,1)S(1)}, bf16[4,1,1600]{2,1,0:T(2,128)(2,1)S(1)}, u32[]{:S(2)}, u32[]{:S(2)}) collective-permute-start(bf16[4,1,1600]{2,1,0:T(2,128)(2,1)S(1)} %get-tuple-element.27), channel_id=1, source_target_pairs={{1,0},{2,1},{3,2},{4,3},{5,4},{6,5},{7,6},{8,7},{9,8},{10,9},{11,1... | collective-permute-start | bytes 38408 | tf_op jit(solution)/shard_map/ppermute | solution.py:143
  52.9 10.0 %collective-permute-start.4 = (bf16[128,1600]{1,0:T(8,128)(2,1)S(1)}, bf16[128,1600]{1,0:T(8,128)(2,1)S(1)}, u32[]{:S(2)}, u32[]{:S(2)}) collective-permute-start(bf16[128,1600]{1,0:T(8,128)(2,1)S(1)} %bitcast.15), channel_id=1, source_target_pairs={{1,0},{2,1},{3,2},{4,3},{5,4},{6,5},{7,6},{0,7},{9,8},{10,9},{11,1... | collective-permute-start | bytes 1228808 | tf_op jit(solution)/shard_map/ppermute | solution.py:121
  56.7 14.6 %collective-permute-start.6 = (bf16[128,1600]{1,0:T(8,128)(2,1)S(1)}, bf16[128,1600]{1,0:T(8,128)(2,1)S(1)}, u32[]{:S(2)}, u32[]{:S(2)}) collective-permute-start(bf16[128,1600]{1,0:T(8,128)(2,1)S(1)} %bitcast.16), channel_id=1, source_target_pairs={{8,0},{9,1},{10,2},{11,3},{12,4},{13,5},{14,6},{15,7},{16,8},{17,9... | collective-permute-start | bytes 1228808 | tf_op jit(solution)/shard_map/ppermute | solution.py:121
  59.0 12.2 %collective-permute-start.7 = (bf16[128,1600]{1,0:T(8,128)(2,1)S(1)}, bf16[128,1600]{1,0:T(8,128)(2,1)S(1)}, u32[]{:S(2)}, u32[]{:S(2)}) collective-permute-start(bf16[128,1600]{1,0:T(8,128)(2,1)S(1)} %bitcast.17), channel_id=1, source_target_pairs={{9,0},{10,1},{11,2},{12,3},{13,4},{14,5},{15,6},{8,7},{17,8},{18,9... | collective-permute-start | bytes 1228808 | tf_op jit(solution)/shard_map/ppermute | solution.py:121

commit v3 on v2

--- a/solution.py
+++ b/solution.py
@@ -13,12 +13,14 @@
 COLS = ("sy", "z", "y")
 
 
-def average_kernel(block_ref, low_ref, high_ref, weight_ref, out_ref):
+def average_kernel(block_ref, far_ref, near_ref, weight_ref, out_ref):
     f32 = jnp.float32
-    lines = [
-        jnp.concatenate([low_ref[row], block_ref[row], high_ref[row]], axis=0).astype(f32)
-        for row in range(4)
-    ]
+    even = weight_ref[0, 0:1, 10:11] > 0.0
+    lines = []
+    for row in range(4):
+        far, near = far_ref[row].astype(f32), near_ref[row].astype(f32)
+        sides = jnp.where(even, far, near), jnp.where(even, near, far)
+        lines.append(jnp.concatenate([sides[0], block_ref[row].astype(f32), sides[1]], axis=0))
     averaged = []
     for row in range(2):
         weight = weight_ref[row]
@@ -47,7 +49,7 @@
     out_ref[...] = (centered / scale)[:, :PIX].astype(jnp.bfloat16)
 
 
-def average(block, low, high, weights):
+def average(block, far, near, weights):
     return pl.pallas_call(
         average_kernel,
         out_shape=jax.ShapeDtypeStruct((8, PIX), jnp.bfloat16),
@@ -55,7 +57,7 @@
         out_specs=pl.BlockSpec(memory_space=pltpu.VMEM),
         compiler_params=pltpu.CompilerParams(vmem_limit_bytes=16 * 1024 * 1024),
         cost_estimate=pl.CostEstimate(flops=1000000, bytes_accessed=200000, transcendentals=0),
-    )(block, low, high, weights)
+    )(block, far, near, weights)
 
 
 def hold_kernel(own_ref, partner_ref, own_held, partner_held, sems):
@@ -130,18 +132,22 @@
     return jnp.max(shares, axis=0)
 
 
+def swap_pairs(starts):
+    return [pair for i in starts for pair in ((i, i + 1), (i + 1, i))]
+
+
 def rim(patterns):
-    count = lax.axis_size(COLS)
-    down = [(i, i + 1) for i in range(3)]
-    up = [(target, source) for source, target in down]
-    below = lax.ppermute(patterns, "sx", up)[:1]
-    above = lax.ppermute(patterns, "sx", down)[1:]
+    even = lax.axis_index("sx") % 2 == 0
+    near = lax.ppermute(patterns, "sx", swap_pairs((0, 2)))
+    far = lax.ppermute(patterns, "sx", swap_pairs((1,)))
+    above = jnp.where(even, far[1:], near[1:])
+    below = jnp.where(even, near[:1], far[:1])
     block = jnp.concatenate([above, patterns, below], axis=0)
-    ahead = [(i, i + 1) for i in range(count - 1)]
-    behind = [(target, source) for source, target in ahead]
-    low = lax.ppermute(block[:, 3:4], COLS, ahead)
-    high = lax.ppermute(block[:, 0:1], COLS, behind)
-    return block, low, high
+    even = lax.axis_index(COLS) % 2 == 0
+    first, last = block[:, 0:1], block[:, 3:4]
+    far = lax.ppermute(jnp.where(even, first, last), COLS, swap_pairs(range(1, 127, 2)))
+    near = lax.ppermute(jnp.where(even, last, first), COLS, swap_pairs(range(0, 128, 2)))
+    return block, far, near
 
 
 def valid_weights(weights, rows, cols):
@@ -154,7 +160,9 @@
     col_valid = (col_near >= 0) & (col_near < cols * lax.axis_size(COLS))
     valid = row_valid[:, None, :, None] & col_valid[None, :, None, :]
     kept = jnp.where(valid.reshape(rows, cols, 9), jnp.transpose(weights, (1, 2, 0)), 0.0)
-    return jnp.concatenate([kept, jnp.sum(kept, axis=2, keepdims=True)], axis=2)
+    total = jnp.sum(kept, axis=2, keepdims=True)
+    even = (lax.axis_index(COLS) % 2 == 0).astype(jnp.float32)
+    return jnp.concatenate([kept, total, jnp.full_like(total, even)], axis=2)
 
 
 def on_device(patterns, nlpar_weights, dictionary):

time: 95.1 us -> 94.2 us (level)
  waiting for transfers between devices: 7.76 us -> 4.52 us
  starting transfers between devices: 22.6 us -> 25.1 us
    ppermute x4, waiting for transfers between devices: 4.74 us -> 2.44 us  [the longest x1 1.73 us: rim(): lax.ppermute(jnp.where(even, last, first), COLS, swap_pairs(range(0, 128,...]
    ppermute x4, starting transfers between devices: 12.4 us -> 14.2 us  [the longest x1 5.08 us: rim(): near = lax.ppermute(patterns, 'sx', swap_pairs((0, 2)))]
  transfers between devices with their start and end apart: 8 -> 8, of which waited for: 5 -> 4; matrix products, arithmetic and copies ran while one was open for 6% -> 6% of each run, Pallas kernels for 5% -> 5%
where the time goes in v3:
time: 94.2 us; the launch traced here: 93.8 us
  blocking collectives  49.6 us (53%)
  starting transfers between devices  25.1 us (27%)
  matrix products  6.71 us (7%)
  waiting for transfers between devices  4.52 us (5%)
  Pallas kernels  4.29 us (5%)
  other arithmetic  2.02 us (2%)
  local copies, waits for them, and re-layouts  1.3 us (1%)
    all_to_all x1, blocking collectives, gather_class(): got = lax.all_to_all(copies, COLS, 0, 0, axis_index_groups=groups)  30.4 us
    all_to_all x1, blocking collectives, merge(): lax.all_to_all(table.reshape(64, -1), COLS, 0, 0, axis_index_groups=groups)  19.3 us
    ppermute x3, starting transfers between devices, from_neighbour(): return lax.ppermute(block, COLS, pairs)  9.02 us
    dot_general x4, matrix products, row_best(): scores = jnp.dot(points, half, preferred_element_type=jnp.float32)  6.71 us
    ppermute x1, starting transfers between devices, rim(): near = lax.ppermute(patterns, 'sx', swap_pairs((0, 2)))  5.08 us
    ppermute x1, starting transfers between devices, rim(): lax.ppermute(jnp.where(even, last, first), COLS, swap_pairs(range(0, 128,...  5.06 us
    pallas_call x1, Pallas kernels, hold(): pl.pallas_call(hold_kernel, out_shape=[pltpu.VMEM(half.shape, half.dtype)...  3.67 us
    ppermute x1, starting transfers between devices, rim(): far = lax.ppermute(patterns, 'sx', swap_pairs((1,)))  3.4 us
  transfers between devices with their start and end apart: 8, of which 4 were waited for; matrix products, arithmetic and copies ran while one was open for 6% of the time, Pallas kernels for 5%

profile of v3, /device:TPU:2, one launch (start us, length us, event | category | flops | bytes accessed | tf_op | source)
XLA Modules:
  0.0 93.8 jit_solution(16729205875673538701)
XLA Ops:
  0.0 1.9 %collective-permute-start.5 = (bf16[1600,1408]{1,0:T(8,128)(2,1)}, bf16[1600,1408]{1,0:T(8,128)(2,1)}, u32[]{:S(2)}, u32[]{:S(2)}) collective-permute-start(bf16[1600,1408]{1,0:T(8,128)(2,1)} %own_ref), channel_id=1, source_target_pairs={{0,64},{64,0},{1,65},{65,1},{2,66},{66,2},{3,67},{67,3},{4,68},{68... | collective-permute-start | bytes 13516808 | tf_op jit(solution)/shard_map/ppermute | solution.py:171
  1.9 3.4 %collective-permute-start = (bf16[2,4,1600]{2,1,0:T(4,128)(2,1)}, bf16[2,4,1600]{2,1,0:T(4,128)(2,1)S(1)}, u32[]{:S(2)}, u32[]{:S(2)}) collective-permute-start(bf16[2,4,1600]{2,1,0:T(4,128)(2,1)} %param.3), channel_id=1, source_target_pairs={{128,256},{256,128},{129,257},{257,129},{130,258},{258,130},{131,2... | collective-permute-start | bytes 76808 | tf_op jit(solution)/shard_map/ppermute | solution.py:142
  5.3 5.1 %collective-permute-start.1 = (bf16[2,4,1600]{2,1,0:T(4,128)(2,1)}, bf16[2,4,1600]{2,1,0:T(4,128)(2,1)S(1)}, u32[]{:S(2)}, u32[]{:S(2)}) collective-permute-start(bf16[2,4,1600]{2,1,0:T(4,128)(2,1)} %param.3), channel_id=1, source_target_pairs={{0,128},{128,0},{256,384},{384,256},{1,129},{129,1},{257,385},{385... | collective-permute-start | bytes 76808 | tf_op jit(solution)/shard_map/ppermute | solution.py:141
  10.5 0.1 fusion
  10.5 0.1 and.68
  10.6 0.1 compare_and_fusion
  10.7 0.1 and.63
  10.8 0.1 and.64
  10.9 0.8 fusion.3
  11.7 0.1 copy.6
  11.8 0.7 collective-permute-done.1
  12.6 0.8 pad_maximum_fusion.3.block_ref
  13.4 0.7 collective-permute-start.2
  14.1 5.1 %collective-permute-start.3 = (bf16[4,1,1600]{2,1,0:T(2,128)(2,1)S(1)}, bf16[4,1,1600]{2,1,0:T(2,128)(2,1)S(1)}, u32[]{:S(2)}, u32[]{:S(2)}) collective-permute-start(bf16[4,1,1600]{2,1,0:T(2,128)(2,1)S(1)} %get-tuple-element.27), channel_id=1, source_target_pairs={{0,1},{1,0},{2,3},{3,2},{4,5},{5,4},{6,7},{7,6},{8,9},{9,8},{10,11... | collective-permute-start | bytes 38408 | tf_op jit(solution)/shard_map/ppermute | solution.py:149
  19.2 0.1 maximum_maximum_fusion.weight_ref
  19.2 1.7 %collective-permute-done.3.near_ref = bf16[4,1,1600]{2,1,0:T(2,128)(2,1)S(1)} collective-permute-done((bf16[4,1,1600]{2,1,0:T(2,128)(2,1)S(1)}, bf16[4,1,1600]{2,1,0:T(2,128)(2,1)S(1)}, u32[]{:S(2)}, u32[]{:S(2)}) %collective-permute-start.3) | collective-permute-done | bytes 12832 | tf_op jit(solution)/shard_map/ppermute | solution.py:149
  21.0 0.6 shard_map.37
  21.6 30.4 %all_to_all.14 = bf16[16,8,1600]{2,1,0:T(8,128)(2,1)S(1)} all-to-all(bf16[16,8,1600]{2,1,0:T(8,128)(2,1)S(1)} %broadcast_in_dim.13), channel_id=1, replica_groups={{0,2,4,6,16,18,20,22,32,34,36,38,48,50,52,54},{1,3,5,7,17,19,21,23,33,3..., dimensions={0} | all-to-all | bytes 819200 | tf_op jit(solution)/shard_map/all_to_all | solution.py:112
  52.0 3.6 %collective-permute-start.4 = (bf16[128,1600]{1,0:T(8,128)(2,1)S(1)}, bf16[128,1600]{1,0:T(8,128)(2,1)S(1)}, u32[]{:S(2)}, u32[]{:S(2)}) collective-permute-start(bf16[128,1600]{1,0:T(8,128)(2,1)S(1)} %bitcast.16), channel_id=1, source_target_pairs={{1,0},{2,1},{3,2},{4,3},{5,4},{6,5},{7,6},{0,7},{9,8},{10,9},{11,1... | collective-permute-start | bytes 1228808 | tf_op jit(solution)/shard_map/ppermute | solution.py:123
  55.6 2.6 %collective-permute-start.6 = (bf16[128,1600]{1,0:T(8,128)(2,1)S(1)}, bf16[128,1600]{1,0:T(8,128)(2,1)S(1)}, u32[]{:S(2)}, u32[]{:S(2)}) collective-permute-start(bf16[128,1600]{1,0:T(8,128)(2,1)S(1)} %bitcast.17), channel_id=1, source_target_pairs={{8,0},{9,1},{10,2},{11,3},{12,4},{13,5},{14,6},{15,7},{16,8},{17,9... | collective-permute-start | bytes 1228808 | tf_op jit(solution)/shard_map/ppermute | solution.py:123
  58.2 2.9 %collective-permute-start.7 = (bf16[128,1600]{1,0:T(8,128)(2,1)S(1)}, bf16[128,1600]{1,0:T(8,128)(2,1)S(1)}, u32[]{:S(2)}, u32[]{:S(2)}) collective-permute-start(bf16[128,1600]{1,0:T(8,128)(2,1)S(1)} %bitcast.18), channel_id=1, source_target_pairs={{9,0},{10,1},{11,2},{12,3},{13,4},{14,5},{15,6},{8,7},{17,8},{18,9... | collective-permute-start | bytes 1228808 | tf_op jit(solution)/shard_map/ppermute | solution.py:123
  61.1 0.9 %collective-permute-done.4 = bf16[128,1600]{1,0:T(8,128)(2,1)S(1)} collective-permute-done((bf16[128,1600]{1,0:T(8,128)(2,1)S(1)}, bf16[128,1600]{1,0:T(8,128)(2,1)S(1)}, u32[]{:S(2)}, u32[]{:S(2)}) %collective-permute-start.4) | collective-permute-done | bytes 409632 | tf_op jit(solution)/shard_map/ppermute | solution.py:123
  62.0 3.7 %shard_map.38 = (bf16[1600,1408]{1,0:T(8,128)(2,1)S(1)}, bf16[1600,1408]{1,0:T(8,128)(2,1)S(1)}) custom-call(bf16[1600,1408]{1,0:T(8,128)(2,1)} %own_ref, bf16[1600,1408]{1,0:T(8,128)(2,1)} %collective-permute-done.5.partner_ref), custom_call_target="tpu_custom_call" | custom-call | bytes 18022400 | tf_op jit(solution)/shard_map/pallas_call | solution.py:75
  65.7 1.7 %convolution_reduce_fusion.2 = f32[256]{0:T(256)S(1)} fusion(bf16[1600,1408]{1,0:T(8,128)(2,1)S(1)} %get-tuple-element.21, bf16[128,1600]{1,0:T(8,128)(2,1)S(1)} %collective-permute-done.4, bf16[128,1600]{1,0:T(8,128)(2,1)S(1)} %bitcast.19), kind=kOutput, calls=%fused_computation.2 | convolution fusion | flops 1155432192 | bytes 5325824 | tf_op jit(solution)/shard_map/dot_general | solution.py:89
  67.4 1.7 %convolution_reduce_fusion.3 = f32[256]{0:T(256)S(1)} fusion(bf16[1600,1408]{1,0:T(8,128)(2,1)S(1)} %get-tuple-element.20, bf16[128,1600]{1,0:T(8,128)(2,1)S(1)} %collective-permute-done.4, bf16[128,1600]{1,0:T(8,128)(2,1)S(1)} %bitcast.20), kind=kOutput, calls=%fused_computation.3 | convolution fusion | flops 1155432192 | bytes 5325824 | tf_op jit(solution)/shard_map/dot_general | solution.py:89
  69.0 1.1 %collective-permute-done.6 = bf16[128,1600]{1,0:T(8,128)(2,1)S(1)} collective-permute-done((bf16[128,1600]{1,0:T(8,128)(2,1)S(1)}, bf16[128,1600]{1,0:T(8,128)(2,1)S(1)}, u32[]{:S(2)}, u32[]{:S(2)}) %collective-permute-start.6) | collective-permute-done | bytes 409632 | tf_op jit(solution)/shard_map/ppermute | solution.py:123
  70.3 1.7 %convolution_reduce_fusion = f32[256]{0:T(256)S(1)} fusion(bf16[256,1600]{1,0:T(8,128)(2,1)S(1)} %constant_dynamic-update-slice_fusion, bf16[1600,1408]{1,0:T(8,128)(2,1)S(1)} %get-tuple-element.21), kind=kOutput, calls=%fused_computation | convolution fusion | flops 1153793792 | bytes 5325824 | tf_op jit(solution)/shard_map/dot_general | solution.py:89
  71.9 1.7 %convolution_reduce_fusion.1 = f32[256]{0:T(256)S(1)} fusion(bf16[256,1600]{1,0:T(8,128)(2,1)S(1)} %constant_dynamic-update-slice_fusion, bf16[1600,1408]{1,0:T(8,128)(2,1)S(1)} %get-tuple-element.20), kind=kOutput, calls=%fused_computation.1 | convolution fusion | flops 1153793792 | bytes 5325824 | tf_op jit(solution)/shard_map/dot_general | solution.py:89
  73.7 0.1 all_to_all.10
  73.8 19.3 %all_to_all.15 = f32[64,1,8]{2,1,0:T(1,128)S(1)} all-to-all(f32[64,1,8]{2,1,0:T(1,128)S(1)} %bitcast.21), channel_id=1, replica_groups={{0,2,4,6,16,18,20,22,32,34,36,38,48,50,52,54,1,3,5,7,17,19,21,23,33,35,..., dimensions={0} | all-to-all | bytes 4096 | tf_op jit(solution)/shard_map/all_to_all | solution.py:131
  93.1 0.1 reduce_max.49
  93.1 0.6 reshape.103
  (20 shorter events, 0.4 us)
Async XLA Ops:
  0.0 62.0 %collective-permute-start.5 = (bf16[1600,1408]{1,0:T(8,128)(2,1)}, bf16[1600,1408]{1,0:T(8,128)(2,1)}, u32[]{:S(2)}, u32[]{:S(2)}) collective-permute-start(bf16[1600,1408]{1,0:T(8,128)(2,1)} %own_ref), channel_id=1, source_target_pairs={{0,64},{64,0},{1,65},{65,1},{2,66},{66,2},{3,67},{67,3},{4,68},{68... | collective-permute-start | bytes 13516808 | tf_op jit(solution)/shard_map/ppermute | solution.py:171
  1.9 9.9 %collective-permute-start = (bf16[2,4,1600]{2,1,0:T(4,128)(2,1)}, bf16[2,4,1600]{2,1,0:T(4,128)(2,1)S(1)}, u32[]{:S(2)}, u32[]{:S(2)}) collective-permute-start(bf16[2,4,1600]{2,1,0:T(4,128)(2,1)} %param.3), channel_id=1, source_target_pairs={{128,256},{256,128},{129,257},{257,129},{130,258},{258,130},{131,2... | collective-permute-start | bytes 76808 | tf_op jit(solution)/shard_map/ppermute | solution.py:142
  5.3 7.2 %collective-permute-start.1 = (bf16[2,4,1600]{2,1,0:T(4,128)(2,1)}, bf16[2,4,1600]{2,1,0:T(4,128)(2,1)S(1)}, u32[]{:S(2)}, u32[]{:S(2)}) collective-permute-start(bf16[2,4,1600]{2,1,0:T(4,128)(2,1)} %param.3), channel_id=1, source_target_pairs={{0,128},{128,0},{256,384},{384,256},{1,129},{129,1},{257,385},{385... | collective-permute-start | bytes 76808 | tf_op jit(solution)/shard_map/ppermute | solution.py:141
  13.4 5.8 %collective-permute-start.2 = (bf16[4,1,1600]{2,1,0:T(2,128)(2,1)S(1)}, bf16[4,1,1600]{2,1,0:T(2,128)(2,1)S(1)}, u32[]{:S(2)}, u32[]{:S(2)}) collective-permute-start(bf16[4,1,1600]{2,1,0:T(2,128)(2,1)S(1)} %get-tuple-element.28), channel_id=1, source_target_pairs={{1,2},{2,1},{3,4},{4,3},{5,6},{6,5},{7,8},{8,7},{9,10},{10,9},{11,... | collective-permute-start | bytes 38408 | tf_op jit(solution)/shard_map/ppermute | solution.py:148
  14.1 6.9 %collective-permute-start.3 = (bf16[4,1,1600]{2,1,0:T(2,128)(2,1)S(1)}, bf16[4,1,1600]{2,1,0:T(2,128)(2,1)S(1)}, u32[]{:S(2)}, u32[]{:S(2)}) collective-permute-start(bf16[4,1,1600]{2,1,0:T(2,128)(2,1)S(1)} %get-tuple-element.27), channel_id=1, source_target_pairs={{0,1},{1,0},{2,3},{3,2},{4,5},{5,4},{6,7},{7,6},{8,9},{9,8},{10,11... | collective-permute-start | bytes 38408 | tf_op jit(solution)/shard_map/ppermute | solution.py:149
  52.0 10.0 %collective-permute-start.4 = (bf16[128,1600]{1,0:T(8,128)(2,1)S(1)}, bf16[128,1600]{1,0:T(8,128)(2,1)S(1)}, u32[]{:S(2)}, u32[]{:S(2)}) collective-permute-start(bf16[128,1600]{1,0:T(8,128)(2,1)S(1)} %bitcast.16), channel_id=1, source_target_pairs={{1,0},{2,1},{3,2},{4,3},{5,4},{6,5},{7,6},{0,7},{9,8},{10,9},{11,1... | collective-permute-start | bytes 1228808 | tf_op jit(solution)/shard_map/ppermute | solution.py:123
  55.6 14.6 %collective-permute-start.6 = (bf16[128,1600]{1,0:T(8,128)(2,1)S(1)}, bf16[128,1600]{1,0:T(8,128)(2,1)S(1)}, u32[]{:S(2)}, u32[]{:S(2)}) collective-permute-start(bf16[128,1600]{1,0:T(8,128)(2,1)S(1)} %bitcast.17), channel_id=1, source_target_pairs={{8,0},{9,1},{10,2},{11,3},{12,4},{13,5},{14,6},{15,7},{16,8},{17,9... | collective-permute-start | bytes 1228808 | tf_op jit(solution)/shard_map/ppermute | solution.py:123
  58.2 12.0 %collective-permute-start.7 = (bf16[128,1600]{1,0:T(8,128)(2,1)S(1)}, bf16[128,1600]{1,0:T(8,128)(2,1)S(1)}, u32[]{:S(2)}, u32[]{:S(2)}) collective-permute-start(bf16[128,1600]{1,0:T(8,128)(2,1)S(1)} %bitcast.18), channel_id=1, source_target_pairs={{9,0},{10,1},{11,2},{12,3},{13,4},{14,5},{15,6},{8,7},{17,8},{18,9... | collective-permute-start | bytes 1228808 | tf_op jit(solution)/shard_map/ppermute | solution.py:123

commit v4 on v3

--- a/solution.py
+++ b/solution.py
@@ -95,6 +95,21 @@
     return jnp.maximum(*[row_best(points, half) for half in halves])
 
 
+def largest_kernel(shares_ref, out_ref):
+    best = jnp.max(shares_ref[...], axis=0, keepdims=True)
+    out_ref[...] = jnp.concatenate([best[:, 0:4], best[:, 4:8]], axis=0)
+
+
+def largest(shares):
+    return pl.pallas_call(
+        largest_kernel,
+        out_shape=jax.ShapeDtypeStruct((2, 4), jnp.float32),
+        in_specs=[pl.BlockSpec(memory_space=pltpu.VMEM)],
+        out_specs=pl.BlockSpec(memory_space=pltpu.VMEM),
+        cost_estimate=pl.CostEstimate(flops=512, bytes_accessed=4096, transcendentals=0),
+    )(shares)
+
+
 def place(core, z, y):
     return 64 * core + 8 * (z % 8) + y % 8
 
@@ -129,7 +144,7 @@
     table = jnp.where(lax.axis_index("y") % 2 == 1, table[:, ::-1], table)
     groups = [sum([parity_class(core, z, y) for z, y in PARITIES], []) for core in range(2)]
     shares = lax.all_to_all(table.reshape(64, -1), COLS, 0, 0, axis_index_groups=groups)
-    return jnp.max(shares, axis=0)
+    return largest(shares)
 
 
 def swap_pairs(starts):
@@ -137,11 +152,11 @@
 
 
 def rim(patterns):
-    even = lax.axis_index("sx") % 2 == 0
+    odd = lax.axis_index("sx") % 2 == 1
     near = lax.ppermute(patterns, "sx", swap_pairs((0, 2)))
     far = lax.ppermute(patterns, "sx", swap_pairs((1,)))
-    above = jnp.where(even, far[1:], near[1:])
-    below = jnp.where(even, near[:1], far[:1])
+    above = jnp.where(odd, near[1:], far[1:])
+    below = jnp.where(odd, far[:1], near[:1])
     block = jnp.concatenate([above, patterns, below], axis=0)
     even = lax.axis_index(COLS) % 2 == 0
     first, last = block[:, 0:1], block[:, 3:4]
@@ -175,12 +190,12 @@
     ahead = from_neighbour(own, 0, 1)
     across = from_neighbour(own, 1, 0)
     diagonal = from_neighbour(own, 1, 1)
-    ahead, *halves = lax.optimization_barrier((ahead, dictionary, partner))
+    own, *halves = lax.optimization_barrier((own, dictionary, partner))
     halves = hold(*halves)
     early = best_of(own, ahead, halves)
     early, across, diagonal = lax.optimization_barrier((early, across, diagonal))
     tables = [early, best_of(across, diagonal, halves)]
-    return merge(tables).reshape(rows, cols)
+    return merge(tables)
 
 
 def solution(mesh):

time: 94.2 us -> 94.7 us (level)
  the two profiles are of different devices: /device:TPU:2 before, /device:TPU:4 now
where the time goes in v4:
time: 94.7 us; the launch traced here: 94.2 us
  blocking collectives  48.8 us (52%)
  starting transfers between devices  24.9 us (26%)
  matrix products  6.74 us (7%)
  Pallas kernels  5.69 us (6%)
  waiting for transfers between devices  5.14 us (5%)
  other arithmetic  1.93 us (2%)
    all_to_all x1, blocking collectives, gather_class(): got = lax.all_to_all(copies, COLS, 0, 0, axis_index_groups=groups)  29.5 us
    all_to_all x1, blocking collectives, merge(): lax.all_to_all(table.reshape(64, -1), COLS, 0, 0, axis_index_groups=groups)  19.3 us
    ppermute x3, starting transfers between devices, from_neighbour(): return lax.ppermute(block, COLS, pairs)  9.02 us
    ppermute x1, starting transfers between devices, rim(): far = lax.ppermute(patterns, 'sx', swap_pairs((1,)))  7.16 us
    dot_general x4, matrix products, row_best(): scores = jnp.dot(points, half, preferred_element_type=jnp.float32)  6.74 us
    pallas_call x1, Pallas kernels, hold(): pl.pallas_call(hold_kernel, out_shape=[pltpu.VMEM(half.shape, half.dtype)...  3.67 us
    ppermute x1, starting transfers between devices, rim(): near = lax.ppermute(patterns, 'sx', swap_pairs((0, 2)))  3.11 us
    ppermute x1, starting transfers between devices, rim(): lax.ppermute(jnp.where(even, last, first), COLS, swap_pairs(range(0, 128,...  3.07 us
  transfers between devices with their start and end apart: 8, of which 3 were waited for; matrix products, arithmetic and copies ran while one was open for 6% of the time, Pallas kernels for 5%

profile of v4, /device:TPU:4, one launch (start us, length us, event | category | flops | bytes accessed | tf_op | source)
XLA Modules:
  0.0 94.2 jit_solution(7666131424078636017)
XLA Ops:
  0.0 1.9 %collective-permute-start.4 = (bf16[1600,1408]{1,0:T(8,128)(2,1)}, bf16[1600,1408]{1,0:T(8,128)(2,1)}, u32[]{:S(2)}, u32[]{:S(2)}) collective-permute-start(bf16[1600,1408]{1,0:T(8,128)(2,1)} %own_ref), channel_id=1, source_target_pairs={{0,64},{64,0},{1,65},{65,1},{2,66},{66,2},{3,67},{67,3},{4,68},{68... | collective-permute-start | bytes 13516808 | tf_op jit(solution)/shard_map/ppermute | solution.py:186
  1.9 3.1 %collective-permute-start = (bf16[2,4,1600]{2,1,0:T(4,128)(2,1)}, bf16[2,4,1600]{2,1,0:T(4,128)(2,1)S(1)}, u32[]{:S(2)}, u32[]{:S(2)}) collective-permute-start(bf16[2,4,1600]{2,1,0:T(4,128)(2,1)} %param.3), channel_id=1, source_target_pairs={{0,128},{128,0},{256,384},{384,256},{1,129},{129,1},{257,385},{385... | collective-permute-start | bytes 76808 | tf_op jit(solution)/shard_map/ppermute | solution.py:156
  5.0 7.2 %collective-permute-start.1 = (bf16[2,4,1600]{2,1,0:T(4,128)(2,1)}, bf16[2,4,1600]{2,1,0:T(4,128)(2,1)S(1)}, u32[]{:S(2)}, u32[]{:S(2)}) collective-permute-start(bf16[2,4,1600]{2,1,0:T(4,128)(2,1)} %param.3), channel_id=1, source_target_pairs={{128,256},{256,128},{129,257},{257,129},{130,258},{258,130},{131,2... | collective-permute-start | bytes 76808 | tf_op jit(solution)/shard_map/ppermute | solution.py:157
  12.2 0.1 fusion
  12.3 0.1 and.68
  12.4 0.1 compare_and_fusion
  12.5 0.1 and.63
  12.6 0.1 and.64
  12.7 0.8 fusion.1
  13.4 0.1 copy.6
  13.5 0.1 pad.4.clone
  13.6 0.6 collective-permute-done.1
  14.2 0.8 pad_maximum_fusion.block_ref
  15.0 0.1 broadcast_select_fusion
  15.1 0.7 collective-permute-start.2
  15.8 3.1 %collective-permute-start.3 = (bf16[4,1,1600]{2,1,0:T(2,128)(2,1)S(1)}, bf16[4,1,1600]{2,1,0:T(2,128)(2,1)S(1)}, u32[]{:S(2)}, u32[]{:S(2)}) collective-permute-start(bf16[4,1,1600]{2,1,0:T(2,128)(2,1)S(1)} %get-tuple-element.27), channel_id=1, source_target_pairs={{0,1},{1,0},{2,3},{3,2},{4,5},{5,4},{6,7},{7,6},{8,9},{9,8},{10,11... | collective-permute-start | bytes 38408 | tf_op jit(solution)/shard_map/ppermute | solution.py:164
  18.9 0.1 maximum_maximum_fusion.weight_ref
  18.9 2.6 %collective-permute-done.3.near_ref = bf16[4,1,1600]{2,1,0:T(2,128)(2,1)S(1)} collective-permute-done((bf16[4,1,1600]{2,1,0:T(2,128)(2,1)S(1)}, bf16[4,1,1600]{2,1,0:T(2,128)(2,1)S(1)}, u32[]{:S(2)}, u32[]{:S(2)}) %collective-permute-start.3) | collective-permute-done | bytes 12832 | tf_op jit(solution)/shard_map/ppermute | solution.py:164
  21.5 0.6 shard_map.37
  22.2 29.5 %all_to_all.16 = bf16[16,8,1600]{2,1,0:T(8,128)(2,1)S(1)} all-to-all(bf16[16,8,1600]{2,1,0:T(8,128)(2,1)S(1)} %broadcast_in_dim.13), channel_id=1, replica_groups={{0,2,4,6,16,18,20,22,32,34,36,38,48,50,52,54},{1,3,5,7,17,19,21,23,33,3..., dimensions={0} | all-to-all | bytes 819200 | tf_op jit(solution)/shard_map/all_to_all | solution.py:127
  51.7 3.6 %collective-permute-start.5 = (bf16[128,1600]{1,0:T(8,128)(2,1)S(1)}, bf16[128,1600]{1,0:T(8,128)(2,1)S(1)}, u32[]{:S(2)}, u32[]{:S(2)}) collective-permute-start(bf16[128,1600]{1,0:T(8,128)(2,1)S(1)} %bitcast.19), channel_id=1, source_target_pairs={{1,0},{2,1},{3,2},{4,3},{5,4},{6,5},{7,6},{0,7},{9,8},{10,9},{11,1... | collective-permute-start | bytes 1228808 | tf_op jit(solution)/shard_map/ppermute | solution.py:138
  55.3 2.6 %collective-permute-start.6 = (bf16[128,1600]{1,0:T(8,128)(2,1)S(1)}, bf16[128,1600]{1,0:T(8,128)(2,1)S(1)}, u32[]{:S(2)}, u32[]{:S(2)}) collective-permute-start(bf16[128,1600]{1,0:T(8,128)(2,1)S(1)} %bitcast.20), channel_id=1, source_target_pairs={{8,0},{9,1},{10,2},{11,3},{12,4},{13,5},{14,6},{15,7},{16,8},{17,9... | collective-permute-start | bytes 1228808 | tf_op jit(solution)/shard_map/ppermute | solution.py:138
  57.9 2.9 %collective-permute-start.7 = (bf16[128,1600]{1,0:T(8,128)(2,1)S(1)}, bf16[128,1600]{1,0:T(8,128)(2,1)S(1)}, u32[]{:S(2)}, u32[]{:S(2)}) collective-permute-start(bf16[128,1600]{1,0:T(8,128)(2,1)S(1)} %bitcast.21), channel_id=1, source_target_pairs={{9,0},{10,1},{11,2},{12,3},{13,4},{14,5},{15,6},{8,7},{17,8},{18,9... | collective-permute-start | bytes 1228808 | tf_op jit(solution)/shard_map/ppermute | solution.py:138
  60.8 3.7 %shard_map.38 = (bf16[1600,1408]{1,0:T(8,128)(2,1)S(1)}, bf16[1600,1408]{1,0:T(8,128)(2,1)S(1)}) custom-call(bf16[1600,1408]{1,0:T(8,128)(2,1)} %own_ref, bf16[1600,1408]{1,0:T(8,128)(2,1)} %collective-permute-done.4.partner_ref), custom_call_target="tpu_custom_call" | custom-call | bytes 18022400 | tf_op jit(solution)/shard_map/pallas_call | solution.py:75
  64.6 1.7 %convolution_reduce_fusion.2 = f32[256]{0:T(256)S(1)} fusion(bf16[256,1600]{1,0:T(8,128)(2,1)S(1)} %constant_dynamic-update-slice_fusion, bf16[1600,1408]{1,0:T(8,128)(2,1)S(1)} %get-tuple-element.21), kind=kOutput, calls=%fused_computation.2 | convolution fusion | flops 1153793792 | bytes 5325824 | tf_op jit(solution)/shard_map/dot_general | solution.py:89
  66.2 1.7 %convolution_reduce_fusion.3 = f32[256]{0:T(256)S(1)} fusion(bf16[256,1600]{1,0:T(8,128)(2,1)S(1)} %constant_dynamic-update-slice_fusion, bf16[1600,1408]{1,0:T(8,128)(2,1)S(1)} %get-tuple-element.20), kind=kOutput, calls=%fused_computation.3 | convolution fusion | flops 1153793792 | bytes 5325824 | tf_op jit(solution)/shard_map/dot_general | solution.py:89
  67.9 1.9 %collective-permute-done.6 = bf16[128,1600]{1,0:T(8,128)(2,1)S(1)} collective-permute-done((bf16[128,1600]{1,0:T(8,128)(2,1)S(1)}, bf16[128,1600]{1,0:T(8,128)(2,1)S(1)}, u32[]{:S(2)}, u32[]{:S(2)}) %collective-permute-start.6) | collective-permute-done | bytes 409632 | tf_op jit(solution)/shard_map/ppermute | solution.py:138
  70.0 1.7 %convolution_reduce_fusion = f32[256]{0:T(256)S(1)} fusion(bf16[256,1600]{1,0:T(8,128)(2,1)S(1)} %constant_dynamic-update-slice_fusion.2, bf16[1600,1408]{1,0:T(8,128)(2,1)S(1)} %get-tuple-element.21), kind=kOutput, calls=%fused_computation | convolution fusion | flops 1153793792 | bytes 5325824 | tf_op jit(solution)/shard_map/dot_general | solution.py:89
  71.7 1.7 %convolution_reduce_fusion.1 = f32[256]{0:T(256)S(1)} fusion(bf16[256,1600]{1,0:T(8,128)(2,1)S(1)} %constant_dynamic-update-slice_fusion.2, bf16[1600,1408]{1,0:T(8,128)(2,1)S(1)} %get-tuple-element.20), kind=kOutput, calls=%fused_computation.1 | convolution fusion | flops 1153793792 | bytes 5325824 | tf_op jit(solution)/shard_map/dot_general | solution.py:89
  73.4 0.1 all_to_all.11
  73.5 19.3 %all_to_all.17 = f32[64,1,8]{2,1,0:T(1,128)} all-to-all(f32[64,1,8]{2,1,0:T(1,128)S(1)} %bitcast.23), channel_id=1, replica_groups={{0,2,4,6,16,18,20,22,32,34,36,38,48,50,52,54,1,3,5,7,17,19,21,23,33,35,..., dimensions={0} | all-to-all | bytes 4096 | tf_op jit(solution)/shard_map/all_to_all | solution.py:146
  92.8 1.4 %shard_map.39 = f32[2,4]{1,0:T(2,128)} custom-call(f32[64,8]{1,0:T(8,128)} %bitcast.24), custom_call_target="tpu_custom_call" | custom-call | flops 512 | bytes 4096 | tf_op jit(solution)/shard_map/pallas_call | solution.py:104
  (21 shorter events, 0.3 us)
Async XLA Ops:
  0.0 60.8 %collective-permute-start.4 = (bf16[1600,1408]{1,0:T(8,128)(2,1)}, bf16[1600,1408]{1,0:T(8,128)(2,1)}, u32[]{:S(2)}, u32[]{:S(2)}) collective-permute-start(bf16[1600,1408]{1,0:T(8,128)(2,1)} %own_ref), channel_id=1, source_target_pairs={{0,64},{64,0},{1,65},{65,1},{2,66},{66,2},{3,67},{67,3},{4,68},{68... | collective-permute-start | bytes 13516808 | tf_op jit(solution)/shard_map/ppermute | solution.py:186
  1.9 11.7 %collective-permute-start = (bf16[2,4,1600]{2,1,0:T(4,128)(2,1)}, bf16[2,4,1600]{2,1,0:T(4,128)(2,1)S(1)}, u32[]{:S(2)}, u32[]{:S(2)}) collective-permute-start(bf16[2,4,1600]{2,1,0:T(4,128)(2,1)} %param.3), channel_id=1, source_target_pairs={{0,128},{128,0},{256,384},{384,256},{1,129},{129,1},{257,385},{385... | collective-permute-start | bytes 76808 | tf_op jit(solution)/shard_map/ppermute | solution.py:156
  5.0 9.2 %collective-permute-start.1 = (bf16[2,4,1600]{2,1,0:T(4,128)(2,1)}, bf16[2,4,1600]{2,1,0:T(4,128)(2,1)S(1)}, u32[]{:S(2)}, u32[]{:S(2)}) collective-permute-start(bf16[2,4,1600]{2,1,0:T(4,128)(2,1)} %param.3), channel_id=1, source_target_pairs={{128,256},{256,128},{129,257},{257,129},{130,258},{258,130},{131,2... | collective-permute-start | bytes 76808 | tf_op jit(solution)/shard_map/ppermute | solution.py:157
  15.1 3.8 %collective-permute-start.2 = (bf16[4,1,1600]{2,1,0:T(2,128)(2,1)S(1)}, bf16[4,1,1600]{2,1,0:T(2,128)(2,1)S(1)}, u32[]{:S(2)}, u32[]{:S(2)}) collective-permute-start(bf16[4,1,1600]{2,1,0:T(2,128)(2,1)S(1)} %get-tuple-element.28), channel_id=1, source_target_pairs={{1,2},{2,1},{3,4},{4,3},{5,6},{6,5},{7,8},{8,7},{9,10},{10,9},{11,... | collective-permute-start | bytes 38408 | tf_op jit(solution)/shard_map/ppermute | solution.py:163
  15.8 5.7 %collective-permute-start.3 = (bf16[4,1,1600]{2,1,0:T(2,128)(2,1)S(1)}, bf16[4,1,1600]{2,1,0:T(2,128)(2,1)S(1)}, u32[]{:S(2)}, u32[]{:S(2)}) collective-permute-start(bf16[4,1,1600]{2,1,0:T(2,128)(2,1)S(1)} %get-tuple-element.27), channel_id=1, source_target_pairs={{0,1},{1,0},{2,3},{3,2},{4,5},{5,4},{6,7},{7,6},{8,9},{9,8},{10,11... | collective-permute-start | bytes 38408 | tf_op jit(solution)/shard_map/ppermute | solution.py:164
  51.7 12.8 %collective-permute-start.5 = (bf16[128,1600]{1,0:T(8,128)(2,1)S(1)}, bf16[128,1600]{1,0:T(8,128)(2,1)S(1)}, u32[]{:S(2)}, u32[]{:S(2)}) collective-permute-start(bf16[128,1600]{1,0:T(8,128)(2,1)S(1)} %bitcast.19), channel_id=1, source_target_pairs={{1,0},{2,1},{3,2},{4,3},{5,4},{6,5},{7,6},{0,7},{9,8},{10,9},{11,1... | collective-permute-start | bytes 1228808 | tf_op jit(solution)/shard_map/ppermute | solution.py:138
  55.3 14.6 %collective-permute-start.6 = (bf16[128,1600]{1,0:T(8,128)(2,1)S(1)}, bf16[128,1600]{1,0:T(8,128)(2,1)S(1)}, u32[]{:S(2)}, u32[]{:S(2)}) collective-permute-start(bf16[128,1600]{1,0:T(8,128)(2,1)S(1)} %bitcast.20), channel_id=1, source_target_pairs={{8,0},{9,1},{10,2},{11,3},{12,4},{13,5},{14,6},{15,7},{16,8},{17,9... | collective-permute-start | bytes 1228808 | tf_op jit(solution)/shard_map/ppermute | solution.py:138
  57.9 12.0 %collective-permute-start.7 = (bf16[128,1600]{1,0:T(8,128)(2,1)S(1)}, bf16[128,1600]{1,0:T(8,128)(2,1)S(1)}, u32[]{:S(2)}, u32[]{:S(2)}) collective-permute-start(bf16[128,1600]{1,0:T(8,128)(2,1)S(1)} %bitcast.21), channel_id=1, source_target_pairs={{9,0},{10,1},{11,2},{12,3},{13,4},{14,5},{15,6},{8,7},{17,8},{18,9... | collective-permute-start | bytes 1228808 | tf_op jit(solution)/shard_map/ppermute | solution.py:138

commit v5 on v3

--- a/solution.py
+++ b/solution.py
@@ -127,8 +127,9 @@
     table = jnp.stack([pair.reshape(2, 128) for pair in tables])
     table = jnp.where(lax.axis_index("z") % 2 == 1, table[::-1], table)
     table = jnp.where(lax.axis_index("y") % 2 == 1, table[:, ::-1], table)
-    groups = [sum([parity_class(core, z, y) for z, y in PARITIES], []) for core in range(2)]
-    shares = lax.all_to_all(table.reshape(64, -1), COLS, 0, 0, axis_index_groups=groups)
+    table = jnp.transpose(table.reshape(2, 2, 4, 4, 8), (2, 0, 3, 1, 4)).reshape(64, 8)
+    groups = [[place(core, z, y) for z in range(8) for y in range(8)] for core in range(2)]
+    shares = lax.all_to_all(table, COLS, 0, 0, axis_index_groups=groups)
     return jnp.max(shares, axis=0)
 
 
@@ -137,11 +138,11 @@
 
 
 def rim(patterns):
-    even = lax.axis_index("sx") % 2 == 0
+    odd = lax.axis_index("sx") % 2 == 1
     near = lax.ppermute(patterns, "sx", swap_pairs((0, 2)))
     far = lax.ppermute(patterns, "sx", swap_pairs((1,)))
-    above = jnp.where(even, far[1:], near[1:])
-    below = jnp.where(even, near[:1], far[:1])
+    above = jnp.where(odd, near[1:], far[1:])
+    below = jnp.where(odd, far[:1], near[:1])
     block = jnp.concatenate([above, patterns, below], axis=0)
     even = lax.axis_index(COLS) % 2 == 0
     first, last = block[:, 0:1], block[:, 3:4]
@@ -175,7 +176,7 @@
     ahead = from_neighbour(own, 0, 1)
     across = from_neighbour(own, 1, 0)
     diagonal = from_neighbour(own, 1, 1)
-    ahead, *halves = lax.optimization_barrier((ahead, dictionary, partner))
+    own, *halves = lax.optimization_barrier((own, dictionary, partner))
     halves = hold(*halves)
     early = best_of(own, ahead, halves)
     early, across, diagonal = lax.optimization_barrier((early, across, diagonal))

time: 94.2 us -> 94.1 us (level)
  the two profiles are of different devices: /device:TPU:2 before, /device:TPU:4 now
where the time goes in v5:
time: 94.1 us; the launch traced here: 93.6 us
  blocking collectives  48.9 us (52%)
  starting transfers between devices  24.9 us (26%)
  matrix products  6.74 us (7%)
  waiting for transfers between devices  5.14 us (5%)
  Pallas kernels  4.29 us (5%)
  other arithmetic  2.02 us (2%)
  local copies, waits for them, and re-layouts  1.41 us (1%)
    all_to_all x1, blocking collectives, gather_class(): got = lax.all_to_all(copies, COLS, 0, 0, axis_index_groups=groups)  29.5 us
    all_to_all x1, blocking collectives, merge(): shares = lax.all_to_all(table, COLS, 0, 0, axis_index_groups=groups)  19.3 us
    ppermute x3, starting transfers between devices, from_neighbour(): return lax.ppermute(block, COLS, pairs)  9.02 us
    ppermute x1, starting transfers between devices, rim(): far = lax.ppermute(patterns, 'sx', swap_pairs((1,)))  7.16 us
    dot_general x4, matrix products, row_best(): scores = jnp.dot(points, half, preferred_element_type=jnp.float32)  6.74 us
    pallas_call x1, Pallas kernels, hold(): pl.pallas_call(hold_kernel, out_shape=[pltpu.VMEM(half.shape, half.dtype)...  3.67 us
    ppermute x1, starting transfers between devices, rim(): near = lax.ppermute(patterns, 'sx', swap_pairs((0, 2)))  3.11 us
    ppermute x1, starting transfers between devices, rim(): lax.ppermute(jnp.where(even, last, first), COLS, swap_pairs(range(0, 128,...  3.07 us
  transfers between devices with their start and end apart: 8, of which 3 were waited for; matrix products, arithmetic and copies ran while one was open for 6% of the time, Pallas kernels for 5%

profile of v5, /device:TPU:4, one launch (start us, length us, event | category | flops | bytes accessed | tf_op | source)
XLA Modules:
  0.0 93.6 jit_solution(657943848495496203)
XLA Ops:
  0.0 1.9 %collective-permute-start.4 = (bf16[1600,1408]{1,0:T(8,128)(2,1)}, bf16[1600,1408]{1,0:T(8,128)(2,1)}, u32[]{:S(2)}, u32[]{:S(2)}) collective-permute-start(bf16[1600,1408]{1,0:T(8,128)(2,1)} %own_ref), channel_id=1, source_target_pairs={{0,64},{64,0},{1,65},{65,1},{2,66},{66,2},{3,67},{67,3},{4,68},{68... | collective-permute-start | bytes 13516808 | tf_op jit(solution)/shard_map/ppermute | solution.py:172
  1.9 3.1 %collective-permute-start = (bf16[2,4,1600]{2,1,0:T(4,128)(2,1)}, bf16[2,4,1600]{2,1,0:T(4,128)(2,1)S(1)}, u32[]{:S(2)}, u32[]{:S(2)}) collective-permute-start(bf16[2,4,1600]{2,1,0:T(4,128)(2,1)} %param.3), channel_id=1, source_target_pairs={{0,128},{128,0},{256,384},{384,256},{1,129},{129,1},{257,385},{385... | collective-permute-start | bytes 76808 | tf_op jit(solution)/shard_map/ppermute | solution.py:142
  5.0 7.2 %collective-permute-start.1 = (bf16[2,4,1600]{2,1,0:T(4,128)(2,1)}, bf16[2,4,1600]{2,1,0:T(4,128)(2,1)S(1)}, u32[]{:S(2)}, u32[]{:S(2)}) collective-permute-start(bf16[2,4,1600]{2,1,0:T(4,128)(2,1)} %param.3), channel_id=1, source_target_pairs={{128,256},{256,128},{129,257},{257,129},{130,258},{258,130},{131,2... | collective-permute-start | bytes 76808 | tf_op jit(solution)/shard_map/ppermute | solution.py:143
  12.2 0.1 fusion
  12.3 0.1 and.68
  12.4 0.1 compare_and_fusion
  12.5 0.1 and.63
  12.6 0.1 and.64
  12.7 0.8 fusion.1
  13.4 0.1 copy.8
  13.5 0.1 pad.4.clone
  13.6 0.6 collective-permute-done.1
  14.2 0.8 pad_maximum_fusion.block_ref
  15.1 0.7 collective-permute-start.2
  15.8 3.1 %collective-permute-start.3 = (bf16[4,1,1600]{2,1,0:T(2,128)(2,1)S(1)}, bf16[4,1,1600]{2,1,0:T(2,128)(2,1)S(1)}, u32[]{:S(2)}, u32[]{:S(2)}) collective-permute-start(bf16[4,1,1600]{2,1,0:T(2,128)(2,1)S(1)} %get-tuple-element.27), channel_id=1, source_target_pairs={{0,1},{1,0},{2,3},{3,2},{4,5},{5,4},{6,7},{7,6},{8,9},{9,8},{10,11... | collective-permute-start | bytes 38408 | tf_op jit(solution)/shard_map/ppermute | solution.py:150
  18.9 0.1 maximum_maximum_fusion.weight_ref
  18.9 2.6 %collective-permute-done.3.near_ref = bf16[4,1,1600]{2,1,0:T(2,128)(2,1)S(1)} collective-permute-done((bf16[4,1,1600]{2,1,0:T(2,128)(2,1)S(1)}, bf16[4,1,1600]{2,1,0:T(2,128)(2,1)S(1)}, u32[]{:S(2)}, u32[]{:S(2)}) %collective-permute-start.3) | collective-permute-done | bytes 12832 | tf_op jit(solution)/shard_map/ppermute | solution.py:150
  21.5 0.6 shard_map.37
  22.2 29.5 %all_to_all.14 = bf16[16,8,1600]{2,1,0:T(8,128)(2,1)S(1)} all-to-all(bf16[16,8,1600]{2,1,0:T(8,128)(2,1)S(1)} %broadcast_in_dim.13), channel_id=1, replica_groups={{0,2,4,6,16,18,20,22,32,34,36,38,48,50,52,54},{1,3,5,7,17,19,21,23,33,3..., dimensions={0} | all-to-all | bytes 819200 | tf_op jit(solution)/shard_map/all_to_all | solution.py:112
  51.7 3.6 %collective-permute-start.5 = (bf16[128,1600]{1,0:T(8,128)(2,1)S(1)}, bf16[128,1600]{1,0:T(8,128)(2,1)S(1)}, u32[]{:S(2)}, u32[]{:S(2)}) collective-permute-start(bf16[128,1600]{1,0:T(8,128)(2,1)S(1)} %bitcast.21), channel_id=1, source_target_pairs={{1,0},{2,1},{3,2},{4,3},{5,4},{6,5},{7,6},{0,7},{9,8},{10,9},{11,1... | collective-permute-start | bytes 1228808 | tf_op jit(solution)/shard_map/ppermute | solution.py:123
  55.3 2.6 %collective-permute-start.6 = (bf16[128,1600]{1,0:T(8,128)(2,1)S(1)}, bf16[128,1600]{1,0:T(8,128)(2,1)S(1)}, u32[]{:S(2)}, u32[]{:S(2)}) collective-permute-start(bf16[128,1600]{1,0:T(8,128)(2,1)S(1)} %bitcast.22), channel_id=1, source_target_pairs={{8,0},{9,1},{10,2},{11,3},{12,4},{13,5},{14,6},{15,7},{16,8},{17,9... | collective-permute-start | bytes 1228808 | tf_op jit(solution)/shard_map/ppermute | solution.py:123
  57.9 2.9 %collective-permute-start.7 = (bf16[128,1600]{1,0:T(8,128)(2,1)S(1)}, bf16[128,1600]{1,0:T(8,128)(2,1)S(1)}, u32[]{:S(2)}, u32[]{:S(2)}) collective-permute-start(bf16[128,1600]{1,0:T(8,128)(2,1)S(1)} %bitcast.23), channel_id=1, source_target_pairs={{9,0},{10,1},{11,2},{12,3},{13,4},{14,5},{15,6},{8,7},{17,8},{18,9... | collective-permute-start | bytes 1228808 | tf_op jit(solution)/shard_map/ppermute | solution.py:123
  60.8 3.7 %shard_map.38 = (bf16[1600,1408]{1,0:T(8,128)(2,1)S(1)}, bf16[1600,1408]{1,0:T(8,128)(2,1)S(1)}) custom-call(bf16[1600,1408]{1,0:T(8,128)(2,1)} %own_ref, bf16[1600,1408]{1,0:T(8,128)(2,1)} %collective-permute-done.4.partner_ref), custom_call_target="tpu_custom_call" | custom-call | bytes 18022400 | tf_op jit(solution)/shard_map/pallas_call | solution.py:75
  64.6 1.7 %convolution_reduce_fusion.2 = f32[256]{0:T(256)S(1)} fusion(bf16[256,1600]{1,0:T(8,128)(2,1)S(1)} %constant_dynamic-update-slice_fusion, bf16[1600,1408]{1,0:T(8,128)(2,1)S(1)} %get-tuple-element.21), kind=kOutput, calls=%fused_computation.2 | convolution fusion | flops 1153793792 | bytes 5325824 | tf_op jit(solution)/shard_map/dot_general | solution.py:89
  66.2 1.7 %convolution_reduce_fusion.3 = f32[256]{0:T(256)S(1)} fusion(bf16[256,1600]{1,0:T(8,128)(2,1)S(1)} %constant_dynamic-update-slice_fusion, bf16[1600,1408]{1,0:T(8,128)(2,1)S(1)} %get-tuple-element.20), kind=kOutput, calls=%fused_computation.3 | convolution fusion | flops 1153793792 | bytes 5325824 | tf_op jit(solution)/shard_map/dot_general | solution.py:89
  67.9 1.9 %collective-permute-done.6 = bf16[128,1600]{1,0:T(8,128)(2,1)S(1)} collective-permute-done((bf16[128,1600]{1,0:T(8,128)(2,1)S(1)}, bf16[128,1600]{1,0:T(8,128)(2,1)S(1)}, u32[]{:S(2)}, u32[]{:S(2)}) %collective-permute-start.6) | collective-permute-done | bytes 409632 | tf_op jit(solution)/shard_map/ppermute | solution.py:123
  70.0 1.7 %convolution_reduce_fusion = f32[256]{0:T(256)S(1)} fusion(bf16[256,1600]{1,0:T(8,128)(2,1)S(1)} %constant_dynamic-update-slice_fusion.2, bf16[1600,1408]{1,0:T(8,128)(2,1)S(1)} %get-tuple-element.21), kind=kOutput, calls=%fused_computation | convolution fusion | flops 1153793792 | bytes 5325824 | tf_op jit(solution)/shard_map/dot_general | solution.py:89
  71.7 1.7 %convolution_reduce_fusion.1 = f32[256]{0:T(256)S(1)} fusion(bf16[256,1600]{1,0:T(8,128)(2,1)S(1)} %constant_dynamic-update-slice_fusion.2, bf16[1600,1408]{1,0:T(8,128)(2,1)S(1)} %get-tuple-element.20), kind=kOutput, calls=%fused_computation.1 | convolution fusion | flops 1153793792 | bytes 5325824 | tf_op jit(solution)/shard_map/dot_general | solution.py:89
  73.4 0.1 reshape.106
  73.5 19.3 %all_to_all.15 = f32[64,1,8]{2,1,0:T(1,128)S(1)} all-to-all(f32[64,1,8]{2,1,0:T(1,128)S(1)} %bitcast.26), channel_id=1, replica_groups={{0,1,2,3,4,5,6,7,8,9,10,11,12,13,14,15,16,17,18,19,20,21,22,23,24,25,26..., dimensions={0} | all-to-all | bytes 4096 | tf_op jit(solution)/shard_map/all_to_all | solution.py:132
  92.9 0.1 reduce_max.49
  93.0 0.6 reshape.107
  (23 shorter events, 0.4 us)
Async XLA Ops:
  0.0 60.8 %collective-permute-start.4 = (bf16[1600,1408]{1,0:T(8,128)(2,1)}, bf16[1600,1408]{1,0:T(8,128)(2,1)}, u32[]{:S(2)}, u32[]{:S(2)}) collective-permute-start(bf16[1600,1408]{1,0:T(8,128)(2,1)} %own_ref), channel_id=1, source_target_pairs={{0,64},{64,0},{1,65},{65,1},{2,66},{66,2},{3,67},{67,3},{4,68},{68... | collective-permute-start | bytes 13516808 | tf_op jit(solution)/shard_map/ppermute | solution.py:172
  1.9 11.7 %collective-permute-start = (bf16[2,4,1600]{2,1,0:T(4,128)(2,1)}, bf16[2,4,1600]{2,1,0:T(4,128)(2,1)S(1)}, u32[]{:S(2)}, u32[]{:S(2)}) collective-permute-start(bf16[2,4,1600]{2,1,0:T(4,128)(2,1)} %param.3), channel_id=1, source_target_pairs={{0,128},{128,0},{256,384},{384,256},{1,129},{129,1},{257,385},{385... | collective-permute-start | bytes 76808 | tf_op jit(solution)/shard_map/ppermute | solution.py:142
  5.0 9.2 %collective-permute-start.1 = (bf16[2,4,1600]{2,1,0:T(4,128)(2,1)}, bf16[2,4,1600]{2,1,0:T(4,128)(2,1)S(1)}, u32[]{:S(2)}, u32[]{:S(2)}) collective-permute-start(bf16[2,4,1600]{2,1,0:T(4,128)(2,1)} %param.3), channel_id=1, source_target_pairs={{128,256},{256,128},{129,257},{257,129},{130,258},{258,130},{131,2... | collective-permute-start | bytes 76808 | tf_op jit(solution)/shard_map/ppermute | solution.py:143
  15.1 3.8 %collective-permute-start.2 = (bf16[4,1,1600]{2,1,0:T(2,128)(2,1)S(1)}, bf16[4,1,1600]{2,1,0:T(2,128)(2,1)S(1)}, u32[]{:S(2)}, u32[]{:S(2)}) collective-permute-start(bf16[4,1,1600]{2,1,0:T(2,128)(2,1)S(1)} %get-tuple-element.28), channel_id=1, source_target_pairs={{1,2},{2,1},{3,4},{4,3},{5,6},{6,5},{7,8},{8,7},{9,10},{10,9},{11,... | collective-permute-start | bytes 38408 | tf_op jit(solution)/shard_map/ppermute | solution.py:149
  15.8 5.7 %collective-permute-start.3 = (bf16[4,1,1600]{2,1,0:T(2,128)(2,1)S(1)}, bf16[4,1,1600]{2,1,0:T(2,128)(2,1)S(1)}, u32[]{:S(2)}, u32[]{:S(2)}) collective-permute-start(bf16[4,1,1600]{2,1,0:T(2,128)(2,1)S(1)} %get-tuple-element.27), channel_id=1, source_target_pairs={{0,1},{1,0},{2,3},{3,2},{4,5},{5,4},{6,7},{7,6},{8,9},{9,8},{10,11... | collective-permute-start | bytes 38408 | tf_op jit(solution)/shard_map/ppermute | solution.py:150
  51.7 12.8 %collective-permute-start.5 = (bf16[128,1600]{1,0:T(8,128)(2,1)S(1)}, bf16[128,1600]{1,0:T(8,128)(2,1)S(1)}, u32[]{:S(2)}, u32[]{:S(2)}) collective-permute-start(bf16[128,1600]{1,0:T(8,128)(2,1)S(1)} %bitcast.21), channel_id=1, source_target_pairs={{1,0},{2,1},{3,2},{4,3},{5,4},{6,5},{7,6},{0,7},{9,8},{10,9},{11,1... | collective-permute-start | bytes 1228808 | tf_op jit(solution)/shard_map/ppermute | solution.py:123
  55.3 14.6 %collective-permute-start.6 = (bf16[128,1600]{1,0:T(8,128)(2,1)S(1)}, bf16[128,1600]{1,0:T(8,128)(2,1)S(1)}, u32[]{:S(2)}, u32[]{:S(2)}) collective-permute-start(bf16[128,1600]{1,0:T(8,128)(2,1)S(1)} %bitcast.22), channel_id=1, source_target_pairs={{8,0},{9,1},{10,2},{11,3},{12,4},{13,5},{14,6},{15,7},{16,8},{17,9... | collective-permute-start | bytes 1228808 | tf_op jit(solution)/shard_map/ppermute | solution.py:123
  57.9 12.0 %collective-permute-start.7 = (bf16[128,1600]{1,0:T(8,128)(2,1)S(1)}, bf16[128,1600]{1,0:T(8,128)(2,1)S(1)}, u32[]{:S(2)}, u32[]{:S(2)}) collective-permute-start(bf16[128,1600]{1,0:T(8,128)(2,1)S(1)} %bitcast.23), channel_id=1, source_target_pairs={{9,0},{10,1},{11,2},{12,3},{13,4},{14,5},{15,6},{8,7},{17,8},{18,9... | collective-permute-start | bytes 1228808 | tf_op jit(solution)/shard_map/ppermute | solution.py:123

commit v6 on v5

--- a/solution.py
+++ b/solution.py
@@ -138,11 +138,11 @@
 
 
 def rim(patterns):
-    odd = lax.axis_index("sx") % 2 == 1
-    near = lax.ppermute(patterns, "sx", swap_pairs((0, 2)))
-    far = lax.ppermute(patterns, "sx", swap_pairs((1,)))
-    above = jnp.where(odd, near[1:], far[1:])
-    below = jnp.where(odd, far[:1], near[:1])
+    plane = lax.axis_index("sx")
+    ahead = (jnp.arange(4) > plane)[:, None, None]
+    rows = lax.all_to_all(jnp.where(ahead, patterns[1], patterns[0]), "sx", 0, 0)
+    above = lax.dynamic_slice_in_dim(rows, jnp.maximum(plane - 1, 0), 1, 0)
+    below = lax.dynamic_slice_in_dim(rows, jnp.minimum(plane + 1, 3), 1, 0)
     block = jnp.concatenate([above, patterns, below], axis=0)
     even = lax.axis_index(COLS) % 2 == 0
     first, last = block[:, 0:1], block[:, 3:4]

time: 94.1 us -> 95.6 us (1.016)
  the two profiles are of different devices: /device:TPU:4 before, /device:TPU:2 now
where the time goes in v6:
time: 95.6 us; the launch traced here: 95 us
  blocking collectives  47.8 us (50%)
  starting transfers between devices  22.7 us (24%)
  waiting for transfers between devices  8.32 us (9%)
  matrix products  6.74 us (7%)
  Pallas kernels  4.29 us (4%)
  other arithmetic  2.73 us (3%)
  local copies, waits for them, and re-layouts  2.16 us (2%)
    all_to_all x1, blocking collectives, gather_class(): got = lax.all_to_all(copies, COLS, 0, 0, axis_index_groups=groups)  28.4 us
    all_to_all x1, blocking collectives, merge(): shares = lax.all_to_all(table, COLS, 0, 0, axis_index_groups=groups)  19.4 us
    all_to_all x1, starting transfers between devices, rim(): lax.all_to_all(jnp.where(ahead, patterns[1], patterns[0]), 'sx', 0, 0)  9.15 us
    ppermute x3, starting transfers between devices, from_neighbour(): return lax.ppermute(block, COLS, pairs)  8.98 us
    dot_general x4, matrix products, row_best(): scores = jnp.dot(points, half, preferred_element_type=jnp.float32)  6.74 us
    ppermute x1, waiting for transfers between devices, rim(): lax.ppermute(jnp.where(even, last, first), COLS, swap_pairs(range(0, 128,...  3.68 us
    pallas_call x1, Pallas kernels, hold(): pl.pallas_call(hold_kernel, out_shape=[pltpu.VMEM(half.shape, half.dtype)...  3.67 us
    all_to_all x1, waiting for transfers between devices, rim(): lax.all_to_all(jnp.where(ahead, patterns[1], patterns[0]), 'sx', 0, 0)  2.72 us
  transfers between devices with their start and end apart: 7, of which 3 were waited for; matrix products, arithmetic and copies ran while one was open for 8% of the time, Pallas kernels for 5%

profile of v6, /device:TPU:2, one launch (start us, length us, event | category | flops | bytes accessed | tf_op | source)
XLA Modules:
  0.0 95.0 jit_solution(14480453920807816720)
XLA Ops:
  0.0 1.9 %collective-permute-start.2 = (bf16[1600,1408]{1,0:T(8,128)(2,1)}, bf16[1600,1408]{1,0:T(8,128)(2,1)}, u32[]{:S(2)}, u32[]{:S(2)}) collective-permute-start(bf16[1600,1408]{1,0:T(8,128)(2,1)} %own_ref), channel_id=1, source_target_pairs={{0,64},{64,0},{1,65},{65,1},{2,66},{66,2},{3,67},{67,3},{4,68},{68... | collective-permute-start | bytes 13516808 | tf_op jit(solution)/shard_map/ppermute | solution.py:172
  1.9 0.7 slice_bitcast_fusion.1
  2.7 0.7 broadcast_select_fusion
  3.4 9.2 %all-to-all-start = ((bf16[4,4,1600]{2,1,0:T(4,128)(2,1)}), bf16[4,4,1600]{2,1,0:T(4,128)(2,1)S(1)}, u32[]{:S(2)}, u32[]{:S(2)}) async-start(bf16[4,4,1600]{2,1,0:T(4,128)(2,1)} %broadcast_select_fusion), calls=%async_computation | async-start | bytes 106496 | tf_op jit(solution)/shard_map/all_to_all | solution.py:143
  12.6 0.1 fusion
  12.7 0.1 and.63
  12.8 0.1 compare_and_fusion
  12.8 0.1 and.58
  12.9 0.1 and.59
  13.0 0.8 fusion.1
  13.8 0.1 copy.8
  14.0 2.7 %all-to-all-done = bf16[4,4,1600]{2,1,0:T(4,128)(2,1)S(1)} async-done(((bf16[4,4,1600]{2,1,0:T(4,128)(2,1)}), bf16[4,4,1600]{2,1,0:T(4,128)(2,1)S(1)}, u32[]{:S(2)}, u32[]{:S(2)}) %all-to-all-start) | async-done | bytes 51232 | tf_op jit(solution)/shard_map/all_to_all | solution.py:143
  16.7 0.8 pad_maximum_fusion.block_ref
  17.6 0.7 collective-permute-start
  18.2 2.0 %collective-permute-start.1 = (bf16[4,1,1600]{2,1,0:T(2,128)(2,1)S(1)}, bf16[4,1,1600]{2,1,0:T(2,128)(2,1)S(1)}, u32[]{:S(2)}, u32[]{:S(2)}) collective-permute-start(bf16[4,1,1600]{2,1,0:T(2,128)(2,1)S(1)} %get-tuple-element.27), channel_id=1, source_target_pairs={{0,1},{1,0},{2,3},{3,2},{4,5},{5,4},{6,7},{7,6},{8,9},{9,8},{10,11... | collective-permute-start | bytes 38408 | tf_op jit(solution)/shard_map/ppermute | solution.py:150
  20.2 0.1 maximum_maximum_fusion.weight_ref
  20.3 3.7 %collective-permute-done.1.near_ref = bf16[4,1,1600]{2,1,0:T(2,128)(2,1)S(1)} collective-permute-done((bf16[4,1,1600]{2,1,0:T(2,128)(2,1)S(1)}, bf16[4,1,1600]{2,1,0:T(2,128)(2,1)S(1)}, u32[]{:S(2)}, u32[]{:S(2)}) %collective-permute-start.1) | collective-permute-done | bytes 12832 | tf_op jit(solution)/shard_map/ppermute | solution.py:150
  24.0 0.6 shard_map.37
  24.6 28.4 %all_to_all.19 = bf16[16,8,1600]{2,1,0:T(8,128)(2,1)S(1)} all-to-all(bf16[16,8,1600]{2,1,0:T(8,128)(2,1)S(1)} %broadcast_in_dim.45), channel_id=1, replica_groups={{0,2,4,6,16,18,20,22,32,34,36,38,48,50,52,54},{1,3,5,7,17,19,21,23,33,3..., dimensions={0} | all-to-all | bytes 819200 | tf_op jit(solution)/shard_map/all_to_all | solution.py:112
  53.1 3.5 %collective-permute-start.3 = (bf16[128,1600]{1,0:T(8,128)(2,1)S(1)}, bf16[128,1600]{1,0:T(8,128)(2,1)S(1)}, u32[]{:S(2)}, u32[]{:S(2)}) collective-permute-start(bf16[128,1600]{1,0:T(8,128)(2,1)S(1)} %bitcast.25), channel_id=1, source_target_pairs={{1,0},{2,1},{3,2},{4,3},{5,4},{6,5},{7,6},{0,7},{9,8},{10,9},{11,1... | collective-permute-start | bytes 1228808 | tf_op jit(solution)/shard_map/ppermute | solution.py:123
  56.6 2.7 %collective-permute-start.4 = (bf16[128,1600]{1,0:T(8,128)(2,1)S(1)}, bf16[128,1600]{1,0:T(8,128)(2,1)S(1)}, u32[]{:S(2)}, u32[]{:S(2)}) collective-permute-start(bf16[128,1600]{1,0:T(8,128)(2,1)S(1)} %bitcast.26), channel_id=1, source_target_pairs={{8,0},{9,1},{10,2},{11,3},{12,4},{13,5},{14,6},{15,7},{16,8},{17,9... | collective-permute-start | bytes 1228808 | tf_op jit(solution)/shard_map/ppermute | solution.py:123
  59.3 2.8 %collective-permute-start.5 = (bf16[128,1600]{1,0:T(8,128)(2,1)S(1)}, bf16[128,1600]{1,0:T(8,128)(2,1)S(1)}, u32[]{:S(2)}, u32[]{:S(2)}) collective-permute-start(bf16[128,1600]{1,0:T(8,128)(2,1)S(1)} %bitcast.27), channel_id=1, source_target_pairs={{9,0},{10,1},{11,2},{12,3},{13,4},{14,5},{15,6},{8,7},{17,8},{18,9... | collective-permute-start | bytes 1228808 | tf_op jit(solution)/shard_map/ppermute | solution.py:123
  62.1 3.7 %shard_map.38 = (bf16[1600,1408]{1,0:T(8,128)(2,1)S(1)}, bf16[1600,1408]{1,0:T(8,128)(2,1)S(1)}) custom-call(bf16[1600,1408]{1,0:T(8,128)(2,1)} %own_ref, bf16[1600,1408]{1,0:T(8,128)(2,1)} %collective-permute-done.2.partner_ref), custom_call_target="tpu_custom_call" | custom-call | bytes 18022400 | tf_op jit(solution)/shard_map/pallas_call | solution.py:75
  65.9 1.7 %convolution_reduce_fusion.2 = f32[256]{0:T(256)S(1)} fusion(bf16[256,1600]{1,0:T(8,128)(2,1)S(1)} %constant_dynamic-update-slice_fusion, bf16[1600,1408]{1,0:T(8,128)(2,1)S(1)} %get-tuple-element.21), kind=kOutput, calls=%fused_computation.2 | convolution fusion | flops 1153793792 | bytes 5325824 | tf_op jit(solution)/shard_map/dot_general | solution.py:89
  67.6 1.7 %convolution_reduce_fusion.3 = f32[256]{0:T(256)S(1)} fusion(bf16[256,1600]{1,0:T(8,128)(2,1)S(1)} %constant_dynamic-update-slice_fusion, bf16[1600,1408]{1,0:T(8,128)(2,1)S(1)} %get-tuple-element.20), kind=kOutput, calls=%fused_computation.3 | convolution fusion | flops 1153793792 | bytes 5325824 | tf_op jit(solution)/shard_map/dot_general | solution.py:89
  69.3 1.9 %collective-permute-done.4 = bf16[128,1600]{1,0:T(8,128)(2,1)S(1)} collective-permute-done((bf16[128,1600]{1,0:T(8,128)(2,1)S(1)}, bf16[128,1600]{1,0:T(8,128)(2,1)S(1)}, u32[]{:S(2)}, u32[]{:S(2)}) %collective-permute-start.4) | collective-permute-done | bytes 409632 | tf_op jit(solution)/shard_map/ppermute | solution.py:123
  71.3 1.7 %convolution_reduce_fusion = f32[256]{0:T(256)S(1)} fusion(bf16[256,1600]{1,0:T(8,128)(2,1)S(1)} %constant_dynamic-update-slice_fusion.2, bf16[1600,1408]{1,0:T(8,128)(2,1)S(1)} %get-tuple-element.21), kind=kOutput, calls=%fused_computation | convolution fusion | flops 1153793792 | bytes 5325824 | tf_op jit(solution)/shard_map/dot_general | solution.py:89
  72.9 1.7 %convolution_reduce_fusion.1 = f32[256]{0:T(256)S(1)} fusion(bf16[256,1600]{1,0:T(8,128)(2,1)S(1)} %constant_dynamic-update-slice_fusion.2, bf16[1600,1408]{1,0:T(8,128)(2,1)S(1)} %get-tuple-element.20), kind=kOutput, calls=%fused_computation.1 | convolution fusion | flops 1153793792 | bytes 5325824 | tf_op jit(solution)/shard_map/dot_general | solution.py:89
  74.7 0.1 reshape.110
  74.8 19.4 %all_to_all.20 = f32[64,1,8]{2,1,0:T(1,128)S(1)} all-to-all(f32[64,1,8]{2,1,0:T(1,128)S(1)} %bitcast.30), channel_id=1, replica_groups={{0,1,2,3,4,5,6,7,8,9,10,11,12,13,14,15,16,17,18,19,20,21,22,23,24,25,26..., dimensions={0} | all-to-all | bytes 4096 | tf_op jit(solution)/shard_map/all_to_all | solution.py:132
  94.2 0.1 reduce_max.49
  94.3 0.6 reshape.111
  (24 shorter events, 0.4 us)
Async XLA Ops:
  0.0 62.1 %collective-permute-start.2 = (bf16[1600,1408]{1,0:T(8,128)(2,1)}, bf16[1600,1408]{1,0:T(8,128)(2,1)}, u32[]{:S(2)}, u32[]{:S(2)}) collective-permute-start(bf16[1600,1408]{1,0:T(8,128)(2,1)} %own_ref), channel_id=1, source_target_pairs={{0,64},{64,0},{1,65},{65,1},{2,66},{66,2},{3,67},{67,3},{4,68},{68... | collective-permute-start | bytes 13516808 | tf_op jit(solution)/shard_map/ppermute | solution.py:172
  3.4 13.3 %all-to-all-start = ((bf16[4,4,1600]{2,1,0:T(4,128)(2,1)}), bf16[4,4,1600]{2,1,0:T(4,128)(2,1)S(1)}, u32[]{:S(2)}, u32[]{:S(2)}) async-start(bf16[4,4,1600]{2,1,0:T(4,128)(2,1)} %broadcast_select_fusion), calls=%async_computation | async-start | bytes 106496 | tf_op jit(solution)/shard_map/all_to_all | solution.py:143
  17.6 2.7 %collective-permute-start = (bf16[4,1,1600]{2,1,0:T(2,128)(2,1)S(1)}, bf16[4,1,1600]{2,1,0:T(2,128)(2,1)S(1)}, u32[]{:S(2)}, u32[]{:S(2)}) collective-permute-start(bf16[4,1,1600]{2,1,0:T(2,128)(2,1)S(1)} %get-tuple-element.28), channel_id=1, source_target_pairs={{1,2},{2,1},{3,4},{4,3},{5,6},{6,5},{7,8},{8,7},{9,10},{10,9},{11,... | collective-permute-start | bytes 38408 | tf_op jit(solution)/shard_map/ppermute | solution.py:149
  18.2 5.7 %collective-permute-start.1 = (bf16[4,1,1600]{2,1,0:T(2,128)(2,1)S(1)}, bf16[4,1,1600]{2,1,0:T(2,128)(2,1)S(1)}, u32[]{:S(2)}, u32[]{:S(2)}) collective-permute-start(bf16[4,1,1600]{2,1,0:T(2,128)(2,1)S(1)} %get-tuple-element.27), channel_id=1, source_target_pairs={{0,1},{1,0},{2,3},{3,2},{4,5},{5,4},{6,7},{7,6},{8,9},{9,8},{10,11... | collective-permute-start | bytes 38408 | tf_op jit(solution)/shard_map/ppermute | solution.py:150
  53.1 12.8 %collective-permute-start.3 = (bf16[128,1600]{1,0:T(8,128)(2,1)S(1)}, bf16[128,1600]{1,0:T(8,128)(2,1)S(1)}, u32[]{:S(2)}, u32[]{:S(2)}) collective-permute-start(bf16[128,1600]{1,0:T(8,128)(2,1)S(1)} %bitcast.25), channel_id=1, source_target_pairs={{1,0},{2,1},{3,2},{4,3},{5,4},{6,5},{7,6},{0,7},{9,8},{10,9},{11,1... | collective-permute-start | bytes 1228808 | tf_op jit(solution)/shard_map/ppermute | solution.py:123
  56.6 14.6 %collective-permute-start.4 = (bf16[128,1600]{1,0:T(8,128)(2,1)S(1)}, bf16[128,1600]{1,0:T(8,128)(2,1)S(1)}, u32[]{:S(2)}, u32[]{:S(2)}) collective-permute-start(bf16[128,1600]{1,0:T(8,128)(2,1)S(1)} %bitcast.26), channel_id=1, source_target_pairs={{8,0},{9,1},{10,2},{11,3},{12,4},{13,5},{14,6},{15,7},{16,8},{17,9... | collective-permute-start | bytes 1228808 | tf_op jit(solution)/shard_map/ppermute | solution.py:123
  59.3 11.9 %collective-permute-start.5 = (bf16[128,1600]{1,0:T(8,128)(2,1)S(1)}, bf16[128,1600]{1,0:T(8,128)(2,1)S(1)}, u32[]{:S(2)}, u32[]{:S(2)}) collective-permute-start(bf16[128,1600]{1,0:T(8,128)(2,1)S(1)} %bitcast.27), channel_id=1, source_target_pairs={{9,0},{10,1},{11,2},{12,3},{13,4},{14,5},{15,6},{8,7},{17,8},{18,9... | collective-permute-start | bytes 1228808 | tf_op jit(solution)/shard_map/ppermute | solution.py:123

commit v7 on v5

--- a/solution.py
+++ b/solution.py
@@ -10,7 +10,8 @@
 PW = 40
 PIX = PH * PW
 WIDE = 1792
-COLS = ("sy", "z", "y")
+SPLIT = ("sx", "sy", "z_pair", "z_odd", "y_pair", "y_odd")
+COLS = SPLIT[1:]
 
 
 def average_kernel(block_ref, far_ref, near_ref, weight_ref, out_ref):
@@ -99,17 +100,9 @@
     return 64 * core + 8 * (z % 8) + y % 8
 
 
-def parity_class(core, z_odd, y_odd):
-    return [place(core, z, y) for z in range(z_odd, 8, 2) for y in range(y_odd, 8, 2)]
-
-
-PARITIES = [(0, 0), (0, 1), (1, 0), (1, 1)]
-
-
 def gather_class(block):
-    groups = [parity_class(core, z, y) for core in range(2) for z, y in PARITIES]
     copies = jnp.broadcast_to(block[None], (16,) + block.shape)
-    got = lax.all_to_all(copies, COLS, 0, 0, axis_index_groups=groups)
+    got = lax.all_to_all(copies, ("z_pair", "y_pair"), 0, 0)
     return got.reshape(-1, block.shape[1])
 
 
@@ -125,11 +118,10 @@
 
 def merge(tables):
     table = jnp.stack([pair.reshape(2, 128) for pair in tables])
-    table = jnp.where(lax.axis_index("z") % 2 == 1, table[::-1], table)
-    table = jnp.where(lax.axis_index("y") % 2 == 1, table[:, ::-1], table)
+    table = jnp.where(lax.axis_index("z_odd") == 1, table[::-1], table)
+    table = jnp.where(lax.axis_index("y_odd") == 1, table[:, ::-1], table)
     table = jnp.transpose(table.reshape(2, 2, 4, 4, 8), (2, 0, 3, 1, 4)).reshape(64, 8)
-    groups = [[place(core, z, y) for z in range(8) for y in range(8)] for core in range(2)]
-    shares = lax.all_to_all(table, COLS, 0, 0, axis_index_groups=groups)
+    shares = lax.all_to_all(table, COLS[1:], 0, 0)
     return jnp.max(shares, axis=0)
 
 
@@ -185,7 +177,7 @@
 
 
 def solution(mesh):
-    split = Mesh(mesh.devices.reshape(4, 2, 8, 8), ("sx",) + COLS)
+    split = Mesh(mesh.devices.reshape(4, 2, 4, 2, 4, 2), SPLIT)
     return jax.shard_map(
         on_device,
         mesh=split,

time: 94.1 us -> 94 us (level)
  no operation moved by 1% of the time
where the time goes in v7:
time: 94 us; the launch traced here: 93.6 us
  blocking collectives  48.9 us (52%)
  starting transfers between devices  24.9 us (26%)
  matrix products  6.74 us (7%)
  waiting for transfers between devices  5.14 us (5%)
  Pallas kernels  4.29 us (5%)
  other arithmetic  2.02 us (2%)
  local copies, waits for them, and re-layouts  1.41 us (2%)
    all_to_all x1, blocking collectives, gather_class(): got = lax.all_to_all(copies, ('z_pair', 'y_pair'), 0, 0)  29.5 us
    all_to_all x1, blocking collectives, merge(): shares = lax.all_to_all(table, COLS[1:], 0, 0)  19.3 us
    ppermute x3, starting transfers between devices, from_neighbour(): return lax.ppermute(block, COLS, pairs)  9.02 us
    ppermute x1, starting transfers between devices, rim(): far = lax.ppermute(patterns, 'sx', swap_pairs((1,)))  7.16 us
    dot_general x4, matrix products, row_best(): scores = jnp.dot(points, half, preferred_element_type=jnp.float32)  6.74 us
    pallas_call x1, Pallas kernels, hold(): pl.pallas_call(hold_kernel, out_shape=[pltpu.VMEM(half.shape, half.dtype)...  3.67 us
    ppermute x1, starting transfers between devices, rim(): near = lax.ppermute(patterns, 'sx', swap_pairs((0, 2)))  3.11 us
    ppermute x1, starting transfers between devices, rim(): lax.ppermute(jnp.where(even, last, first), COLS, swap_pairs(range(0, 128,...  3.07 us
  transfers between devices with their start and end apart: 8, of which 3 were waited for; matrix products, arithmetic and copies ran while one was open for 6% of the time, Pallas kernels for 5%

profile of v7, /device:TPU:4, one launch (start us, length us, event | category | flops | bytes accessed | tf_op | source)
XLA Modules:
  0.0 93.6 jit_solution(5905752633503342662)
XLA Ops:
  0.0 1.9 %collective-permute-start.4 = (bf16[1600,1408]{1,0:T(8,128)(2,1)}, bf16[1600,1408]{1,0:T(8,128)(2,1)}, u32[]{:S(2)}, u32[]{:S(2)}) collective-permute-start(bf16[1600,1408]{1,0:T(8,128)(2,1)} %own_ref), channel_id=1, source_target_pairs={{0,64},{64,0},{1,65},{65,1},{2,66},{66,2},{3,67},{67,3},{4,68},{68... | collective-permute-start | bytes 13516808 | tf_op jit(solution)/shard_map/ppermute | solution.py:164
  1.9 3.1 %collective-permute-start = (bf16[2,4,1600]{2,1,0:T(4,128)(2,1)}, bf16[2,4,1600]{2,1,0:T(4,128)(2,1)S(1)}, u32[]{:S(2)}, u32[]{:S(2)}) collective-permute-start(bf16[2,4,1600]{2,1,0:T(4,128)(2,1)} %param.3), channel_id=1, source_target_pairs={{0,128},{128,0},{256,384},{384,256},{1,129},{129,1},{257,385},{385... | collective-permute-start | bytes 76808 | tf_op jit(solution)/shard_map/ppermute | solution.py:134
  5.0 7.2 %collective-permute-start.1 = (bf16[2,4,1600]{2,1,0:T(4,128)(2,1)}, bf16[2,4,1600]{2,1,0:T(4,128)(2,1)S(1)}, u32[]{:S(2)}, u32[]{:S(2)}) collective-permute-start(bf16[2,4,1600]{2,1,0:T(4,128)(2,1)} %param.3), channel_id=1, source_target_pairs={{128,256},{256,128},{129,257},{257,129},{130,258},{258,130},{131,2... | collective-permute-start | bytes 76808 | tf_op jit(solution)/shard_map/ppermute | solution.py:135
  12.2 0.1 fusion
  12.3 0.1 and.60
  12.4 0.1 compare_and_fusion
  12.5 0.1 and.55
  12.6 0.1 and.56
  12.7 0.8 fusion.1
  13.4 0.1 copy.8
  13.5 0.1 pad.4.clone
  13.6 0.6 collective-permute-done.1
  14.2 0.8 pad_maximum_fusion.block_ref
  15.1 0.7 collective-permute-start.2
  15.8 3.1 %collective-permute-start.3 = (bf16[4,1,1600]{2,1,0:T(2,128)(2,1)S(1)}, bf16[4,1,1600]{2,1,0:T(2,128)(2,1)S(1)}, u32[]{:S(2)}, u32[]{:S(2)}) collective-permute-start(bf16[4,1,1600]{2,1,0:T(2,128)(2,1)S(1)} %get-tuple-element.27), channel_id=1, source_target_pairs={{0,1},{1,0},{2,3},{3,2},{4,5},{5,4},{6,7},{7,6},{8,9},{9,8},{10,11... | collective-permute-start | bytes 38408 | tf_op jit(solution)/shard_map/ppermute | solution.py:142
  18.9 0.1 maximum_maximum_fusion.weight_ref
  18.9 2.6 %collective-permute-done.3.near_ref = bf16[4,1,1600]{2,1,0:T(2,128)(2,1)S(1)} collective-permute-done((bf16[4,1,1600]{2,1,0:T(2,128)(2,1)S(1)}, bf16[4,1,1600]{2,1,0:T(2,128)(2,1)S(1)}, u32[]{:S(2)}, u32[]{:S(2)}) %collective-permute-start.3) | collective-permute-done | bytes 12832 | tf_op jit(solution)/shard_map/ppermute | solution.py:142
  21.5 0.6 shard_map.37
  22.2 29.5 %all_to_all.14 = bf16[16,8,1600]{2,1,0:T(8,128)(2,1)S(1)} all-to-all(bf16[16,8,1600]{2,1,0:T(8,128)(2,1)S(1)} %broadcast_in_dim.13), channel_id=1, replica_groups=mesh['sx'=4,'sy'=2,'z_pair'=4,'z_odd'=2,'y_pair'=4,'y_odd'=2] {'z_pair',..., dimensions={0} | all-to-all | bytes 819200 | tf_op jit(solution)/shard_map/all_to_all | solution.py:105
  51.7 3.6 %collective-permute-start.5 = (bf16[128,1600]{1,0:T(8,128)(2,1)S(1)}, bf16[128,1600]{1,0:T(8,128)(2,1)S(1)}, u32[]{:S(2)}, u32[]{:S(2)}) collective-permute-start(bf16[128,1600]{1,0:T(8,128)(2,1)S(1)} %bitcast.21), channel_id=1, source_target_pairs={{1,0},{2,1},{3,2},{4,3},{5,4},{6,5},{7,6},{0,7},{9,8},{10,9},{11,1... | collective-permute-start | bytes 1228808 | tf_op jit(solution)/shard_map/ppermute | solution.py:116
  55.3 2.6 %collective-permute-start.6 = (bf16[128,1600]{1,0:T(8,128)(2,1)S(1)}, bf16[128,1600]{1,0:T(8,128)(2,1)S(1)}, u32[]{:S(2)}, u32[]{:S(2)}) collective-permute-start(bf16[128,1600]{1,0:T(8,128)(2,1)S(1)} %bitcast.22), channel_id=1, source_target_pairs={{8,0},{9,1},{10,2},{11,3},{12,4},{13,5},{14,6},{15,7},{16,8},{17,9... | collective-permute-start | bytes 1228808 | tf_op jit(solution)/shard_map/ppermute | solution.py:116
  57.9 2.9 %collective-permute-start.7 = (bf16[128,1600]{1,0:T(8,128)(2,1)S(1)}, bf16[128,1600]{1,0:T(8,128)(2,1)S(1)}, u32[]{:S(2)}, u32[]{:S(2)}) collective-permute-start(bf16[128,1600]{1,0:T(8,128)(2,1)S(1)} %bitcast.23), channel_id=1, source_target_pairs={{9,0},{10,1},{11,2},{12,3},{13,4},{14,5},{15,6},{8,7},{17,8},{18,9... | collective-permute-start | bytes 1228808 | tf_op jit(solution)/shard_map/ppermute | solution.py:116
  60.8 3.7 %shard_map.38 = (bf16[1600,1408]{1,0:T(8,128)(2,1)S(1)}, bf16[1600,1408]{1,0:T(8,128)(2,1)S(1)}) custom-call(bf16[1600,1408]{1,0:T(8,128)(2,1)} %own_ref, bf16[1600,1408]{1,0:T(8,128)(2,1)} %collective-permute-done.4.partner_ref), custom_call_target="tpu_custom_call" | custom-call | bytes 18022400 | tf_op jit(solution)/shard_map/pallas_call | solution.py:76
  64.5 1.7 %convolution_reduce_fusion.2 = f32[256]{0:T(256)S(1)} fusion(bf16[256,1600]{1,0:T(8,128)(2,1)S(1)} %constant_dynamic-update-slice_fusion, bf16[1600,1408]{1,0:T(8,128)(2,1)S(1)} %get-tuple-element.21), kind=kOutput, calls=%fused_computation.2 | convolution fusion | flops 1153793792 | bytes 5325824 | tf_op jit(solution)/shard_map/dot_general | solution.py:90
  66.2 1.7 %convolution_reduce_fusion.3 = f32[256]{0:T(256)S(1)} fusion(bf16[256,1600]{1,0:T(8,128)(2,1)S(1)} %constant_dynamic-update-slice_fusion, bf16[1600,1408]{1,0:T(8,128)(2,1)S(1)} %get-tuple-element.20), kind=kOutput, calls=%fused_computation.3 | convolution fusion | flops 1153793792 | bytes 5325824 | tf_op jit(solution)/shard_map/dot_general | solution.py:90
  67.9 1.9 %collective-permute-done.6 = bf16[128,1600]{1,0:T(8,128)(2,1)S(1)} collective-permute-done((bf16[128,1600]{1,0:T(8,128)(2,1)S(1)}, bf16[128,1600]{1,0:T(8,128)(2,1)S(1)}, u32[]{:S(2)}, u32[]{:S(2)}) %collective-permute-start.6) | collective-permute-done | bytes 409632 | tf_op jit(solution)/shard_map/ppermute | solution.py:116
  69.9 1.7 %convolution_reduce_fusion = f32[256]{0:T(256)S(1)} fusion(bf16[256,1600]{1,0:T(8,128)(2,1)S(1)} %constant_dynamic-update-slice_fusion.2, bf16[1600,1408]{1,0:T(8,128)(2,1)S(1)} %get-tuple-element.21), kind=kOutput, calls=%fused_computation | convolution fusion | flops 1153793792 | bytes 5325824 | tf_op jit(solution)/shard_map/dot_general | solution.py:90
  71.6 1.7 %convolution_reduce_fusion.1 = f32[256]{0:T(256)S(1)} fusion(bf16[256,1600]{1,0:T(8,128)(2,1)S(1)} %constant_dynamic-update-slice_fusion.2, bf16[1600,1408]{1,0:T(8,128)(2,1)S(1)} %get-tuple-element.20), kind=kOutput, calls=%fused_computation.1 | convolution fusion | flops 1153793792 | bytes 5325824 | tf_op jit(solution)/shard_map/dot_general | solution.py:90
  73.4 0.1 reshape.106
  73.5 19.3 %all_to_all.15 = f32[64,1,8]{2,1,0:T(1,128)S(1)} all-to-all(f32[64,1,8]{2,1,0:T(1,128)S(1)} %bitcast.26), channel_id=1, replica_groups=mesh['sx'=4,'sy'=2,'z_pair'=4,'z_odd'=2,'y_pair'=4,'y_odd'=2] {'z_pair',..., dimensions={0} | all-to-all | bytes 4096 | tf_op jit(solution)/shard_map/all_to_all | solution.py:124
  92.9 0.1 reduce_max.49
  92.9 0.6 reshape.107
  (23 shorter events, 0.4 us)
Async XLA Ops:
  0.0 60.8 %collective-permute-start.4 = (bf16[1600,1408]{1,0:T(8,128)(2,1)}, bf16[1600,1408]{1,0:T(8,128)(2,1)}, u32[]{:S(2)}, u32[]{:S(2)}) collective-permute-start(bf16[1600,1408]{1,0:T(8,128)(2,1)} %own_ref), channel_id=1, source_target_pairs={{0,64},{64,0},{1,65},{65,1},{2,66},{66,2},{3,67},{67,3},{4,68},{68... | collective-permute-start | bytes 13516808 | tf_op jit(solution)/shard_map/ppermute | solution.py:164
  1.9 11.7 %collective-permute-start = (bf16[2,4,1600]{2,1,0:T(4,128)(2,1)}, bf16[2,4,1600]{2,1,0:T(4,128)(2,1)S(1)}, u32[]{:S(2)}, u32[]{:S(2)}) collective-permute-start(bf16[2,4,1600]{2,1,0:T(4,128)(2,1)} %param.3), channel_id=1, source_target_pairs={{0,128},{128,0},{256,384},{384,256},{1,129},{129,1},{257,385},{385... | collective-permute-start | bytes 76808 | tf_op jit(solution)/shard_map/ppermute | solution.py:134
  5.0 9.2 %collective-permute-start.1 = (bf16[2,4,1600]{2,1,0:T(4,128)(2,1)}, bf16[2,4,1600]{2,1,0:T(4,128)(2,1)S(1)}, u32[]{:S(2)}, u32[]{:S(2)}) collective-permute-start(bf16[2,4,1600]{2,1,0:T(4,128)(2,1)} %param.3), channel_id=1, source_target_pairs={{128,256},{256,128},{129,257},{257,129},{130,258},{258,130},{131,2... | collective-permute-start | bytes 76808 | tf_op jit(solution)/shard_map/ppermute | solution.py:135
  15.1 3.8 %collective-permute-start.2 = (bf16[4,1,1600]{2,1,0:T(2,128)(2,1)S(1)}, bf16[4,1,1600]{2,1,0:T(2,128)(2,1)S(1)}, u32[]{:S(2)}, u32[]{:S(2)}) collective-permute-start(bf16[4,1,1600]{2,1,0:T(2,128)(2,1)S(1)} %get-tuple-element.28), channel_id=1, source_target_pairs={{1,2},{2,1},{3,4},{4,3},{5,6},{6,5},{7,8},{8,7},{9,10},{10,9},{11,... | collective-permute-start | bytes 38408 | tf_op jit(solution)/shard_map/ppermute | solution.py:141
  15.8 5.7 %collective-permute-start.3 = (bf16[4,1,1600]{2,1,0:T(2,128)(2,1)S(1)}, bf16[4,1,1600]{2,1,0:T(2,128)(2,1)S(1)}, u32[]{:S(2)}, u32[]{:S(2)}) collective-permute-start(bf16[4,1,1600]{2,1,0:T(2,128)(2,1)S(1)} %get-tuple-element.27), channel_id=1, source_target_pairs={{0,1},{1,0},{2,3},{3,2},{4,5},{5,4},{6,7},{7,6},{8,9},{9,8},{10,11... | collective-permute-start | bytes 38408 | tf_op jit(solution)/shard_map/ppermute | solution.py:142
  51.7 12.8 %collective-permute-start.5 = (bf16[128,1600]{1,0:T(8,128)(2,1)S(1)}, bf16[128,1600]{1,0:T(8,128)(2,1)S(1)}, u32[]{:S(2)}, u32[]{:S(2)}) collective-permute-start(bf16[128,1600]{1,0:T(8,128)(2,1)S(1)} %bitcast.21), channel_id=1, source_target_pairs={{1,0},{2,1},{3,2},{4,3},{5,4},{6,5},{7,6},{0,7},{9,8},{10,9},{11,1... | collective-permute-start | bytes 1228808 | tf_op jit(solution)/shard_map/ppermute | solution.py:116
  55.3 14.6 %collective-permute-start.6 = (bf16[128,1600]{1,0:T(8,128)(2,1)S(1)}, bf16[128,1600]{1,0:T(8,128)(2,1)S(1)}, u32[]{:S(2)}, u32[]{:S(2)}) collective-permute-start(bf16[128,1600]{1,0:T(8,128)(2,1)S(1)} %bitcast.22), channel_id=1, source_target_pairs={{8,0},{9,1},{10,2},{11,3},{12,4},{13,5},{14,6},{15,7},{16,8},{17,9... | collective-permute-start | bytes 1228808 | tf_op jit(solution)/shard_map/ppermute | solution.py:116
  57.9 12.0 %collective-permute-start.7 = (bf16[128,1600]{1,0:T(8,128)(2,1)S(1)}, bf16[128,1600]{1,0:T(8,128)(2,1)S(1)}, u32[]{:S(2)}, u32[]{:S(2)}) collective-permute-start(bf16[128,1600]{1,0:T(8,128)(2,1)S(1)} %bitcast.23), channel_id=1, source_target_pairs={{9,0},{10,1},{11,2},{12,3},{13,4},{14,5},{15,6},{8,7},{17,8},{18,9... | collective-permute-start | bytes 1228808 | tf_op jit(solution)/shard_map/ppermute | solution.py:116

commit v8 on v5

--- a/solution.py
+++ b/solution.py
@@ -60,10 +60,11 @@
     )(block, far, near, weights)
 
 
-def hold_kernel(own_ref, partner_ref, own_held, partner_held, sems):
+def hold_kernel(own_ref, partner_ref, held_ref, sems):
+    columns = own_ref.shape[1]
     copies = [
-        pltpu.make_async_copy(own_ref, own_held, sems.at[0]),
-        pltpu.make_async_copy(partner_ref, partner_held, sems.at[1]),
+        pltpu.make_async_copy(own_ref, held_ref.at[:, pl.ds(0, columns)], sems.at[0]),
+        pltpu.make_async_copy(partner_ref, held_ref.at[:, pl.ds(columns, columns)], sems.at[1]),
     ]
     for copy in copies:
         copy.start()
@@ -74,9 +75,9 @@
 def hold(own, partner):
     return pl.pallas_call(
         hold_kernel,
-        out_shape=[pltpu.VMEM(half.shape, half.dtype) for half in (own, partner)],
+        out_shape=pltpu.VMEM((own.shape[0], 2 * own.shape[1]), own.dtype),
         in_specs=[pl.BlockSpec(memory_space=space) for space in (pltpu.HBM, pl.ANY)],
-        out_specs=[pl.BlockSpec(memory_space=pltpu.VMEM)] * 2,
+        out_specs=pl.BlockSpec(memory_space=pltpu.VMEM),
         scratch_shapes=[pltpu.SemaphoreType.DMA((2,))],
         compiler_params=pltpu.CompilerParams(vmem_limit_bytes=16 * 1024 * 1024),
         cost_estimate=pl.CostEstimate(
@@ -85,14 +86,9 @@
     )(pltpu.with_memory_space_constraint(own, pltpu.HBM), partner)
 
 
-def row_best(points, half):
-    scores = jnp.dot(points, half, preferred_element_type=jnp.float32)
-    return jnp.max(scores, axis=1)
-
-
-def best_of(first, second, halves):
+def best_of(first, second, held):
     points = jnp.concatenate([first, second], axis=0)
-    return jnp.maximum(*[row_best(points, half) for half in halves])
+    return jnp.max(jnp.dot(points, held, preferred_element_type=jnp.float32), axis=1)
 
 
 def place(core, z, y):
@@ -127,9 +123,9 @@
     table = jnp.stack([pair.reshape(2, 128) for pair in tables])
     table = jnp.where(lax.axis_index("z") % 2 == 1, table[::-1], table)
     table = jnp.where(lax.axis_index("y") % 2 == 1, table[:, ::-1], table)
-    table = jnp.transpose(table.reshape(2, 2, 4, 4, 8), (2, 0, 3, 1, 4)).reshape(64, 8)
+    table = jnp.transpose(table.reshape(2, 2, 4, 4, 2, 4), (2, 0, 3, 1, 4, 5))
     groups = [[place(core, z, y) for z in range(8) for y in range(8)] for core in range(2)]
-    shares = lax.all_to_all(table, COLS, 0, 0, axis_index_groups=groups)
+    shares = lax.all_to_all(table.reshape(64, 2, 4), COLS, 0, 0, axis_index_groups=groups)
     return jnp.max(shares, axis=0)
 
 
@@ -177,11 +173,11 @@
     across = from_neighbour(own, 1, 0)
     diagonal = from_neighbour(own, 1, 1)
     own, *halves = lax.optimization_barrier((own, dictionary, partner))
-    halves = hold(*halves)
-    early = best_of(own, ahead, halves)
+    held = hold(*halves)
+    early = best_of(own, ahead, held)
     early, across, diagonal = lax.optimization_barrier((early, across, diagonal))
-    tables = [early, best_of(across, diagonal, halves)]
-    return merge(tables).reshape(rows, cols)
+    tables = [early, best_of(across, diagonal, held)]
+    return merge(tables)
 
 
 def solution(mesh):

time: 94.1 us -> 93.8 us (level)
  matrix products: 6.74 us -> 5.79 us
    dot_general x4 -> x2, matrix products: 6.74 us -> 5.79 us  [best_of(): jnp.dot(points, held, preferred_element_type=jnp.float32)]
where the time goes in v8:
time: 93.8 us; the launch traced here: 93.4 us
  blocking collectives  49.1 us (52%)
  starting transfers between devices  24.9 us (27%)
  matrix products  5.79 us (6%)
  waiting for transfers between devices  5.75 us (6%)
  Pallas kernels  4.29 us (5%)
  other arithmetic  2.56 us (3%)
    all_to_all x1, blocking collectives, gather_class(): got = lax.all_to_all(copies, COLS, 0, 0, axis_index_groups=groups)  29.5 us
    all_to_all x1, blocking collectives, merge(): lax.all_to_all(table.reshape(64, 2, 4), COLS, 0, 0, axis_index_groups=gro...  19.6 us
    ppermute x3, starting transfers between devices, from_neighbour(): return lax.ppermute(block, COLS, pairs)  9.02 us
    ppermute x1, starting transfers between devices, rim(): far = lax.ppermute(patterns, 'sx', swap_pairs((1,)))  7.16 us
    dot_general x2, matrix products, best_of(): jnp.dot(points, held, preferred_element_type=jnp.float32)  5.79 us
    pallas_call x1, Pallas kernels, hold(): pl.pallas_call(hold_kernel, out_shape=pltpu.VMEM((own.shape[0], 2 * own.s...  3.67 us
    ppermute x1, starting transfers between devices, rim(): near = lax.ppermute(patterns, 'sx', swap_pairs((0, 2)))  3.11 us
    ppermute x1, starting transfers between devices, rim(): lax.ppermute(jnp.where(even, last, first), COLS, swap_pairs(range(0, 128,...  3.07 us
  transfers between devices with their start and end apart: 8, of which 3 were waited for; matrix products, arithmetic and copies ran while one was open for 6% of the time, Pallas kernels for 5%

profile of v8, /device:TPU:4, one launch (start us, length us, event | category | flops | bytes accessed | tf_op | source)
XLA Modules:
  0.0 93.4 jit_solution(12014279392760009936)
XLA Ops:
  0.0 1.9 %collective-permute-start.4 = (bf16[1600,1408]{1,0:T(8,128)(2,1)}, bf16[1600,1408]{1,0:T(8,128)(2,1)}, u32[]{:S(2)}, u32[]{:S(2)}) collective-permute-start(bf16[1600,1408]{1,0:T(8,128)(2,1)} %own_ref), channel_id=1, source_target_pairs={{0,64},{64,0},{1,65},{65,1},{2,66},{66,2},{3,67},{67,3},{4,68},{68... | collective-permute-start | bytes 13516808 | tf_op jit(solution)/shard_map/ppermute | solution.py:168
  1.9 3.1 %collective-permute-start = (bf16[2,4,1600]{2,1,0:T(4,128)(2,1)}, bf16[2,4,1600]{2,1,0:T(4,128)(2,1)S(1)}, u32[]{:S(2)}, u32[]{:S(2)}) collective-permute-start(bf16[2,4,1600]{2,1,0:T(4,128)(2,1)} %param.3), channel_id=1, source_target_pairs={{0,128},{128,0},{256,384},{384,256},{1,129},{129,1},{257,385},{385... | collective-permute-start | bytes 76808 | tf_op jit(solution)/shard_map/ppermute | solution.py:138
  5.0 7.2 %collective-permute-start.1 = (bf16[2,4,1600]{2,1,0:T(4,128)(2,1)}, bf16[2,4,1600]{2,1,0:T(4,128)(2,1)S(1)}, u32[]{:S(2)}, u32[]{:S(2)}) collective-permute-start(bf16[2,4,1600]{2,1,0:T(4,128)(2,1)} %param.3), channel_id=1, source_target_pairs={{128,256},{256,128},{129,257},{257,129},{130,258},{258,130},{131,2... | collective-permute-start | bytes 76808 | tf_op jit(solution)/shard_map/ppermute | solution.py:139
  12.2 0.1 fusion.6
  12.3 0.1 and.68
  12.4 0.1 compare_and_fusion
  12.5 0.1 and.63
  12.6 0.1 and.64
  12.7 0.8 fusion.9
  13.4 0.1 copy.8
  13.5 0.1 pad.8.clone
  13.6 0.6 collective-permute-done.1
  14.2 0.8 pad_maximum_fusion.block_ref
  15.0 0.1 broadcast_select_fusion
  15.1 0.7 collective-permute-start.2
  15.8 3.1 %collective-permute-start.3 = (bf16[4,1,1600]{2,1,0:T(2,128)(2,1)S(1)}, bf16[4,1,1600]{2,1,0:T(2,128)(2,1)S(1)}, u32[]{:S(2)}, u32[]{:S(2)}) collective-permute-start(bf16[4,1,1600]{2,1,0:T(2,128)(2,1)S(1)} %get-tuple-element.23), channel_id=1, source_target_pairs={{0,1},{1,0},{2,3},{3,2},{4,5},{5,4},{6,7},{7,6},{8,9},{9,8},{10,11... | collective-permute-start | bytes 38408 | tf_op jit(solution)/shard_map/ppermute | solution.py:146
  18.9 0.1 maximum_maximum_fusion.weight_ref
  18.9 2.6 %collective-permute-done.3.near_ref = bf16[4,1,1600]{2,1,0:T(2,128)(2,1)S(1)} collective-permute-done((bf16[4,1,1600]{2,1,0:T(2,128)(2,1)S(1)}, bf16[4,1,1600]{2,1,0:T(2,128)(2,1)S(1)}, u32[]{:S(2)}, u32[]{:S(2)}) %collective-permute-start.3) | collective-permute-done | bytes 12832 | tf_op jit(solution)/shard_map/ppermute | solution.py:146
  21.5 0.6 shard_map.37
  22.2 29.5 %all_to_all.10 = bf16[16,8,1600]{2,1,0:T(8,128)(2,1)S(1)} all-to-all(bf16[16,8,1600]{2,1,0:T(8,128)(2,1)S(1)} %broadcast_in_dim.13), channel_id=1, replica_groups={{0,2,4,6,16,18,20,22,32,34,36,38,48,50,52,54},{1,3,5,7,17,19,21,23,33,3..., dimensions={0} | all-to-all | bytes 819200 | tf_op jit(solution)/shard_map/all_to_all | solution.py:108
  51.7 3.6 %collective-permute-start.5 = (bf16[128,1600]{1,0:T(8,128)(2,1)S(1)}, bf16[128,1600]{1,0:T(8,128)(2,1)S(1)}, u32[]{:S(2)}, u32[]{:S(2)}) collective-permute-start(bf16[128,1600]{1,0:T(8,128)(2,1)S(1)} %bitcast.12), channel_id=1, source_target_pairs={{1,0},{2,1},{3,2},{4,3},{5,4},{6,5},{7,6},{0,7},{9,8},{10,9},{11,1... | collective-permute-start | bytes 1228808 | tf_op jit(solution)/shard_map/ppermute | solution.py:119
  55.3 2.6 %collective-permute-start.6 = (bf16[128,1600]{1,0:T(8,128)(2,1)S(1)}, bf16[128,1600]{1,0:T(8,128)(2,1)S(1)}, u32[]{:S(2)}, u32[]{:S(2)}) collective-permute-start(bf16[128,1600]{1,0:T(8,128)(2,1)S(1)} %bitcast.13), channel_id=1, source_target_pairs={{8,0},{9,1},{10,2},{11,3},{12,4},{13,5},{14,6},{15,7},{16,8},{17,9... | collective-permute-start | bytes 1228808 | tf_op jit(solution)/shard_map/ppermute | solution.py:119
  57.9 2.9 %collective-permute-start.7 = (bf16[128,1600]{1,0:T(8,128)(2,1)S(1)}, bf16[128,1600]{1,0:T(8,128)(2,1)S(1)}, u32[]{:S(2)}, u32[]{:S(2)}) collective-permute-start(bf16[128,1600]{1,0:T(8,128)(2,1)S(1)} %bitcast.14), channel_id=1, source_target_pairs={{9,0},{10,1},{11,2},{12,3},{13,4},{14,5},{15,6},{8,7},{17,8},{18,9... | collective-permute-start | bytes 1228808 | tf_op jit(solution)/shard_map/ppermute | solution.py:119
  60.8 3.7 %shard_map.38 = bf16[1600,2816]{1,0:T(8,128)(2,1)S(1)} custom-call(bf16[1600,1408]{1,0:T(8,128)(2,1)} %own_ref, bf16[1600,1408]{1,0:T(8,128)(2,1)} %collective-permute-done.4.partner_ref), custom_call_target="tpu_custom_call" | custom-call | bytes 18022400 | tf_op jit(solution)/shard_map/pallas_call | solution.py:76
  64.5 2.9 %convolution_reduce_fusion.1 = f32[256]{0:T(256)S(1)} fusion(bf16[1600,2816]{1,0:T(8,128)(2,1)S(1)} %shard_map.38, bf16[128,1600]{1,0:T(8,128)(2,1)S(1)} %collective-permute-done.5, bf16[128,1600]{1,0:T(8,128)(2,1)S(1)} %bitcast.15), kind=kOutput, calls=%fused_computation.1 | convolution fusion | flops 2309226240 | bytes 9831424 | tf_op jit(solution)/shard_map/dot_general | solution.py:91
  67.3 2.6 %collective-permute-done.6 = bf16[128,1600]{1,0:T(8,128)(2,1)S(1)} collective-permute-done((bf16[128,1600]{1,0:T(8,128)(2,1)S(1)}, bf16[128,1600]{1,0:T(8,128)(2,1)S(1)}, u32[]{:S(2)}, u32[]{:S(2)}) %collective-permute-start.6) | collective-permute-done | bytes 409632 | tf_op jit(solution)/shard_map/ppermute | solution.py:119
  69.9 2.9 %convolution_reduce_fusion = f32[256]{0:T(256)S(1)} fusion(bf16[1600,2816]{1,0:T(8,128)(2,1)S(1)} %shard_map.38, bf16[128,1600]{1,0:T(8,128)(2,1)S(1)} %collective-permute-done.7, bf16[128,1600]{1,0:T(8,128)(2,1)S(1)} %collective-permute-done.6), kind=kOutput, calls=%fused_computation | convolution fusion | flops 2309226240 | bytes 9831424 | tf_op jit(solution)/shard_map/dot_general | solution.py:91
  72.9 0.1 reshape.84
  73.0 0.1 copy.9
  73.1 0.1 copy.10
  73.2 19.6 %all_to_all.11 = f32[64,2,4]{2,1,0:T(2,128)S(1)} all-to-all(f32[64,2,4]{2,1,0:T(2,128)S(1)} %copy.10), channel_id=1, replica_groups={{0,1,2,3,4,5,6,7,8,9,10,11,12,13,14,15,16,17,18,19,20,21,22,23,24,25,26..., dimensions={0} | all-to-all | bytes 4096 | tf_op jit(solution)/shard_map/all_to_all | solution.py:128
  92.7 0.6 reduce_max.29
  (15 shorter events, 0.1 us)
Async XLA Ops:
  0.0 60.8 %collective-permute-start.4 = (bf16[1600,1408]{1,0:T(8,128)(2,1)}, bf16[1600,1408]{1,0:T(8,128)(2,1)}, u32[]{:S(2)}, u32[]{:S(2)}) collective-permute-start(bf16[1600,1408]{1,0:T(8,128)(2,1)} %own_ref), channel_id=1, source_target_pairs={{0,64},{64,0},{1,65},{65,1},{2,66},{66,2},{3,67},{67,3},{4,68},{68... | collective-permute-start | bytes 13516808 | tf_op jit(solution)/shard_map/ppermute | solution.py:168
  1.9 11.7 %collective-permute-start = (bf16[2,4,1600]{2,1,0:T(4,128)(2,1)}, bf16[2,4,1600]{2,1,0:T(4,128)(2,1)S(1)}, u32[]{:S(2)}, u32[]{:S(2)}) collective-permute-start(bf16[2,4,1600]{2,1,0:T(4,128)(2,1)} %param.3), channel_id=1, source_target_pairs={{0,128},{128,0},{256,384},{384,256},{1,129},{129,1},{257,385},{385... | collective-permute-start | bytes 76808 | tf_op jit(solution)/shard_map/ppermute | solution.py:138
  5.0 9.2 %collective-permute-start.1 = (bf16[2,4,1600]{2,1,0:T(4,128)(2,1)}, bf16[2,4,1600]{2,1,0:T(4,128)(2,1)S(1)}, u32[]{:S(2)}, u32[]{:S(2)}) collective-permute-start(bf16[2,4,1600]{2,1,0:T(4,128)(2,1)} %param.3), channel_id=1, source_target_pairs={{128,256},{256,128},{129,257},{257,129},{130,258},{258,130},{131,2... | collective-permute-start | bytes 76808 | tf_op jit(solution)/shard_map/ppermute | solution.py:139
  15.1 3.8 %collective-permute-start.2 = (bf16[4,1,1600]{2,1,0:T(2,128)(2,1)S(1)}, bf16[4,1,1600]{2,1,0:T(2,128)(2,1)S(1)}, u32[]{:S(2)}, u32[]{:S(2)}) collective-permute-start(bf16[4,1,1600]{2,1,0:T(2,128)(2,1)S(1)} %get-tuple-element.24), channel_id=1, source_target_pairs={{1,2},{2,1},{3,4},{4,3},{5,6},{6,5},{7,8},{8,7},{9,10},{10,9},{11,... | collective-permute-start | bytes 38408 | tf_op jit(solution)/shard_map/ppermute | solution.py:145
  15.8 5.7 %collective-permute-start.3 = (bf16[4,1,1600]{2,1,0:T(2,128)(2,1)S(1)}, bf16[4,1,1600]{2,1,0:T(2,128)(2,1)S(1)}, u32[]{:S(2)}, u32[]{:S(2)}) collective-permute-start(bf16[4,1,1600]{2,1,0:T(2,128)(2,1)S(1)} %get-tuple-element.23), channel_id=1, source_target_pairs={{0,1},{1,0},{2,3},{3,2},{4,5},{5,4},{6,7},{7,6},{8,9},{9,8},{10,11... | collective-permute-start | bytes 38408 | tf_op jit(solution)/shard_map/ppermute | solution.py:146
  51.7 12.8 %collective-permute-start.5 = (bf16[128,1600]{1,0:T(8,128)(2,1)S(1)}, bf16[128,1600]{1,0:T(8,128)(2,1)S(1)}, u32[]{:S(2)}, u32[]{:S(2)}) collective-permute-start(bf16[128,1600]{1,0:T(8,128)(2,1)S(1)} %bitcast.12), channel_id=1, source_target_pairs={{1,0},{2,1},{3,2},{4,3},{5,4},{6,5},{7,6},{0,7},{9,8},{10,9},{11,1... | collective-permute-start | bytes 1228808 | tf_op jit(solution)/shard_map/ppermute | solution.py:119
  55.3 14.6 %collective-permute-start.6 = (bf16[128,1600]{1,0:T(8,128)(2,1)S(1)}, bf16[128,1600]{1,0:T(8,128)(2,1)S(1)}, u32[]{:S(2)}, u32[]{:S(2)}) collective-permute-start(bf16[128,1600]{1,0:T(8,128)(2,1)S(1)} %bitcast.13), channel_id=1, source_target_pairs={{8,0},{9,1},{10,2},{11,3},{12,4},{13,5},{14,6},{15,7},{16,8},{17,9... | collective-permute-start | bytes 1228808 | tf_op jit(solution)/shard_map/ppermute | solution.py:119
  57.9 12.0 %collective-permute-start.7 = (bf16[128,1600]{1,0:T(8,128)(2,1)S(1)}, bf16[128,1600]{1,0:T(8,128)(2,1)S(1)}, u32[]{:S(2)}, u32[]{:S(2)}) collective-permute-start(bf16[128,1600]{1,0:T(8,128)(2,1)S(1)} %bitcast.14), channel_id=1, source_target_pairs={{9,0},{10,1},{11,2},{12,3},{13,4},{14,5},{15,6},{8,7},{17,8},{18,9... | collective-permute-start | bytes 1228808 | tf_op jit(solution)/shard_map/ppermute | solution.py:119

commit v9 on v8

--- a/solution.py
+++ b/solution.py
@@ -56,7 +56,9 @@
         in_specs=[pl.BlockSpec(memory_space=pltpu.VMEM)] * 4,
         out_specs=pl.BlockSpec(memory_space=pltpu.VMEM),
         compiler_params=pltpu.CompilerParams(vmem_limit_bytes=16 * 1024 * 1024),
-        cost_estimate=pl.CostEstimate(flops=1000000, bytes_accessed=200000, transcendentals=0),
+        cost_estimate=pl.CostEstimate(
+            flops=100000000000, bytes_accessed=200000, transcendentals=0
+        ),
     )(block, far, near, weights)
 
 
@@ -164,8 +166,7 @@
 
 def on_device(patterns, nlpar_weights, dictionary):
     rows, cols = patterns.shape[:2]
-    shared, patterns = lax.optimization_barrier((dictionary, patterns))
-    partner = lax.ppermute(shared, "sy", [(0, 1), (1, 0)])
+    partner = lax.ppermute(dictionary, "sy", [(0, 1), (1, 0)])
     weights = valid_weights(nlpar_weights, rows, cols)
     normalized = average(*rim(patterns), weights)
     own = gather_class(normalized)

time: 93.8 us -> 94.2 us (level)
  the two profiles are of different devices: /device:TPU:4 before, /device:TPU:2 now
where the time goes in v9:
time: 94.2 us; the launch traced here: 93.8 us
  blocking collectives  49.8 us (53%)
  starting transfers between devices  23.9 us (25%)
  waiting for transfers between devices  6.46 us (7%)
  matrix products  5.8 us (6%)
  Pallas kernels  4.29 us (5%)
  other arithmetic  2.55 us (3%)
    all_to_all x1, blocking collectives, gather_class(): got = lax.all_to_all(copies, COLS, 0, 0, axis_index_groups=groups)  30.1 us
    all_to_all x1, blocking collectives, merge(): lax.all_to_all(table.reshape(64, 2, 4), COLS, 0, 0, axis_index_groups=gro...  19.6 us
    ppermute x3, starting transfers between devices, from_neighbour(): return lax.ppermute(block, COLS, pairs)  9.19 us
    ppermute x1, starting transfers between devices, rim(): near = lax.ppermute(patterns, 'sx', swap_pairs((0, 2)))  7.81 us
    dot_general x2, matrix products, best_of(): jnp.dot(points, held, preferred_element_type=jnp.float32)  5.8 us
    pallas_call x1, Pallas kernels, hold(): pl.pallas_call(hold_kernel, out_shape=pltpu.VMEM((own.shape[0], 2 * own.s...  3.67 us
    ppermute x1, waiting for transfers between devices, rim(): lax.ppermute(jnp.where(even, last, first), COLS, swap_pairs(range(0, 128,...  3.25 us
    ppermute x3, waiting for transfers between devices, from_neighbour(): return lax.ppermute(block, COLS, pairs)  2.53 us
  transfers between devices with their start and end apart: 8, of which 3 were waited for; matrix products, arithmetic and copies ran while one was open for 6% of the time, Pallas kernels for 5%

profile of v9, /device:TPU:2, one launch (start us, length us, event | category | flops | bytes accessed | tf_op | source)
XLA Modules:
  0.0 93.8 jit_solution(18342319337733618143)
XLA Ops:
  0.0 7.8 %collective-permute-start = (bf16[2,4,1600]{2,1,0:T(4,128)(2,1)}, bf16[2,4,1600]{2,1,0:T(4,128)(2,1)S(1)}, u32[]{:S(2)}, u32[]{:S(2)}) collective-permute-start(bf16[2,4,1600]{2,1,0:T(4,128)(2,1)} %param.3), channel_id=1, source_target_pairs={{0,128},{128,0},{256,384},{384,256},{1,129},{129,1},{257,385},{385... | collective-permute-start | bytes 76808 | tf_op jit(solution)/shard_map/ppermute | solution.py:140
  7.8 1.9 %collective-permute-start.1 = (bf16[2,4,1600]{2,1,0:T(4,128)(2,1)}, bf16[2,4,1600]{2,1,0:T(4,128)(2,1)S(1)}, u32[]{:S(2)}, u32[]{:S(2)}) collective-permute-start(bf16[2,4,1600]{2,1,0:T(4,128)(2,1)} %param.3), channel_id=1, source_target_pairs={{128,256},{256,128},{129,257},{257,129},{130,258},{258,130},{131,2... | collective-permute-start | bytes 76808 | tf_op jit(solution)/shard_map/ppermute | solution.py:141
  9.7 1.9 %collective-permute-start.4 = (bf16[1600,1408]{1,0:T(8,128)(2,1)}, bf16[1600,1408]{1,0:T(8,128)(2,1)}, u32[]{:S(2)}, u32[]{:S(2)}) collective-permute-start(bf16[1600,1408]{1,0:T(8,128)(2,1)} %own_ref), channel_id=1, source_target_pairs={{0,64},{64,0},{1,65},{65,1},{2,66},{66,2},{3,67},{67,3},{4,68},{68... | collective-permute-start | bytes 13516808 | tf_op jit(solution)/shard_map/ppermute | solution.py:169
  11.7 0.1 fusion.6
  11.8 0.1 and.68
  11.9 0.1 compare_and_fusion
  12.0 0.1 and.63
  12.0 0.1 and.64
  12.1 0.8 fusion.9
  12.9 0.1 copy.8
  13.0 0.1 pad.8.clone
  13.1 0.7 collective-permute-done.1
  13.8 0.8 pad_maximum_fusion.block_ref
  14.6 0.1 broadcast_select_fusion
  14.7 0.7 collective-permute-start.2
  15.3 2.4 %collective-permute-start.3 = (bf16[4,1,1600]{2,1,0:T(2,128)(2,1)S(1)}, bf16[4,1,1600]{2,1,0:T(2,128)(2,1)S(1)}, u32[]{:S(2)}, u32[]{:S(2)}) collective-permute-start(bf16[4,1,1600]{2,1,0:T(2,128)(2,1)S(1)} %get-tuple-element.19), channel_id=1, source_target_pairs={{0,1},{1,0},{2,3},{3,2},{4,5},{5,4},{6,7},{7,6},{8,9},{9,8},{10,11... | collective-permute-start | bytes 38408 | tf_op jit(solution)/shard_map/ppermute | solution.py:148
  17.7 0.1 maximum_maximum_fusion.weight_ref
  17.8 3.2 %collective-permute-done.3.near_ref = bf16[4,1,1600]{2,1,0:T(2,128)(2,1)S(1)} collective-permute-done((bf16[4,1,1600]{2,1,0:T(2,128)(2,1)S(1)}, bf16[4,1,1600]{2,1,0:T(2,128)(2,1)S(1)}, u32[]{:S(2)}, u32[]{:S(2)}) %collective-permute-start.3) | collective-permute-done | bytes 12832 | tf_op jit(solution)/shard_map/ppermute | solution.py:148
  21.1 0.6 shard_map.37
  21.7 30.1 %all_to_all.10 = bf16[16,8,1600]{2,1,0:T(8,128)(2,1)S(1)} all-to-all(bf16[16,8,1600]{2,1,0:T(8,128)(2,1)S(1)} %broadcast_in_dim.13), channel_id=1, replica_groups={{0,2,4,6,16,18,20,22,32,34,36,38,48,50,52,54},{1,3,5,7,17,19,21,23,33,3..., dimensions={0} | all-to-all | bytes 819200 | tf_op jit(solution)/shard_map/all_to_all | solution.py:110
  51.9 3.7 %collective-permute-start.5 = (bf16[128,1600]{1,0:T(8,128)(2,1)S(1)}, bf16[128,1600]{1,0:T(8,128)(2,1)S(1)}, u32[]{:S(2)}, u32[]{:S(2)}) collective-permute-start(bf16[128,1600]{1,0:T(8,128)(2,1)S(1)} %bitcast.12), channel_id=1, source_target_pairs={{1,0},{2,1},{3,2},{4,3},{5,4},{6,5},{7,6},{0,7},{9,8},{10,9},{11,1... | collective-permute-start | bytes 1228808 | tf_op jit(solution)/shard_map/ppermute | solution.py:121
  55.6 2.5 %collective-permute-start.6 = (bf16[128,1600]{1,0:T(8,128)(2,1)S(1)}, bf16[128,1600]{1,0:T(8,128)(2,1)S(1)}, u32[]{:S(2)}, u32[]{:S(2)}) collective-permute-start(bf16[128,1600]{1,0:T(8,128)(2,1)S(1)} %bitcast.13), channel_id=1, source_target_pairs={{8,0},{9,1},{10,2},{11,3},{12,4},{13,5},{14,6},{15,7},{16,8},{17,9... | collective-permute-start | bytes 1228808 | tf_op jit(solution)/shard_map/ppermute | solution.py:121
  58.1 3.0 %collective-permute-start.7 = (bf16[128,1600]{1,0:T(8,128)(2,1)S(1)}, bf16[128,1600]{1,0:T(8,128)(2,1)S(1)}, u32[]{:S(2)}, u32[]{:S(2)}) collective-permute-start(bf16[128,1600]{1,0:T(8,128)(2,1)S(1)} %bitcast.14), channel_id=1, source_target_pairs={{9,0},{10,1},{11,2},{12,3},{13,4},{14,5},{15,6},{8,7},{17,8},{18,9... | collective-permute-start | bytes 1228808 | tf_op jit(solution)/shard_map/ppermute | solution.py:121
  61.1 3.7 %shard_map.38 = bf16[1600,2816]{1,0:T(8,128)(2,1)S(1)} custom-call(bf16[1600,1408]{1,0:T(8,128)(2,1)} %own_ref, bf16[1600,1408]{1,0:T(8,128)(2,1)} %collective-permute-done.4.partner_ref), custom_call_target="tpu_custom_call" | custom-call | bytes 18022400 | tf_op jit(solution)/shard_map/pallas_call | solution.py:78
  64.8 2.9 %convolution_reduce_fusion.1 = f32[256]{0:T(256)S(1)} fusion(bf16[1600,2816]{1,0:T(8,128)(2,1)S(1)} %shard_map.38, bf16[128,1600]{1,0:T(8,128)(2,1)S(1)} %collective-permute-done.5, bf16[128,1600]{1,0:T(8,128)(2,1)S(1)} %bitcast.15), kind=kOutput, calls=%fused_computation.1 | convolution fusion | flops 2309226240 | bytes 9831424 | tf_op jit(solution)/shard_map/dot_general | solution.py:93
  67.7 2.5 %collective-permute-done.6 = bf16[128,1600]{1,0:T(8,128)(2,1)S(1)} collective-permute-done((bf16[128,1600]{1,0:T(8,128)(2,1)S(1)}, bf16[128,1600]{1,0:T(8,128)(2,1)S(1)}, u32[]{:S(2)}, u32[]{:S(2)}) %collective-permute-start.6) | collective-permute-done | bytes 409632 | tf_op jit(solution)/shard_map/ppermute | solution.py:121
  70.2 2.9 %convolution_reduce_fusion = f32[256]{0:T(256)S(1)} fusion(bf16[1600,2816]{1,0:T(8,128)(2,1)S(1)} %shard_map.38, bf16[128,1600]{1,0:T(8,128)(2,1)S(1)} %collective-permute-done.7, bf16[128,1600]{1,0:T(8,128)(2,1)S(1)} %collective-permute-done.6), kind=kOutput, calls=%fused_computation | convolution fusion | flops 2309226240 | bytes 9831424 | tf_op jit(solution)/shard_map/dot_general | solution.py:93
  73.2 0.1 reshape.84
  73.3 0.1 copy.9
  73.4 0.1 copy.10
  73.5 19.6 %all_to_all.11 = f32[64,2,4]{2,1,0:T(2,128)S(1)} all-to-all(f32[64,2,4]{2,1,0:T(2,128)S(1)} %copy.10), channel_id=1, replica_groups={{0,1,2,3,4,5,6,7,8,9,10,11,12,13,14,15,16,17,18,19,20,21,22,23,24,25,26..., dimensions={0} | all-to-all | bytes 4096 | tf_op jit(solution)/shard_map/all_to_all | solution.py:130
  93.1 0.6 reduce_max.29
  (15 shorter events, 0.1 us)
Async XLA Ops:
  0.0 13.1 %collective-permute-start = (bf16[2,4,1600]{2,1,0:T(4,128)(2,1)}, bf16[2,4,1600]{2,1,0:T(4,128)(2,1)S(1)}, u32[]{:S(2)}, u32[]{:S(2)}) collective-permute-start(bf16[2,4,1600]{2,1,0:T(4,128)(2,1)} %param.3), channel_id=1, source_target_pairs={{0,128},{128,0},{256,384},{384,256},{1,129},{129,1},{257,385},{385... | collective-permute-start | bytes 76808 | tf_op jit(solution)/shard_map/ppermute | solution.py:140
  7.8 6.0 %collective-permute-start.1 = (bf16[2,4,1600]{2,1,0:T(4,128)(2,1)}, bf16[2,4,1600]{2,1,0:T(4,128)(2,1)S(1)}, u32[]{:S(2)}, u32[]{:S(2)}) collective-permute-start(bf16[2,4,1600]{2,1,0:T(4,128)(2,1)} %param.3), channel_id=1, source_target_pairs={{128,256},{256,128},{129,257},{257,129},{130,258},{258,130},{131,2... | collective-permute-start | bytes 76808 | tf_op jit(solution)/shard_map/ppermute | solution.py:141
  9.7 51.4 %collective-permute-start.4 = (bf16[1600,1408]{1,0:T(8,128)(2,1)}, bf16[1600,1408]{1,0:T(8,128)(2,1)}, u32[]{:S(2)}, u32[]{:S(2)}) collective-permute-start(bf16[1600,1408]{1,0:T(8,128)(2,1)} %own_ref), channel_id=1, source_target_pairs={{0,64},{64,0},{1,65},{65,1},{2,66},{66,2},{3,67},{67,3},{4,68},{68... | collective-permute-start | bytes 13516808 | tf_op jit(solution)/shard_map/ppermute | solution.py:169
  14.7 3.2 %collective-permute-start.2 = (bf16[4,1,1600]{2,1,0:T(2,128)(2,1)S(1)}, bf16[4,1,1600]{2,1,0:T(2,128)(2,1)S(1)}, u32[]{:S(2)}, u32[]{:S(2)}) collective-permute-start(bf16[4,1,1600]{2,1,0:T(2,128)(2,1)S(1)} %get-tuple-element.20), channel_id=1, source_target_pairs={{1,2},{2,1},{3,4},{4,3},{5,6},{6,5},{7,8},{8,7},{9,10},{10,9},{11,... | collective-permute-start | bytes 38408 | tf_op jit(solution)/shard_map/ppermute | solution.py:147
  15.3 5.7 %collective-permute-start.3 = (bf16[4,1,1600]{2,1,0:T(2,128)(2,1)S(1)}, bf16[4,1,1600]{2,1,0:T(2,128)(2,1)S(1)}, u32[]{:S(2)}, u32[]{:S(2)}) collective-permute-start(bf16[4,1,1600]{2,1,0:T(2,128)(2,1)S(1)} %get-tuple-element.19), channel_id=1, source_target_pairs={{0,1},{1,0},{2,3},{3,2},{4,5},{5,4},{6,7},{7,6},{8,9},{9,8},{10,11... | collective-permute-start | bytes 38408 | tf_op jit(solution)/shard_map/ppermute | solution.py:148
  51.9 12.9 %collective-permute-start.5 = (bf16[128,1600]{1,0:T(8,128)(2,1)S(1)}, bf16[128,1600]{1,0:T(8,128)(2,1)S(1)}, u32[]{:S(2)}, u32[]{:S(2)}) collective-permute-start(bf16[128,1600]{1,0:T(8,128)(2,1)S(1)} %bitcast.12), channel_id=1, source_target_pairs={{1,0},{2,1},{3,2},{4,3},{5,4},{6,5},{7,6},{0,7},{9,8},{10,9},{11,1... | collective-permute-start | bytes 1228808 | tf_op jit(solution)/shard_map/ppermute | solution.py:121
  55.6 14.6 %collective-permute-start.6 = (bf16[128,1600]{1,0:T(8,128)(2,1)S(1)}, bf16[128,1600]{1,0:T(8,128)(2,1)S(1)}, u32[]{:S(2)}, u32[]{:S(2)}) collective-permute-start(bf16[128,1600]{1,0:T(8,128)(2,1)S(1)} %bitcast.13), channel_id=1, source_target_pairs={{8,0},{9,1},{10,2},{11,3},{12,4},{13,5},{14,6},{15,7},{16,8},{17,9... | collective-permute-start | bytes 1228808 | tf_op jit(solution)/shard_map/ppermute | solution.py:121
  58.1 12.1 %collective-permute-start.7 = (bf16[128,1600]{1,0:T(8,128)(2,1)S(1)}, bf16[128,1600]{1,0:T(8,128)(2,1)S(1)}, u32[]{:S(2)}, u32[]{:S(2)}) collective-permute-start(bf16[128,1600]{1,0:T(8,128)(2,1)S(1)} %bitcast.14), channel_id=1, source_target_pairs={{9,0},{10,1},{11,2},{12,3},{13,4},{14,5},{15,6},{8,7},{17,8},{18,9... | collective-permute-start | bytes 1228808 | tf_op jit(solution)/shard_map/ppermute | solution.py:121

commit v10 on v9

--- a/solution.py
+++ b/solution.py
@@ -88,8 +88,7 @@
     )(pltpu.with_memory_space_constraint(own, pltpu.HBM), partner)
 
 
-def best_of(first, second, held):
-    points = jnp.concatenate([first, second], axis=0)
+def best_of(points, held):
     return jnp.max(jnp.dot(points, held, preferred_element_type=jnp.float32), axis=1)
 
 
@@ -175,9 +174,12 @@
     diagonal = from_neighbour(own, 1, 1)
     own, *halves = lax.optimization_barrier((own, dictionary, partner))
     held = hold(*halves)
-    early = best_of(own, ahead, held)
-    early, across, diagonal = lax.optimization_barrier((early, across, diagonal))
-    tables = [early, best_of(across, diagonal, held)]
+    early = best_of(jnp.concatenate([own, ahead], axis=0), held)
+    early, diagonal = lax.optimization_barrier((early, diagonal))
+    late = best_of(diagonal, held)
+    late, across = lax.optimization_barrier((late, across))
+    last = best_of(across, held)
+    tables = [early, jnp.concatenate([last, late], axis=0)]
     return merge(tables)
 
 

time: 94.2 us -> 93.8 us (level)
    dot_general x2 -> x3, matrix products: 5.8 us -> 5.99 us  [best_of(): jnp.dot(points, held, preferred_element_type=jnp.float32)]
  transfers between devices with their start and end apart: 8 -> 8, of which waited for: 3 -> 3; matrix products, arithmetic and copies ran while one was open for 6% -> 7% of each run, Pallas kernels for 5% -> 5%
where the time goes in v10:
time: 93.8 us; the launch traced here: 93.4 us
  blocking collectives  49.1 us (52%)
  starting transfers between devices  23.9 us (25%)
  waiting for transfers between devices  6.59 us (7%)
  matrix products  5.99 us (6%)
  Pallas kernels  4.29 us (5%)
  other arithmetic  2.56 us (3%)
    all_to_all x1, blocking collectives, gather_class(): got = lax.all_to_all(copies, COLS, 0, 0, axis_index_groups=groups)  30.1 us
    all_to_all x1, blocking collectives, merge(): lax.all_to_all(table.reshape(64, 2, 4), COLS, 0, 0, axis_index_groups=gro...  19 us
    ppermute x3, starting transfers between devices, from_neighbour(): return lax.ppermute(block, COLS, pairs)  9.19 us
    ppermute x1, starting transfers between devices, rim(): near = lax.ppermute(patterns, 'sx', swap_pairs((0, 2)))  7.81 us
    dot_general x3, matrix products, best_of(): jnp.dot(points, held, preferred_element_type=jnp.float32)  5.99 us
    pallas_call x1, Pallas kernels, hold(): pl.pallas_call(hold_kernel, out_shape=pltpu.VMEM((own.shape[0], 2 * own.s...  3.67 us
    ppermute x1, waiting for transfers between devices, rim(): lax.ppermute(jnp.where(even, last, first), COLS, swap_pairs(range(0, 128,...  3.25 us
    ppermute x3, waiting for transfers between devices, from_neighbour(): return lax.ppermute(block, COLS, pairs)  2.65 us
  transfers between devices with their start and end apart: 8, of which 3 were waited for; matrix products, arithmetic and copies ran while one was open for 7% of the time, Pallas kernels for 5%

profile of v10, /device:TPU:2, one launch (start us, length us, event | category | flops | bytes accessed | tf_op | source)
XLA Modules:
  0.0 93.4 jit_solution(3105106785841921671)
XLA Ops:
  0.0 7.8 %collective-permute-start = (bf16[2,4,1600]{2,1,0:T(4,128)(2,1)}, bf16[2,4,1600]{2,1,0:T(4,128)(2,1)S(1)}, u32[]{:S(2)}, u32[]{:S(2)}) collective-permute-start(bf16[2,4,1600]{2,1,0:T(4,128)(2,1)} %param.3), channel_id=1, source_target_pairs={{0,128},{128,0},{256,384},{384,256},{1,129},{129,1},{257,385},{385... | collective-permute-start | bytes 76808 | tf_op jit(solution)/shard_map/ppermute | solution.py:139
  7.8 1.9 %collective-permute-start.1 = (bf16[2,4,1600]{2,1,0:T(4,128)(2,1)}, bf16[2,4,1600]{2,1,0:T(4,128)(2,1)S(1)}, u32[]{:S(2)}, u32[]{:S(2)}) collective-permute-start(bf16[2,4,1600]{2,1,0:T(4,128)(2,1)} %param.3), channel_id=1, source_target_pairs={{128,256},{256,128},{129,257},{257,129},{130,258},{258,130},{131,2... | collective-permute-start | bytes 76808 | tf_op jit(solution)/shard_map/ppermute | solution.py:140
  9.7 1.9 %collective-permute-start.4 = (bf16[1600,1408]{1,0:T(8,128)(2,1)}, bf16[1600,1408]{1,0:T(8,128)(2,1)}, u32[]{:S(2)}, u32[]{:S(2)}) collective-permute-start(bf16[1600,1408]{1,0:T(8,128)(2,1)} %own_ref), channel_id=1, source_target_pairs={{0,64},{64,0},{1,65},{65,1},{2,66},{66,2},{3,67},{67,3},{4,68},{68... | collective-permute-start | bytes 13516808 | tf_op jit(solution)/shard_map/ppermute | solution.py:168
  11.7 0.1 fusion.3
  11.8 0.1 and.68
  11.9 0.1 compare_and_fusion
  12.0 0.1 and.63
  12.0 0.1 and.64
  12.1 0.8 fusion.5
  12.9 0.1 copy.8
  13.0 0.1 pad.8.clone
  13.1 0.7 collective-permute-done.1
  13.8 0.8 pad_maximum_fusion.block_ref
  14.6 0.1 broadcast_select_fusion
  14.7 0.7 collective-permute-start.2
  15.3 2.4 %collective-permute-start.3 = (bf16[4,1,1600]{2,1,0:T(2,128)(2,1)S(1)}, bf16[4,1,1600]{2,1,0:T(2,128)(2,1)S(1)}, u32[]{:S(2)}, u32[]{:S(2)}) collective-permute-start(bf16[4,1,1600]{2,1,0:T(2,128)(2,1)S(1)} %get-tuple-element.21), channel_id=1, source_target_pairs={{0,1},{1,0},{2,3},{3,2},{4,5},{5,4},{6,7},{7,6},{8,9},{9,8},{10,11... | collective-permute-start | bytes 38408 | tf_op jit(solution)/shard_map/ppermute | solution.py:147
  17.7 0.1 maximum_maximum_fusion.weight_ref
  17.8 3.2 %collective-permute-done.3.near_ref = bf16[4,1,1600]{2,1,0:T(2,128)(2,1)S(1)} collective-permute-done((bf16[4,1,1600]{2,1,0:T(2,128)(2,1)S(1)}, bf16[4,1,1600]{2,1,0:T(2,128)(2,1)S(1)}, u32[]{:S(2)}, u32[]{:S(2)}) %collective-permute-start.3) | collective-permute-done | bytes 12832 | tf_op jit(solution)/shard_map/ppermute | solution.py:147
  21.1 0.6 shard_map.37
  21.7 30.1 %all_to_all.10 = bf16[16,8,1600]{2,1,0:T(8,128)(2,1)S(1)} all-to-all(bf16[16,8,1600]{2,1,0:T(8,128)(2,1)S(1)} %broadcast_in_dim.13), channel_id=1, replica_groups={{0,2,4,6,16,18,20,22,32,34,36,38,48,50,52,54},{1,3,5,7,17,19,21,23,33,3..., dimensions={0} | all-to-all | bytes 819200 | tf_op jit(solution)/shard_map/all_to_all | solution.py:109
  51.9 3.7 %collective-permute-start.5 = (bf16[128,1600]{1,0:T(8,128)(2,1)S(1)}, bf16[128,1600]{1,0:T(8,128)(2,1)S(1)}, u32[]{:S(2)}, u32[]{:S(2)}) collective-permute-start(bf16[128,1600]{1,0:T(8,128)(2,1)S(1)} %bitcast.16), channel_id=1, source_target_pairs={{1,0},{2,1},{3,2},{4,3},{5,4},{6,5},{7,6},{0,7},{9,8},{10,9},{11,1... | collective-permute-start | bytes 1228808 | tf_op jit(solution)/shard_map/ppermute | solution.py:120
  55.6 2.7 %collective-permute-start.6 = (bf16[128,1600]{1,0:T(8,128)(2,1)S(1)}, bf16[128,1600]{1,0:T(8,128)(2,1)S(1)}, u32[]{:S(2)}, u32[]{:S(2)}) collective-permute-start(bf16[128,1600]{1,0:T(8,128)(2,1)S(1)} %bitcast.17), channel_id=1, source_target_pairs={{9,0},{10,1},{11,2},{12,3},{13,4},{14,5},{15,6},{8,7},{17,8},{18,9... | collective-permute-start | bytes 1228808 | tf_op jit(solution)/shard_map/ppermute | solution.py:120
  58.3 2.8 %collective-permute-start.7 = (bf16[128,1600]{1,0:T(8,128)(2,1)S(1)}, bf16[128,1600]{1,0:T(8,128)(2,1)S(1)}, u32[]{:S(2)}, u32[]{:S(2)}) collective-permute-start(bf16[128,1600]{1,0:T(8,128)(2,1)S(1)} %bitcast.18), channel_id=1, source_target_pairs={{8,0},{9,1},{10,2},{11,3},{12,4},{13,5},{14,6},{15,7},{16,8},{17,9... | collective-permute-start | bytes 1228808 | tf_op jit(solution)/shard_map/ppermute | solution.py:120
  61.1 3.7 %shard_map.38 = bf16[1600,2816]{1,0:T(8,128)(2,1)S(1)} custom-call(bf16[1600,1408]{1,0:T(8,128)(2,1)} %own_ref, bf16[1600,1408]{1,0:T(8,128)(2,1)} %collective-permute-done.4.partner_ref), custom_call_target="tpu_custom_call" | custom-call | bytes 18022400 | tf_op jit(solution)/shard_map/pallas_call | solution.py:78
  64.8 2.9 %convolution_reduce_fusion = f32[256]{0:T(256)S(1)} fusion(bf16[1600,2816]{1,0:T(8,128)(2,1)S(1)} %shard_map.38, bf16[128,1600]{1,0:T(8,128)(2,1)S(1)} %collective-permute-done.5, bf16[128,1600]{1,0:T(8,128)(2,1)S(1)} %bitcast.19), kind=kOutput, calls=%fused_computation | convolution fusion | flops 2309226240 | bytes 9831424 | tf_op jit(solution)/shard_map/dot_general | solution.py:92
  67.7 1.6 %convolution_reduce_fusion.2 = f32[128]{0:T(128)S(1)} fusion(bf16[128,1600]{1,0:T(8,128)(2,1)S(1)} %collective-permute-done.6, bf16[1600,2816]{1,0:T(8,128)(2,1)S(1)} %shard_map.38), kind=kOutput, calls=%fused_computation.2 | convolution fusion | flops 1153793920 | bytes 9421312 | tf_op jit(solution)/shard_map/dot_general | solution.py:92
  69.2 2.6 %collective-permute-done.7 = bf16[128,1600]{1,0:T(8,128)(2,1)S(1)} collective-permute-done((bf16[128,1600]{1,0:T(8,128)(2,1)S(1)}, bf16[128,1600]{1,0:T(8,128)(2,1)S(1)}, u32[]{:S(2)}, u32[]{:S(2)}) %collective-permute-start.7) | collective-permute-done | bytes 409632 | tf_op jit(solution)/shard_map/ppermute | solution.py:120
  71.9 1.6 %convolution_reduce_fusion.1 = f32[128]{0:T(128)S(1)} fusion(bf16[128,1600]{1,0:T(8,128)(2,1)S(1)} %collective-permute-done.7, bf16[1600,2816]{1,0:T(8,128)(2,1)S(1)} %shard_map.38), kind=kOutput, calls=%fused_computation.1 | convolution fusion | flops 1153793920 | bytes 9421312 | tf_op jit(solution)/shard_map/dot_general | solution.py:92
  73.5 0.1 reshape.84
  73.7 0.1 copy.9
  73.8 19.0 %all_to_all.11 = f32[64,2,4]{2,1,0:T(2,128)S(1)} all-to-all(f32[64,2,4]{2,1,0:T(2,128)S(1)} %copy.10), channel_id=1, replica_groups={{0,1,2,3,4,5,6,7,8,9,10,11,12,13,14,15,16,17,18,19,20,21,22,23,24,25,26..., dimensions={0} | all-to-all | bytes 4096 | tf_op jit(solution)/shard_map/all_to_all | solution.py:129
  92.8 0.6 reduce_max.39
  (17 shorter events, 0.2 us)
Async XLA Ops:
  0.0 13.1 %collective-permute-start = (bf16[2,4,1600]{2,1,0:T(4,128)(2,1)}, bf16[2,4,1600]{2,1,0:T(4,128)(2,1)S(1)}, u32[]{:S(2)}, u32[]{:S(2)}) collective-permute-start(bf16[2,4,1600]{2,1,0:T(4,128)(2,1)} %param.3), channel_id=1, source_target_pairs={{0,128},{128,0},{256,384},{384,256},{1,129},{129,1},{257,385},{385... | collective-permute-start | bytes 76808 | tf_op jit(solution)/shard_map/ppermute | solution.py:139
  7.8 6.0 %collective-permute-start.1 = (bf16[2,4,1600]{2,1,0:T(4,128)(2,1)}, bf16[2,4,1600]{2,1,0:T(4,128)(2,1)S(1)}, u32[]{:S(2)}, u32[]{:S(2)}) collective-permute-start(bf16[2,4,1600]{2,1,0:T(4,128)(2,1)} %param.3), channel_id=1, source_target_pairs={{128,256},{256,128},{129,257},{257,129},{130,258},{258,130},{131,2... | collective-permute-start | bytes 76808 | tf_op jit(solution)/shard_map/ppermute | solution.py:140
  9.7 51.4 %collective-permute-start.4 = (bf16[1600,1408]{1,0:T(8,128)(2,1)}, bf16[1600,1408]{1,0:T(8,128)(2,1)}, u32[]{:S(2)}, u32[]{:S(2)}) collective-permute-start(bf16[1600,1408]{1,0:T(8,128)(2,1)} %own_ref), channel_id=1, source_target_pairs={{0,64},{64,0},{1,65},{65,1},{2,66},{66,2},{3,67},{67,3},{4,68},{68... | collective-permute-start | bytes 13516808 | tf_op jit(solution)/shard_map/ppermute | solution.py:168
  14.7 3.2 %collective-permute-start.2 = (bf16[4,1,1600]{2,1,0:T(2,128)(2,1)S(1)}, bf16[4,1,1600]{2,1,0:T(2,128)(2,1)S(1)}, u32[]{:S(2)}, u32[]{:S(2)}) collective-permute-start(bf16[4,1,1600]{2,1,0:T(2,128)(2,1)S(1)} %get-tuple-element.22), channel_id=1, source_target_pairs={{1,2},{2,1},{3,4},{4,3},{5,6},{6,5},{7,8},{8,7},{9,10},{10,9},{11,... | collective-permute-start | bytes 38408 | tf_op jit(solution)/shard_map/ppermute | solution.py:146
  15.3 5.7 %collective-permute-start.3 = (bf16[4,1,1600]{2,1,0:T(2,128)(2,1)S(1)}, bf16[4,1,1600]{2,1,0:T(2,128)(2,1)S(1)}, u32[]{:S(2)}, u32[]{:S(2)}) collective-permute-start(bf16[4,1,1600]{2,1,0:T(2,128)(2,1)S(1)} %get-tuple-element.21), channel_id=1, source_target_pairs={{0,1},{1,0},{2,3},{3,2},{4,5},{5,4},{6,7},{7,6},{8,9},{9,8},{10,11... | collective-permute-start | bytes 38408 | tf_op jit(solution)/shard_map/ppermute | solution.py:147
  51.9 12.9 %collective-permute-start.5 = (bf16[128,1600]{1,0:T(8,128)(2,1)S(1)}, bf16[128,1600]{1,0:T(8,128)(2,1)S(1)}, u32[]{:S(2)}, u32[]{:S(2)}) collective-permute-start(bf16[128,1600]{1,0:T(8,128)(2,1)S(1)} %bitcast.16), channel_id=1, source_target_pairs={{1,0},{2,1},{3,2},{4,3},{5,4},{6,5},{7,6},{0,7},{9,8},{10,9},{11,1... | collective-permute-start | bytes 1228808 | tf_op jit(solution)/shard_map/ppermute | solution.py:120
  55.6 12.1 %collective-permute-start.6 = (bf16[128,1600]{1,0:T(8,128)(2,1)S(1)}, bf16[128,1600]{1,0:T(8,128)(2,1)S(1)}, u32[]{:S(2)}, u32[]{:S(2)}) collective-permute-start(bf16[128,1600]{1,0:T(8,128)(2,1)S(1)} %bitcast.17), channel_id=1, source_target_pairs={{9,0},{10,1},{11,2},{12,3},{13,4},{14,5},{15,6},{8,7},{17,8},{18,9... | collective-permute-start | bytes 1228808 | tf_op jit(solution)/shard_map/ppermute | solution.py:120
  58.3 13.6 %collective-permute-start.7 = (bf16[128,1600]{1,0:T(8,128)(2,1)S(1)}, bf16[128,1600]{1,0:T(8,128)(2,1)S(1)}, u32[]{:S(2)}, u32[]{:S(2)}) collective-permute-start(bf16[128,1600]{1,0:T(8,128)(2,1)S(1)} %bitcast.18), channel_id=1, source_target_pairs={{8,0},{9,1},{10,2},{11,3},{12,4},{13,5},{14,6},{15,7},{16,8},{17,9... | collective-permute-start | bytes 1228808 | tf_op jit(solution)/shard_map/ppermute | solution.py:120
